TPU v7x, 256 devices: a whole 4x4x8 slice. The times are simulated.
256 devices in a mesh: seq: 64 (over z_lo, y, x), chan: 4 (over z_hi, core).
Axes of the slice: x: 4, y: 4, z: 8 (z_hi: 2, z_lo: 4; z = z_hi * 4 + z_lo), core: 2. Of those that a mesh axis runs over, the one named last changes fastest.
Arguments:
- residual: bfloat16 [8192, 4096], P('seq', 'chan'), may hold values from -40 to 40
- query_feats: bfloat16 [8192, 4096], P('seq', 'chan'), may hold values from -6 to 6
- key_feats: bfloat16 [8192, 4096], P('seq', 'chan'), may hold values from -6 to 6
- value_feats: bfloat16 [8192, 4096], P('seq', 'chan'), may hold values from -6 to 6
- filters: bfloat16 [8192, 4096], P('seq', 'chan'), may hold values from -1 to 1
- cotangent: bfloat16 [8192, 4096], P('seq', 'chan'), may hold values from -12 to 12
- skip_bias: float32 [4096], P('chan'), may hold values from -1 to 1
- norm_gain: float32 [4096], P('chan'), may hold values from 0.5 to 1.5
Outputs:
- normed: bfloat16 [8192, 4096], P('seq', 'chan')
- grad_residual: bfloat16 [8192, 4096], P('seq', 'chan')
- grad_query: bfloat16 [8192, 4096], P('seq', 'chan')
- grad_key: bfloat16 [8192, 4096], P('seq', 'chan')
- grad_value: bfloat16 [8192, 4096], P('seq', 'chan')
- grad_filter: float32 [8192, 4096], P('seq', 'chan')
- grad_bias: float32 [4096], P('chan')
- grad_gain: float32 [4096], P('chan')
All inputs are finite; a program needn't handle non-finite values.
Results may differ from a plain program's by a relative error of at most 0.007.
Values may be sent and summed in bfloat16 or wider, within the bound.
No kernel may reach another device: no remote copies, remote signals or barrier semaphores. Data moves between devices by JAX's collectives and lax.ppermute only.
A program may use at most 64 MiB of HBM per device.

v0:
```python
import math

import jax
import jax.numpy as jnp
from jax import lax
from jax.sharding import PartitionSpec as P

highest = lax.Precision.HIGHEST
epsilon = 1e-06


def counting(count):
    return jnp.arange(count, dtype=jnp.int32)


def angle_tables(first_index, later_position_index, length):
    product = first_index[:, None] * later_position_index[None, :] % length
    angle = product.astype(jnp.float32) * (2.0 * math.pi / length)
    return (jnp.cos(angle), jnp.sin(angle))


def rotate(real_part, imag_part, cosine, sine, sign):
    return (
        real_part * cosine - sign * imag_part * sine,
        imag_part * cosine + sign * real_part * sine,
    )


def across_blocks(blocks):
    seq_count = blocks.shape[1]
    cosine, sine = angle_tables(counting(2 * seq_count), counting(seq_count), 2 * seq_count)
    values = blocks.astype(jnp.float32)
    real_part = jnp.einsum("ka,sa...->sk...", cosine, values, precision=highest)
    imag_part = -jnp.einsum("ka,sa...->sk...", sine, values, precision=highest)
    return (real_part, imag_part)


def within_blocks(real_part, imag_part, sign):
    extent = real_part.shape[-2]
    cosine, sine = angle_tables(counting(extent), counting(extent), extent)
    stacked = jnp.stack((real_part, imag_part))
    pattern = "kb,...bc->...kc"
    cos_terms = jnp.einsum(pattern, cosine, stacked, precision=highest)
    sin_terms = jnp.einsum(pattern, sine, stacked, precision=highest)
    return (cos_terms[0] - sign * sin_terms[1], cos_terms[1] + sign * sin_terms[0])


def back_to_blocks(real_part, imag_part, length):
    doubled = real_part.shape[1]
    cosine, sine = angle_tables(counting(doubled // 2), counting(doubled), doubled)
    result = jnp.einsum("ak,sk...->sa...", cosine, real_part, precision=highest)
    result = result - jnp.einsum("ak,sk...->sa...", sine, imag_part, precision=highest)
    return result / length


def to_spectra(series):
    seq_count = lax.axis_size("seq")
    tokens_dev = series.shape[1]
    length = 2 * seq_count * tokens_dev
    blocks = lax.all_to_all(series[:, None], "seq", split_axis=2, concat_axis=1, tiled=True)
    per_dev = blocks.shape[2]
    real_part, imag_part = across_blocks(blocks)
    device_slots = lax.axis_index("seq") * per_dev + counting(per_dev)
    cosine, sine = angle_tables(counting(2 * seq_count), device_slots, length)
    real_part, imag_part = rotate(real_part, imag_part, cosine[:, :, None], sine[:, :, None], -1.0)
    stacked = jnp.stack((real_part, imag_part), 1)
    stacked = stacked.reshape(stacked.shape[0], 2, 2 * seq_count, 1, per_dev, stacked.shape[4])
    moved = lax.all_to_all(stacked, "seq", split_axis=2, concat_axis=3, tiled=True)
    moved = moved.reshape(moved.shape[0], 2, moved.shape[2], tokens_dev, moved.shape[5])
    result = within_blocks(moved[:, 0], moved[:, 1], -1.0)
    return result


def from_spectra(real_part, imag_part):
    seq_count = lax.axis_size("seq")
    tokens_dev = real_part.shape[2]
    length = 2 * seq_count * tokens_dev
    per_dev = tokens_dev // seq_count
    real_part, imag_part = within_blocks(real_part, imag_part, 1.0)
    stacked = jnp.stack((real_part, imag_part), 1)
    stacked = stacked.reshape(
        stacked.shape[0], 2, stacked.shape[2], seq_count, per_dev, stacked.shape[4]
    )
    moved = lax.all_to_all(stacked, "seq", split_axis=3, concat_axis=2, tiled=True)
    moved = moved.reshape(moved.shape[0], 2, moved.shape[2], per_dev, moved.shape[5])
    device_slots = lax.axis_index("seq") * per_dev + counting(per_dev)
    cosine, sine = angle_tables(counting(2 * seq_count), device_slots, length)
    real_part, imag_part = rotate(
        moved[:, 0], moved[:, 1], cosine[:, :, None], sine[:, :, None], 1.0
    )
    values = back_to_blocks(real_part, imag_part, length)
    moved_back = lax.all_to_all(values, "seq", split_axis=1, concat_axis=2, tiled=True)
    result = moved_back[:, 0]
    return result


def on_device(
    residual, query_feats, key_feats, value_feats, filters, cotangent, skip_bias, norm_gain
):
    total_width = float(residual.shape[1] * lax.axis_size("chan"))
    query_wide = query_feats.astype(jnp.float32)
    key_wide = key_feats.astype(jnp.float32)
    value_wide = value_feats.astype(jnp.float32)
    product = (key_wide * value_wide).astype(jnp.bfloat16)
    product_wide = product.astype(jnp.float32)
    real_part, imag_part = to_spectra(jnp.stack((product, filters), 0))
    prod_real, prod_imag = (real_part[0], imag_part[0])
    filt_real, filt_imag = (real_part[1], imag_part[1])
    conv_real = prod_real * filt_real - prod_imag * filt_imag
    convolution_imaginary = prod_real * filt_imag + prod_imag * filt_real
    conv = from_spectra(conv_real[None], convolution_imaginary[None])[0]
    mixed = conv + skip_bias[None, :] * product_wide
    summed = residual.astype(jnp.float32) + query_wide * mixed
    grad_wide = cotangent.astype(jnp.float32)
    scaled_grad = grad_wide * norm_gain[None, :]
    square_sum, inner_sum = lax.psum(
        (jnp.sum(summed * summed, axis=1), jnp.sum(scaled_grad * summed, axis=1)), "chan"
    )
    inv_rms = lax.rsqrt(square_sum / total_width + epsilon)
    normed = (summed * inv_rms[:, None] * norm_gain[None, :]).astype(jnp.bfloat16)
    grad_summed = (
        inv_rms[:, None] * scaled_grad - summed * (inv_rms**3 * inner_sum / total_width)[:, None]
    )
    grad_residual = grad_summed.astype(jnp.bfloat16)
    grad_query = (grad_summed * mixed).astype(jnp.bfloat16)
    grad_mixed = (grad_summed * query_wide).astype(jnp.bfloat16)
    mixed_back = grad_mixed.astype(jnp.float32)
    back_real, back_imag = to_spectra(grad_mixed[None])
    back_real, back_imag = (back_real[0], back_imag[0])
    lag_real = jnp.stack(
        (
            filt_real * back_real + filt_imag * back_imag,
            prod_real * back_real + prod_imag * back_imag,
        )
    )
    lag_imag = jnp.stack(
        (
            filt_real * back_imag - filt_imag * back_real,
            prod_real * back_imag - prod_imag * back_real,
        )
    )
    lagged = from_spectra(lag_real, lag_imag)
    grad_product = lagged[0] + skip_bias[None, :] * mixed_back
    grad_key = (grad_product * value_wide).astype(jnp.bfloat16)
    grad_value = (grad_product * key_wide).astype(jnp.bfloat16)
    grad_filter = lagged[1]
    grad_bias, grad_gain = lax.psum(
        (
            jnp.sum(mixed_back * product_wide, axis=0),
            jnp.sum(grad_wide * summed * inv_rms[:, None], axis=0),
        ),
        "seq",
    )
    return (
        normed,
        grad_residual,
        grad_query,
        grad_key,
        grad_value,
        grad_filter,
        grad_bias,
        grad_gain,
    )


def solution(mesh):
    return jax.shard_map(
        on_device,
        mesh=mesh,
        in_specs=(
            P("seq", "chan"),
            P("seq", "chan"),
            P("seq", "chan"),
            P("seq", "chan"),
            P("seq", "chan"),
            P("seq", "chan"),
            P("chan"),
            P("chan"),
        ),
        out_specs=(
            P("seq", "chan"),
            P("seq", "chan"),
            P("seq", "chan"),
            P("seq", "chan"),
            P("seq", "chan"),
            P("seq", "chan"),
            P("chan"),
            P("chan"),
        ),
        check_vma=False,
    )
```

profile of v0, /device:TPU:2, one launch (start us, length us, event | category | flops | bytes accessed | tf_op | source)
XLA Modules:
  0.0 750.0 jit_solution(6019205565151572169)
XLA Ops:
  4.1 12.1 %all-to-all-start = ((bf16[2,1,128,1024]{3,0,1,2:T(2,128)(2,1)}), bf16[2,1,128,1024]{3,0,1,2:T(2,128)(2,1)S(1)}, u32[]{:S(2)}, u32[]{:S(2)}) async-start(bf16[2,1,128,1024]{3,0,1,2:T(2,128)(2,1)} %copy.85), calls=%async_computation | async-start | bytes 1048576 | tf_op jit(solution)/shard_map/all_to_all | solution.py:60
  16.3 16.9 %all-to-all-done = bf16[2,1,128,1024]{3,0,1,2:T(2,128)(2,1)S(1)} async-done(((bf16[2,1,128,1024]{3,0,1,2:T(2,128)(2,1)}), bf16[2,1,128,1024]{3,0,1,2:T(2,128)(2,1)S(1)}, u32[]{:S(2)}, u32[]{:S(2)}) %all-to-all-start) | async-done | bytes 524320 | tf_op jit(solution)/shard_map/all_to_all | solution.py:60
  38.4 7.3 copy.88
  45.8 100.7 %all_to_all.99 = f32[2,2,128,1,2,1024]{5,4,0,1,3,2:T(2,128)S(1)} all-to-all(f32[2,2,128,1,2,1024]{5,4,0,1,3,2:T(2,128)} %copy.88), channel_id=1, replica_groups=mesh['seq'=64,'chan'=4] {'seq'}, dimensions={2} | all-to-all | bytes 8388608 | tf_op jit(solution)/shard_map/all_to_all | solution.py:68
  156.4 4.3 copy.139
  160.7 5.6 fusion.5
  166.3 3.8 fusion.4
  187.6 6.1 all-to-all-start.2
  194.0 49.0 %all-to-all-done.2 = f32[1,2,2,64,2,1024]{5,4,2,1,0,3:T(2,128)} async-done(((f32[1,2,2,64,2,1024]{5,4,2,1,0,3:T(2,128)}), f32[1,2,2,64,2,1024]{5,4,2,1,0,3:T(2,128)}, u32[]{:S(2)}, u32[]{:S(2)}) %all-to-all-start.2) | async-done | bytes 2097184 | tf_op jit(solution)/shard_map/all_to_all | solution.py:84
  249.3 22.0 %all_to_all.100 = f32[1,64,2,1024]{3,2,0,1:T(2,128)S(1)} all-to-all(f32[1,64,2,1024]{3,2,0,1:T(2,128)S(1)} %copy.102), channel_id=1, replica_groups=mesh['seq'=64,'chan'=4] {'seq'}, dimensions={1} | all-to-all | bytes 1048576 | tf_op jit(solution)/shard_map/all_to_all | solution.py:92
  272.9 11.8 %psum.28 = f32[128]{0:T(128)S(1)} all-reduce(f32[128]{0:T(128)S(1)} %get-tuple-element.17), channel_id=1, replica_groups=mesh['seq'=64,'chan'=4] {'chan'}, use_global_device_ids=true, to_apply=%region_1.2 | all-reduce | flops 128 | bytes 1024 | tf_op jit(solution)/shard_map/psum | solution.py:116
  285.9 11.9 %psum.29 = f32[128]{0:T(128)S(1)} all-reduce(f32[128]{0:T(128)S(1)} %get-tuple-element.9), channel_id=1, replica_groups=mesh['seq'=64,'chan'=4] {'chan'}, use_global_device_ids=true, to_apply=%region_3.4 | all-reduce | flops 128 | bytes 1024 | tf_op jit(solution)/shard_map/psum | solution.py:116
  304.0 16.6 %all_to_all.101 = bf16[64,2,1024]{2,1,0:T(2,128)(2,1)S(1)} all-to-all(bf16[64,2,1024]{2,1,0:T(2,128)(2,1)S(1)} %reshape.402), channel_id=1, replica_groups=mesh['seq'=64,'chan'=4] {'seq'}, dimensions={0} | all-to-all | bytes 524288 | tf_op jit(solution)/shard_map/all_to_all | solution.py:60
  325.5 4.2 copy.106
  329.8 53.6 %all_to_all.102 = f32[1,2,128,1,2,1024]{5,4,1,3,0,2:T(2,128)S(1)} all-to-all(f32[1,2,128,1,2,1024]{5,4,1,3,0,2:T(2,128)} %copy.106), channel_id=1, replica_groups=mesh['seq'=64,'chan'=4] {'seq'}, dimensions={2} | all-to-all | bytes 4194304 | tf_op jit(solution)/shard_map/all_to_all | solution.py:68
  397.6 4.6 fusion.7
  402.2 4.7 fusion.6
  409.1 3.5 sub.108
  414.8 4.4 pad_maximum_fusion.2
  421.9 99.9 %all_to_all.103 = f32[2,2,2,64,2,1024]{5,4,2,1,0,3:T(2,128)S(1)} all-to-all(f32[2,2,2,64,2,1024]{5,4,2,1,0,3:T(2,128)S(1)} %copy.136), channel_id=1, replica_groups=mesh['seq'=64,'chan'=4] {'seq'}, dimensions={3} | all-to-all | bytes 8388608 | tf_op jit(solution)/shard_map/all_to_all | solution.py:84
  530.5 4.1 copy.143
  534.6 4.5 fusion.11
  543.7 6.0 all-to-all-start.7
  549.7 197.2 %all-reduce = (f32[1024]{0:T(1024)}, f32[1024]{0:T(1024)}) all-reduce(f32[1024]{0:T(1024)S(1)} %get-tuple-element.12, f32[1024]{0:T(1024)S(1)} %get-tuple-element.8), channel_id=1, replica_groups=mesh['seq'=64,'chan'=4] {'seq'}, use_global_device_ids=true, to_apply=%region_5.6 | all-reduce | flops 2048 | bytes 16384 | tf_op jit(solution)/shard_map/psum | solution.py:147
  (89 shorter events, 93.6 us)
Async XLA Ops:
  4.1 29.1 %all-to-all-start = ((bf16[2,1,128,1024]{3,0,1,2:T(2,128)(2,1)}), bf16[2,1,128,1024]{3,0,1,2:T(2,128)(2,1)S(1)}, u32[]{:S(2)}, u32[]{:S(2)}) async-start(bf16[2,1,128,1024]{3,0,1,2:T(2,128)(2,1)} %copy.85), calls=%async_computation | async-start | bytes 1048576 | tf_op jit(solution)/shard_map/all_to_all | solution.py:60
  160.7 5.6 copy-start.3
  170.6 1.3 copy-start
  187.6 55.4 %all-to-all-start.2 = ((f32[1,2,2,64,2,1024]{5,4,2,1,0,3:T(2,128)}), f32[1,2,2,64,2,1024]{5,4,2,1,0,3:T(2,128)}, u32[]{:S(2)}, u32[]{:S(2)}) async-start(f32[1,2,2,64,2,1024]{5,4,2,1,0,3:T(2,128)} %copy.135), calls=%async_computation.2 | async-start | bytes 4194304 | tf_op jit(solution)/shard_map/all_to_all | solution.py:84
  248.8 22.8 %copy-start.9 = (f32[1024]{0:T(1024)S(1)}, f32[1024]{0:T(1024)}, u32[]{:S(2)}) copy-start(f32[1024]{0:T(1024)} %param.14) | copy-start | bytes 12292
  249.3 35.5 %copy-start.10 = (f32[1024]{0:T(1024)S(1)}, f32[1024]{0:T(1024)}, u32[]{:S(2)}) copy-start(f32[1024]{0:T(1024)} %param.15) | copy-start | bytes 12292
  300.1 0.7 copy-start.5
  391.2 3.4 copy-start.4
  394.6 2.1 copy-start.1
  534.6 4.5 copy-start.2
  543.7 203.3 %all-to-all-start.7 = ((f32[2,64,2,1024]{3,2,0,1:T(2,128)}), f32[2,64,2,1024]{3,2,0,1:T(2,128)S(1)}, u32[]{:S(2)}, u32[]{:S(2)}) async-start(f32[2,64,2,1024]{3,2,0,1:T(2,128)} %copy.120), calls=%async_computation.7 | async-start | bytes 2097152 | tf_op jit(solution)/shard_map/all_to_all | solution.py:92
  747.0 1.6 copy-start.6
  747.0 1.6 copy-start.7
  747.0 1.6 copy-start.8
where the time goes:
time: 756 us; the launch traced here: 750 us
  blocking collectives  514 us (68%)
  local copies, waits for them, and re-layouts  74.8 us (10%)
  waiting for transfers between devices  65.9 us (9%)
  matrix products  42.8 us (6%)
  other arithmetic  27 us (4%)
  starting transfers between devices  24.3 us (3%)
    psum x1, blocking collectives, on_device(): lax.psum((jnp.sum(mixed_back * product_wide, axis=0), jnp.sum(grad_wide *...  197 us
    all_to_all x2, blocking collectives, to_spectra(): lax.all_to_all(stacked, 'seq', split_axis=2, concat_axis=3, tiled=True)  154 us
    all_to_all x1, blocking collectives, from_spectra(): lax.all_to_all(stacked, 'seq', split_axis=3, concat_axis=2, tiled=True)  99.9 us
    all_to_all x1, waiting for transfers between devices, from_spectra(): lax.all_to_all(stacked, 'seq', split_axis=3, concat_axis=2, tiled=True)  49 us
    psum x2, blocking collectives, on_device(): lax.psum((jnp.sum(summed * summed, axis=1), jnp.sum(scaled_grad * summed,...  23.7 us
    all_to_all x1, blocking collectives, from_spectra(): lax.all_to_all(values, 'seq', split_axis=1, concat_axis=2, tiled=True)  22 us
    unnamed x31, local copies, waits for them, and re-layouts  20.5 us
    all_to_all x1, waiting for transfers between devices, to_spectra(): lax.all_to_all(series[:, None], 'seq', split_axis=2, concat_axis=1, tiled...  16.9 us
  transfers between devices with their start and end apart: 3, of which 2 were waited for; matrix products, arithmetic and copies ran while one was open for 0% of the time, Pallas kernels for 0%

commit v1 on v0

v1 whole, which is shorter than its diff:
```python
import functools
import math

import jax
import jax.numpy as jnp
import ml_dtypes
import numpy as np
from jax import lax
from jax.experimental import pallas as pl
from jax.experimental.pallas import tpu as pltpu
from jax.sharding import PartitionSpec as P

epsilon = 1e-06
f32 = jnp.float32
bf16 = jnp.bfloat16


def split_host(table):
    high = table.astype(ml_dtypes.bfloat16)
    low = (table - high.astype(np.float64)).astype(ml_dtypes.bfloat16)
    return high, low


@functools.cache
def tables(blocks, lanes):
    length = 2 * blocks * lanes
    k1 = np.arange(blocks)[:, None] + 0.5
    a = np.arange(blocks)[None, :]
    angle = 2.0 * np.pi * k1 * a / (2 * blocks)
    outer = np.concatenate((np.cos(angle), -np.sin(angle)), 0)
    outer_high, outer_low = split_host(outer)
    first = np.concatenate((outer_high, outer_low), 1)
    back = outer.T * (2.0 / length)
    back_high, back_low = split_host(back)
    last = np.concatenate((back_high, back_low, back_high), 1)
    b = np.arange(lanes)[None, :]
    angle = 2.0 * np.pi * k1 * b / length
    twiddle = np.concatenate((np.cos(angle), np.sin(angle)), 0).astype(np.float32)
    angle = 2.0 * np.pi * (np.arange(lanes)[:, None] * b % lanes) / lanes
    cosine, sine = np.cos(angle), np.sin(angle)
    inner = np.block([[cosine, -sine], [sine, cosine]])
    inner_high, inner_low = split_host(inner)
    inverse_high, inverse_low = split_host(inner.T)
    return (first, last, twiddle, inner_high, inner_low, inverse_high, inverse_low)


def split(values):
    high = values.astype(bf16)
    low = (values - high.astype(f32)).astype(bf16)
    return high, low


def matmul(left, right):
    return jnp.dot(left, right, preferred_element_type=f32)


def forward(series_ref, stride, rows, first_ref, twiddle_ref, high_ref, low_ref, uh_ref, ul_ref):
    blocks = first_ref.shape[0] // 2
    lanes = twiddle_ref.shape[1]
    cosine = twiddle_ref[:blocks]
    sine = twiddle_ref[blocks:]
    for pair in range(rows // 2):
        columns = []
        for row in (2 * pair, 2 * pair + 1):
            x = series_ref[pl.ds(row, blocks, stride=stride), :].astype(bf16)
            columns.append(jnp.concatenate((x, x), 0))
        out = matmul(first_ref[...], jnp.concatenate(columns, 1))
        for i in range(2):
            re = out[:blocks, i * lanes : (i + 1) * lanes]
            im = out[blocks:, i * lanes : (i + 1) * lanes]
            here = pl.ds((2 * pair + i) * blocks, blocks)
            uh, ul = split(re * cosine + im * sine)
            uh_ref[here, :lanes] = uh
            ul_ref[here, :lanes] = ul
            uh, ul = split(im * cosine - re * sine)
            uh_ref[here, lanes:] = uh
            ul_ref[here, lanes:] = ul
    count = rows * blocks
    uh, ul = uh_ref[:count], ul_ref[:count]
    return matmul(uh, high_ref[...]) + matmul(ul, high_ref[...]) + matmul(uh, low_ref[...])


def inverse(rows, last_ref, twiddle_ref, high_ref, low_ref, uh_ref, ul_ref, z_ref, out_ref, stride):
    blocks = last_ref.shape[0]
    lanes = twiddle_ref.shape[1]
    cosine = twiddle_ref[:blocks]
    sine = twiddle_ref[blocks:]
    count = rows * blocks
    uh, ul = uh_ref[:count], ul_ref[:count]
    z_ref[:count] = matmul(uh, high_ref[...]) + matmul(ul, high_ref[...]) + matmul(uh, low_ref[...])
    for pair in range(rows // 2):
        columns = []
        for row in (2 * pair, 2 * pair + 1):
            re = z_ref[pl.ds(row * blocks, blocks), :lanes]
            im = z_ref[pl.ds(row * blocks, blocks), lanes:]
            zh, zl = split(
                jnp.concatenate((re * cosine - im * sine, im * cosine + re * sine), 0)
            )
            columns.append(jnp.concatenate((zh, zh, zl), 0))
        out = matmul(last_ref[...], jnp.concatenate(columns, 1))
        for i in range(2):
            out_ref[pl.ds(2 * pair + i, blocks, stride=stride), :] = out[
                :, i * lanes : (i + 1) * lanes
            ]


def conv_kernel(
    recv_ref, skip_ref, first_ref, last_ref, twiddle_ref, high_ref, low_ref, ihigh_ref, ilow_ref,
    mixed_ref, spec_ref, x_ref, uh_ref, ul_ref, z_ref, y_ref,
):
    blocks, rows, lanes = recv_ref.shape
    channels = rows // 2
    half = channels * blocks
    x_ref[...] = recv_ref[...].astype(f32).reshape(blocks * rows, lanes)
    spec_ref[...] = forward(
        x_ref, rows, rows, first_ref, twiddle_ref, high_ref, low_ref, uh_ref, ul_ref
    )
    for c in range(channels):
        prod = pl.ds(c * blocks, blocks)
        filt = pl.ds(half + c * blocks, blocks)
        fre = spec_ref[filt, :lanes] + skip_ref[c]
        spec_ref[filt, :lanes] = fre
        fim = spec_ref[filt, lanes:]
        pre, pim = spec_ref[prod, :lanes], spec_ref[prod, lanes:]
        uh_ref[prod, :lanes], ul_ref[prod, :lanes] = split(pre * fre - pim * fim)
        uh_ref[prod, lanes:], ul_ref[prod, lanes:] = split(pre * fim + pim * fre)
    inverse(
        channels, last_ref, twiddle_ref, ihigh_ref, ilow_ref, uh_ref, ul_ref, z_ref, y_ref, channels
    )
    mixed_ref[...] = y_ref[...].reshape(blocks, channels, lanes).astype(bf16)


def lag_kernel(
    recv_ref, spec_ref, first_ref, last_ref, twiddle_ref, high_ref, low_ref, ihigh_ref, ilow_ref,
    out_ref, x_ref, g_ref, uh_ref, ul_ref, z_ref, y_ref,
):
    blocks, rows, lanes = recv_ref.shape
    channels = rows // 2
    half = channels * blocks
    x_ref[...] = recv_ref[:, :channels, :].astype(f32).reshape(half, lanes)
    gain = jnp.sum(recv_ref[:, channels:, :].astype(f32), axis=0)
    gain = jnp.sum(gain, axis=1, keepdims=True) * (2.0 / lanes)
    g_ref[...] = forward(
        x_ref, channels, channels, first_ref, twiddle_ref, high_ref, low_ref, uh_ref, ul_ref
    )
    for c in range(channels):
        prod = pl.ds(c * blocks, blocks)
        filt = pl.ds(half + c * blocks, blocks)
        gre, gim = g_ref[prod, :lanes], g_ref[prod, lanes:]
        for source, target in ((filt, prod), (prod, filt)):
            sre, sim = spec_ref[source, :lanes], spec_ref[source, lanes:]
            uh_ref[target, :lanes], ul_ref[target, :lanes] = split(sre * gre + sim * gim)
            uh_ref[target, lanes:], ul_ref[target, lanes:] = split(sre * gim - sim * gre)
    inverse(
        rows, last_ref, twiddle_ref, ihigh_ref, ilow_ref, uh_ref, ul_ref, z_ref, y_ref, rows
    )
    out_ref[:, :rows, :] = y_ref[...].reshape(blocks, rows, lanes).astype(bf16)
    bias = y_ref[channels:rows, 0:1]
    lane = lax.broadcasted_iota(jnp.int32, (channels, lanes), 1)
    quarter = lanes // 4
    value = jnp.where(lane < 2 * quarter, bias, gain)
    vh = value.astype(bf16).astype(f32)
    value = jnp.where((lane // quarter) % 2 == 0, vh, value - vh).astype(bf16)
    out_ref[:, rows:, :] = jnp.broadcast_to(value[None], (blocks, channels, lanes))


def send_kernel(key_ref, value_ref, filters_ref, out_ref):
    tokens, width = key_ref.shape
    peers, rows, _ = out_ref.shape
    channels = rows // 2
    group = tokens // channels
    for j in range(width // tokens):
        cols = pl.ds(j * tokens, tokens)
        dest = pl.ds(j * group, group)
        product = key_ref[:, cols].astype(f32) * value_ref[:, cols].astype(f32)
        out_ref[dest, :channels, :] = product.astype(bf16).T.reshape(group, channels, tokens)
        out_ref[dest, channels:, :] = filters_ref[:, cols].T.reshape(group, channels, tokens)


def turn_kernel(residual_ref, query_ref, cotangent_ref, gain_ref, res_ref, q_ref, g_ref, sg_ref):
    tokens, width = residual_ref.shape
    for j in range(width // tokens):
        cols = pl.ds(j * tokens, tokens)
        res_ref[cols, :] = residual_ref[:, cols].T
        q_ref[cols, :] = query_ref[:, cols].T
        g_ref[cols, :] = cotangent_ref[:, cols].T
        sg_ref[cols, :] = (cotangent_ref[:, cols].astype(f32) * gain_ref[:, cols]).T


def sums_kernel(mixed_ref, res_ref, q_ref, sg_ref, out_ref):
    width, tokens = res_ref.shape
    summed = res_ref[...].astype(f32) + q_ref[...].astype(f32) * mixed_ref[...].astype(f32)
    out_ref[0:1, :] = jnp.sum(summed * summed, axis=0, keepdims=True)
    out_ref[1:2, :] = jnp.sum(sg_ref[...] * summed, axis=0, keepdims=True)


def norm_terms(sums_ref, total):
    inv_rms = lax.rsqrt(sums_ref[0:1, :] * (1.0 / total) + epsilon)
    alpha = inv_rms * inv_rms * inv_rms * sums_ref[1:2, :] * (1.0 / total)
    return inv_rms, alpha


def grad_kernel(total, sums_ref, mixed_ref, res_ref, q_ref, g_ref, sg_ref, out_ref):
    width, tokens = res_ref.shape
    peers, rows, _ = out_ref.shape
    channels = rows // 2
    inv_rms, alpha = norm_terms(sums_ref, total)
    lane = lax.broadcasted_iota(jnp.int32, (tokens, tokens), 1)
    group = tokens // channels
    for j in range(width // tokens):
        cols = pl.ds(j * tokens, tokens)
        dest = pl.ds(j * group, group)
        query = q_ref[cols, :].astype(f32)
        summed = res_ref[cols, :].astype(f32) + query * mixed_ref[cols, :].astype(f32)
        grad_summed = inv_rms * sg_ref[cols, :] - summed * alpha
        out_ref[dest, :channels, :] = (
            (grad_summed * query).astype(bf16).reshape(group, channels, tokens)
        )
        part = g_ref[cols, :].astype(f32) * (summed * inv_rms)
        part = jnp.sum(part, axis=1, keepdims=True)
        ph = part.astype(bf16).astype(f32)
        part = jnp.where(lane < tokens // 2, ph, part - ph).astype(bf16)
        out_ref[dest, channels:, :] = part.reshape(group, channels, tokens)


def norm_kernel(
    total, sums_ref, mixed_ref, res_ref, q_ref, sg_ref, gain_ref, normed_ref, gres_ref, gq_ref
):
    width, tokens = res_ref.shape
    inv_rms, alpha = norm_terms(sums_ref, total)
    for j in range(width // tokens):
        cols = pl.ds(j * tokens, tokens)
        mixed = mixed_ref[cols, :].astype(f32)
        summed = res_ref[cols, :].astype(f32) + q_ref[cols, :].astype(f32) * mixed
        grad_summed = inv_rms * sg_ref[cols, :] - summed * alpha
        normed_ref[:, cols] = ((summed * inv_rms).T * gain_ref[:, cols]).astype(bf16)
        gres_ref[:, cols] = grad_summed.astype(bf16).T
        gq_ref[:, cols] = (grad_summed * mixed).astype(bf16).T


def finish_kernel(recv_ref, key_ref, value_ref, gk_ref, gv_ref, gf_ref, sums_ref):
    tokens, width = key_ref.shape
    peers, rows, _ = recv_ref.shape
    channels = rows // 3
    group = tokens // channels
    quarter = tokens // 4
    for j in range(width // tokens):
        cols = pl.ds(j * tokens, tokens)
        dest = pl.ds(j * group, group)
        back = recv_ref[dest, :channels, :].reshape(tokens, tokens).T.astype(f32)
        gk_ref[:, cols] = (back * value_ref[:, cols].astype(f32)).astype(bf16)
        gv_ref[:, cols] = (back * key_ref[:, cols].astype(f32)).astype(bf16)
        gf_ref[:, cols] = (
            recv_ref[dest, channels : 2 * channels, :].reshape(tokens, tokens).T.astype(f32)
        )
        aux = recv_ref[dest, 2 * channels :, :].reshape(tokens, tokens).T.astype(f32)
        sums_ref[0:1, cols] = aux[0:1] + aux[quarter : quarter + 1]
        sums_ref[1:2, cols] = aux[2 * quarter : 2 * quarter + 1] + aux[3 * quarter : 3 * quarter + 1]


def call(kernel, out_shape, scratch=(), cost=None, smem=None, n_in=0):
    in_specs = [
        pl.BlockSpec(memory_space=pltpu.SMEM if i == smem else pltpu.VMEM) for i in range(n_in)
    ]
    return pl.pallas_call(
        kernel,
        out_shape=out_shape,
        in_specs=in_specs,
        out_specs=jax.tree.map(lambda _: pl.BlockSpec(memory_space=pltpu.VMEM), out_shape),
        scratch_shapes=list(scratch),
        compiler_params=pltpu.CompilerParams(vmem_limit_bytes=48 * 1024 * 1024),
        cost_estimate=cost,
    )


def shape(dims, dtype):
    return jax.ShapeDtypeStruct(dims, dtype)


def on_device(
    residual, query_feats, key_feats, value_feats, filters, cotangent, skip_bias, norm_gain
):
    tokens, width = residual.shape
    peers = lax.axis_size("seq")
    total = float(width * lax.axis_size("chan"))
    channels = width // peers
    constants = [jnp.asarray(t) for t in tables(peers, tokens)]
    half = channels * peers
    vm = pltpu.VMEM

    def exchange(values):
        return lax.all_to_all(values, "seq", split_axis=0, concat_axis=0, tiled=True)

    sent = call(send_kernel, shape((peers, 2 * channels, tokens), bf16), n_in=3)(
        key_feats, value_feats, filters
    )
    received = exchange(sent)
    gain_row = norm_gain[None, :]
    turned = (width, tokens)
    res_t, q_t, g_t, sg_t = call(
        turn_kernel,
        (shape(turned, bf16), shape(turned, bf16), shape(turned, bf16), shape(turned, f32)),
        n_in=4,
        cost=pl.CostEstimate(flops=10**6, bytes_accessed=4 * 10**6, transcendentals=0),
    )(residual, query_feats, cotangent, gain_row)
    skip_here = lax.dynamic_slice_in_dim(skip_bias, lax.axis_index("seq") * channels, channels)
    mixed_sent, spectra = call(
        conv_kernel,
        (shape((peers, channels, tokens), bf16), shape((2 * half, 2 * tokens), f32)),
        scratch=(
            vm((2 * half, tokens), f32),
            vm((2 * half, 2 * tokens), bf16),
            vm((2 * half, 2 * tokens), bf16),
            vm((half, 2 * tokens), f32),
            vm((half, tokens), f32),
        ),
        smem=1,
        n_in=9,
    )(received, skip_here, *constants)
    mixed_t = exchange(mixed_sent).reshape(width, tokens)
    sums = call(sums_kernel, shape((2, tokens), f32), n_in=4)(mixed_t, res_t, q_t, sg_t)
    sums = lax.psum(sums, "chan")
    grad_sent = call(
        functools.partial(grad_kernel, total), shape((peers, 2 * channels, tokens), bf16), n_in=6
    )(sums, mixed_t, res_t, q_t, g_t, sg_t)
    grad_received = exchange(grad_sent)
    plain = (tokens, width)
    normed, grad_residual, grad_query = call(
        functools.partial(norm_kernel, total),
        (shape(plain, bf16), shape(plain, bf16), shape(plain, bf16)),
        n_in=6,
        cost=pl.CostEstimate(flops=10**6, bytes_accessed=4 * 10**6, transcendentals=0),
    )(sums, mixed_t, res_t, q_t, sg_t, gain_row)
    lag_sent = call(
        lag_kernel,
        shape((peers, 3 * channels, tokens), bf16),
        scratch=(
            vm((half, tokens), f32),
            vm((half, 2 * tokens), f32),
            vm((2 * half, 2 * tokens), bf16),
            vm((2 * half, 2 * tokens), bf16),
            vm((2 * half, 2 * tokens), f32),
            vm((2 * half, tokens), f32),
        ),
        n_in=9,
    )(grad_received, spectra, *constants)
    lag_received = exchange(lag_sent)
    grad_key, grad_value, grad_filter, ends = call(
        finish_kernel,
        (shape(plain, bf16), shape(plain, bf16), shape(plain, f32), shape((2, width), f32)),
        n_in=3,
    )(lag_received, key_feats, value_feats)
    return (
        normed,
        grad_residual,
        grad_query,
        grad_key,
        grad_value,
        grad_filter,
        ends[0],
        ends[1],
    )


def solution(mesh):
    return jax.shard_map(
        on_device,
        mesh=mesh,
        in_specs=(P("seq", "chan"),) * 6 + (P("chan"),) * 2,
        out_specs=(P("seq", "chan"),) * 6 + (P("chan"),) * 2,
        check_vma=False,
    )
```

time: 756 us -> 126 us (0.17)
  blocking collectives: 514 us -> 32.4 us
  local copies, waits for them, and re-layouts: 74.8 us -> 7.19 us
  matrix products: 42.8 us -> 0 us
  other arithmetic: 27 us -> 0 us
  waiting for transfers between devices: 65.9 us -> 46.3 us
  Pallas kernels: 0 us -> 14.5 us
    all_to_all x5 -> x1, blocking collectives: 293 us -> 21.2 us  [exchange(): lax.all_to_all(values, 'seq', split_axis=0, concat_axis=0, tiled=True)]
    psum x3 -> x1, blocking collectives: 221 us -> 11.2 us  [on_device(): sums = lax.psum(sums, 'chan')]
    dot_general x16 -> x0, matrix products: 42.8 us -> none  [the longest x4 15.8 us: within_blocks(): sin_terms = jnp.einsum(pattern, sine, stacked, precision=highest)]
    all_to_all x3, waiting for transfers between devices: 65.9 us -> 46.3 us  [exchange(): lax.all_to_all(values, 'seq', split_axis=0, concat_axis=0, tiled=True)]
    unnamed x31 -> x36, local copies, waits for them, and re-layouts: 20.5 us -> 5.82 us
    pallas_call x0 -> x8, Pallas kernels: none -> 14.5 us  [the longest x1 5.09 us: on_device(): call(conv_kernel, (shape((peers, channels, tokens), bf16), shape((2 * hal...]
    all_to_all x7 -> x0, local copies, waits for them, and re-layouts: 12.2 us -> none  [the longest x4 5.6 us: to_spectra(): lax.all_to_all(stacked, 'seq', split_axis=2, concat_axis=3, tiled=True)]
    reshape x2 -> x0, local copies, waits for them, and re-layouts: 11.6 us -> none  [to_spectra(): stacked.reshape(stacked.shape[0], 2, 2 * seq_count, 1, per_dev, stacked.s...]
  transfers between devices with their start and end apart: 3 -> 3, of which waited for: 2 -> 3; matrix products, arithmetic and copies ran while one was open for 0% -> 1% of each run, Pallas kernels for 0% -> 1%
where the time goes in v1:
time: 126 us; the launch traced here: 125 us
  waiting for transfers between devices  46.3 us (37%)
  blocking collectives  32.4 us (26%)
  starting transfers between devices  24.1 us (19%)
  Pallas kernels  14.5 us (12%)
  local copies, waits for them, and re-layouts  7.19 us (6%)
    all_to_all x3, waiting for transfers between devices, exchange(): lax.all_to_all(values, 'seq', split_axis=0, concat_axis=0, tiled=True)  46.3 us
    all_to_all x3, starting transfers between devices, exchange(): lax.all_to_all(values, 'seq', split_axis=0, concat_axis=0, tiled=True)  24.1 us
    all_to_all x1, blocking collectives, exchange(): lax.all_to_all(values, 'seq', split_axis=0, concat_axis=0, tiled=True)  21.2 us
    psum x1, blocking collectives, on_device(): sums = lax.psum(sums, 'chan')  11.2 us
    unnamed x36, local copies, waits for them, and re-layouts  5.82 us
    pallas_call x1, Pallas kernels, on_device(): call(conv_kernel, (shape((peers, channels, tokens), bf16), shape((2 * hal...  5.09 us
    pallas_call x1, Pallas kernels, on_device(): call(lag_kernel, shape((peers, 3 * channels, tokens), bf16), scratch=(vm(...  4.94 us
  transfers between devices with their start and end apart: 3, of which 3 were waited for; matrix products, arithmetic and copies ran while one was open for 1% of the time, Pallas kernels for 1%

profile of v1, /device:TPU:2, one launch (start us, length us, event | category | flops | bytes accessed | tf_op | source)
XLA Modules:
  0.0 125.2 jit_solution(12685402999792596224)
XLA Ops:
  0.6 0.9 copy-done.2
  1.6 0.9 copy-done.4
  2.5 0.9 copy-done.11
  3.5 0.0 copy-start.10
  3.6 1.0 shard_map.206
  4.6 12.1 %all-to-all-start = ((bf16[64,32,128]{2,1,0:T(8,128)(2,1)}), bf16[64,32,128]{2,1,0:T(8,128)(2,1)S(1)}, u32[]{:S(2)}, u32[]{:S(2)}) async-start(bf16[64,32,128]{2,1,0:T(8,128)(2,1)} %shard_map.206), calls=%async_computation | async-start | bytes 1048576 | tf_op jit(solution)/shard_map/all_to_all | solution.py:292
  16.7 0.8 dynamic_slice.3.skip_ref
  17.4 16.3 %all-to-all-done.recv_ref = bf16[64,32,128]{2,1,0:T(8,128)(2,1)S(1)} async-done(((bf16[64,32,128]{2,1,0:T(8,128)(2,1)}), bf16[64,32,128]{2,1,0:T(8,128)(2,1)S(1)}, u32[]{:S(2)}, u32[]{:S(2)}) %all-to-all-start) | async-done | bytes 524320 | tf_op jit(solution)/shard_map/all_to_all | solution.py:292
  33.7 5.1 %shard_map.207 = (bf16[64,16,128]{2,1,0:T(8,128)(2,1)}, f32[2048,256]{1,0:T(8,128)S(1)}) custom-call(bf16[64,32,128]{2,1,0:T(8,128)(2,1)S(1)} %all-to-all-done.recv_ref, f32[16]{0:T(128)S(1)} %dynamic_slice.3.skip_ref, bf16[128,128]{1,0:T(8,128)(2,1)S(1)} %copy-done.16, bf16[64,384]{1,0:T(8,128)(2,1)S(1)} %copy-done.15, f32[128,128]{1,0:T(8,128)S(1)} %copy-done.10, ...), custom_call_target="tpu_custom_call" | custom-call | tf_op jit(solution)/shard_map/pallas_call | solution.py:307
  38.8 1.3 %copy-done = f32[2048,256]{1,0:T(8,128)} copy-done((f32[2048,256]{1,0:T(8,128)}, f32[2048,256]{1,0:T(8,128)S(1)}, u32[]{:S(2)}) %copy-start) | copy-done | bytes 2097176
  40.2 5.9 %all-to-all-start.1 = ((bf16[64,16,128]{2,1,0:T(8,128)(2,1)}), bf16[64,16,128]{2,1,0:T(8,128)(2,1)S(1)}, u32[]{:S(2)}, u32[]{:S(2)}) async-start(bf16[64,16,128]{2,1,0:T(8,128)(2,1)} %get-tuple-element.21), calls=%async_computation.1 | async-start | bytes 524288 | tf_op jit(solution)/shard_map/all_to_all | solution.py:292
  46.1 0.5 shard_map.208
  46.6 10.4 %all-to-all-done.1 = bf16[64,16,128]{2,1,0:T(8,128)(2,1)S(1)} async-done(((bf16[64,16,128]{2,1,0:T(8,128)(2,1)}), bf16[64,16,128]{2,1,0:T(8,128)(2,1)S(1)}, u32[]{:S(2)}, u32[]{:S(2)}) %all-to-all-start.1) | async-done | bytes 262176 | tf_op jit(solution)/shard_map/all_to_all | solution.py:292
  57.0 0.3 shard_map.209
  57.2 11.2 %psum.7.sums_ref = f32[2,128]{1,0:T(2,128)S(1)} all-reduce(f32[2,128]{1,0:T(2,128)S(1)} %shard_map.209), channel_id=1, replica_groups=mesh['seq'=64,'chan'=4] {'chan'}, use_global_device_ids=true, to_apply=%region_0.0 | all-reduce | flops 256 | bytes 2048 | tf_op jit(solution)/shard_map/psum | solution.py:322
  68.4 0.3 shard_map.211
  68.8 21.2 %all_to_all.20.recv_ref = bf16[64,32,128]{2,1,0:T(8,128)(2,1)S(1)} all-to-all(bf16[64,32,128]{2,1,0:T(8,128)(2,1)S(1)} %shard_map.211), channel_id=1, replica_groups=mesh['seq'=64,'chan'=4] {'seq'}, dimensions={0} | all-to-all | bytes 1048576 | tf_op jit(solution)/shard_map/all_to_all | solution.py:292
  89.9 1.6 %copy-done.1 = f32[2048,256]{1,0:T(8,128)S(1)} copy-done((f32[2048,256]{1,0:T(8,128)S(1)}, f32[2048,256]{1,0:T(8,128)}, u32[]{:S(2)}) %copy-start.1) | copy-done | bytes 2097176
  91.5 4.9 %shard_map.212 = bf16[64,48,128]{2,1,0:T(8,128)(2,1)} custom-call(bf16[64,32,128]{2,1,0:T(8,128)(2,1)S(1)} %all_to_all.20.recv_ref, f32[2048,256]{1,0:T(8,128)S(1)} %copy-done.1, bf16[128,128]{1,0:T(8,128)(2,1)S(1)} %copy-done.16, bf16[64,384]{1,0:T(8,128)(2,1)S(1)} %copy-done.15, f32[128,128]{1,0:T(8,128)S(1)} %copy-done.10, ...), custom_call_target="tpu_custom_call" | custom-call | tf_op jit(solution)/shard_map/pallas_call | solution.py:334
  96.4 6.1 %all-to-all-start.3 = ((bf16[64,48,128]{2,1,0:T(8,128)(2,1)}), bf16[64,48,128]{2,1,0:T(8,128)(2,1)S(1)}, u32[]{:S(2)}, u32[]{:S(2)}) async-start(bf16[64,48,128]{2,1,0:T(8,128)(2,1)} %shard_map.212), calls=%async_computation.3 | async-start | bytes 1572864 | tf_op jit(solution)/shard_map/all_to_all | solution.py:292
  102.5 1.2 shard_map.210
  103.8 19.6 %all-to-all-done.3.recv_ref = bf16[64,48,128]{2,1,0:T(8,128)(2,1)S(1)} async-done(((bf16[64,48,128]{2,1,0:T(8,128)(2,1)}), bf16[64,48,128]{2,1,0:T(8,128)(2,1)S(1)}, u32[]{:S(2)}, u32[]{:S(2)}) %all-to-all-start.3) | async-done | bytes 786464 | tf_op jit(solution)/shard_map/all_to_all | solution.py:292
  123.4 1.2 shard_map.213
  124.6 0.6 fusion
  (30 shorter events, 0.1 us)
Async XLA Ops:
  0.6 1.0 copy-start.2
  1.6 0.9 copy-start.4
  2.5 0.9 copy-start.11
  3.5 30.2 %copy-start.6 = (bf16[256,256]{1,0:T(8,128)(2,1)S(1)}, bf16[256,256]{1,0:T(8,128)(2,1)}, u32[]{:S(2)}) copy-start(bf16[256,256]{1,0:T(8,128)(2,1)} %constant.29.clone.high_ref) | copy-start | bytes 393220
  3.5 30.2 %copy-start.7 = (bf16[256,256]{1,0:T(8,128)(2,1)S(1)}, bf16[256,256]{1,0:T(8,128)(2,1)}, u32[]{:S(2)}) copy-start(bf16[256,256]{1,0:T(8,128)(2,1)} %constant.30.clone.low_ref) | copy-start | bytes 393220
  3.5 30.2 %copy-start.8 = (bf16[256,256]{1,0:T(8,128)(2,1)S(1)}, bf16[256,256]{1,0:T(8,128)(2,1)}, u32[]{:S(2)}) copy-start(bf16[256,256]{1,0:T(8,128)(2,1)} %constant.31.clone.ihigh_ref) | copy-start | bytes 393220
  3.5 30.2 %copy-start.9 = (bf16[256,256]{1,0:T(8,128)(2,1)S(1)}, bf16[256,256]{1,0:T(8,128)(2,1)}, u32[]{:S(2)}) copy-start(bf16[256,256]{1,0:T(8,128)(2,1)} %constant.32.clone.ilow_ref) | copy-start | bytes 393220
  3.5 30.2 %copy-start.10 = (f32[128,128]{1,0:T(8,128)S(1)}, f32[128,128]{1,0:T(8,128)}, u32[]{:S(2)}) copy-start(f32[128,128]{1,0:T(8,128)} %constant.28.clone.twiddle_ref) | copy-start | bytes 196612
  3.5 30.2 %copy-start.15 = (bf16[64,384]{1,0:T(8,128)(2,1)S(1)}, bf16[64,384]{1,0:T(8,128)(2,1)}, u32[]{:S(2)}) copy-start(bf16[64,384]{1,0:T(8,128)(2,1)} %constant.27.clone.last_ref) | copy-start | bytes 147460
  3.5 30.2 %copy-start.16 = (bf16[128,128]{1,0:T(8,128)(2,1)S(1)}, bf16[128,128]{1,0:T(8,128)(2,1)}, u32[]{:S(2)}) copy-start(bf16[128,128]{1,0:T(8,128)(2,1)} %constant.26.clone.first_ref) | copy-start | bytes 98308
  3.5 42.5 %copy-start.12 = (bf16[128,1024]{1,0:T(8,128)(2,1)S(1)}, bf16[128,1024]{1,0:T(8,128)(2,1)}, u32[]{:S(2)}) copy-start(bf16[128,1024]{1,0:T(8,128)(2,1)} %residual_ref.1) | copy-start | bytes 786436
  3.5 42.5 %copy-start.13 = (bf16[128,1024]{1,0:T(8,128)(2,1)S(1)}, bf16[128,1024]{1,0:T(8,128)(2,1)}, u32[]{:S(2)}) copy-start(bf16[128,1024]{1,0:T(8,128)(2,1)} %query_ref.1) | copy-start | bytes 786436
  3.6 42.5 %copy-start.14 = (bf16[128,1024]{1,0:T(8,128)(2,1)S(1)}, bf16[128,1024]{1,0:T(8,128)(2,1)}, u32[]{:S(2)}) copy-start(bf16[128,1024]{1,0:T(8,128)(2,1)} %cotangent_ref.1) | copy-start | bytes 786436
  3.6 42.5 %copy-start.17 = (f32[1024]{0:T(1024)S(1)}, f32[1024]{0:T(1024)}, u32[]{:S(2)}) copy-start(f32[1024]{0:T(1024)} %param.22) | copy-start | bytes 12292
  4.6 29.1 %all-to-all-start = ((bf16[64,32,128]{2,1,0:T(8,128)(2,1)}), bf16[64,32,128]{2,1,0:T(8,128)(2,1)S(1)}, u32[]{:S(2)}, u32[]{:S(2)}) async-start(bf16[64,32,128]{2,1,0:T(8,128)(2,1)} %shard_map.206), calls=%async_computation | async-start | bytes 1048576 | tf_op jit(solution)/shard_map/all_to_all | solution.py:292
  38.8 1.3 %copy-start = (f32[2048,256]{1,0:T(8,128)}, f32[2048,256]{1,0:T(8,128)S(1)}, u32[]{:S(2)}) copy-start(f32[2048,256]{1,0:T(8,128)S(1)} %get-tuple-element.29.spec_ref) | copy-start | bytes 6291460
  40.2 16.8 %all-to-all-start.1 = ((bf16[64,16,128]{2,1,0:T(8,128)(2,1)}), bf16[64,16,128]{2,1,0:T(8,128)(2,1)S(1)}, u32[]{:S(2)}, u32[]{:S(2)}) async-start(bf16[64,16,128]{2,1,0:T(8,128)(2,1)} %get-tuple-element.21), calls=%async_computation.1 | async-start | bytes 524288 | tf_op jit(solution)/shard_map/all_to_all | solution.py:292
  89.9 1.6 %copy-start.1 = (f32[2048,256]{1,0:T(8,128)S(1)}, f32[2048,256]{1,0:T(8,128)}, u32[]{:S(2)}) copy-start(f32[2048,256]{1,0:T(8,128)} %copy-done) | copy-start | bytes 6291460
  96.4 26.9 %copy-start.3 = (bf16[128,1024]{1,0:T(8,128)(2,1)S(1)}, bf16[128,1024]{1,0:T(8,128)(2,1)}, u32[]{:S(2)}) copy-start(bf16[128,1024]{1,0:T(8,128)(2,1)} %key_ref.3) | copy-start | bytes 786436
  96.4 26.9 %copy-start.5 = (bf16[128,1024]{1,0:T(8,128)(2,1)S(1)}, bf16[128,1024]{1,0:T(8,128)(2,1)}, u32[]{:S(2)}) copy-start(bf16[128,1024]{1,0:T(8,128)(2,1)} %value_ref.3) | copy-start | bytes 786436
  96.4 26.9 %all-to-all-start.3 = ((bf16[64,48,128]{2,1,0:T(8,128)(2,1)}), bf16[64,48,128]{2,1,0:T(8,128)(2,1)S(1)}, u32[]{:S(2)}, u32[]{:S(2)}) async-start(bf16[64,48,128]{2,1,0:T(8,128)(2,1)} %shard_map.212), calls=%async_computation.3 | async-start | bytes 1572864 | tf_op jit(solution)/shard_map/all_to_all | solution.py:292

commit v2 on v1

v2 whole, which is shorter than its diff:
```python
import functools
import math

import jax
import jax.numpy as jnp
import ml_dtypes
import numpy as np
from jax import lax
from jax.experimental import pallas as pl
from jax.experimental.pallas import tpu as pltpu
from jax.sharding import PartitionSpec as P

epsilon = 1e-06
f32 = jnp.float32
bf16 = jnp.bfloat16


def split_host(table):
    high = table.astype(ml_dtypes.bfloat16)
    low = (table - high.astype(np.float64)).astype(ml_dtypes.bfloat16)
    return high, low


@functools.cache
def tables(blocks, lanes):
    length = 2 * blocks * lanes
    k1 = np.arange(blocks)[:, None] + 0.5
    a = np.arange(blocks)[None, :]
    angle = 2.0 * np.pi * k1 * a / (2 * blocks)
    outer = np.concatenate((np.cos(angle), -np.sin(angle)), 0)
    outer_high, outer_low = split_host(outer)
    first = np.concatenate((outer_high, outer_low), 1)
    back = outer.T * (2.0 / length)
    back_high, back_low = split_host(back)
    last = np.concatenate((back_high, back_low, back_high), 1)
    b = np.arange(lanes)[None, :]
    angle = 2.0 * np.pi * k1 * b / length
    twiddle = np.concatenate((np.cos(angle), np.sin(angle)), 0).astype(np.float32)
    angle = 2.0 * np.pi * (np.arange(lanes)[:, None] * b % lanes) / lanes
    cosine, sine = np.cos(angle), np.sin(angle)
    inner = np.block([[cosine, -sine], [sine, cosine]])
    inner_high, inner_low = split_host(inner)
    inner = np.concatenate((inner_high, inner_high, inner_low), 0)
    inverse_high, inverse_low = inner_high.T, inner_low.T
    inverse = np.concatenate((inverse_high, inverse_high, inverse_low), 0)
    return (first, last, twiddle, inner, inverse)


def split(values):
    high = values.astype(bf16)
    low = (values - high.astype(f32)).astype(bf16)
    return high, low


def matmul(left, right):
    return jnp.dot(left, right, preferred_element_type=f32)


def put(u_ref, here, offset, values):
    high, low = split(values)
    width = u_ref.shape[1] // 2
    lanes = values.shape[1]
    u_ref[here, offset : offset + lanes] = high
    u_ref[here, width + offset : width + offset + lanes] = low


def forward(series_ref, stride, rows, first_ref, twiddle_ref, inner_ref, u_ref, out_ref, copies=()):
    blocks = first_ref.shape[0] // 2
    lanes = twiddle_ref.shape[1]
    cosine = twiddle_ref[:blocks]
    sine = twiddle_ref[blocks:]
    for pair in range(rows // 2):
        columns = []
        for row in (2 * pair, 2 * pair + 1):
            x = series_ref[pl.ds(row, blocks, stride=stride), :].astype(bf16)
            columns.append(jnp.concatenate((x, x), 0))
        out = matmul(first_ref[...], jnp.concatenate(columns, 1))
        for i in range(2):
            re = out[:blocks, i * lanes : (i + 1) * lanes]
            im = out[blocks:, i * lanes : (i + 1) * lanes]
            here = pl.ds((2 * pair + i) * blocks, blocks)
            put(u_ref, here, 0, re * cosine + im * sine)
            put(u_ref, here, lanes, im * cosine - re * sine)
    n = 2 * lanes
    chunk = 4 * blocks
    for i in range(rows // 4):
        c = pl.ds(i * chunk, chunk)
        out_ref[c] = matmul(u_ref[c, : 2 * n], inner_ref[: 2 * n]) + matmul(
            u_ref[c, :n], inner_ref[2 * n :]
        )
        if copies:
            copies[i].start()


def inverse(rows, last_ref, twiddle_ref, inverse_ref, u_ref, z_ref, out_ref, stride):
    blocks = last_ref.shape[0]
    lanes = twiddle_ref.shape[1]
    cosine = twiddle_ref[:blocks]
    sine = twiddle_ref[blocks:]
    n = 2 * lanes
    chunk = 4 * blocks
    for i in range(rows // 4):
        c = pl.ds(i * chunk, chunk)
        z_ref[c] = matmul(u_ref[c, : 2 * n], inverse_ref[: 2 * n]) + matmul(
            u_ref[c, :n], inverse_ref[2 * n :]
        )
    for pair in range(rows // 2):
        columns = []
        for row in (2 * pair, 2 * pair + 1):
            re = z_ref[pl.ds(row * blocks, blocks), :lanes]
            im = z_ref[pl.ds(row * blocks, blocks), lanes:]
            zh, zl = split(
                jnp.concatenate((re * cosine - im * sine, im * cosine + re * sine), 0)
            )
            columns.append(jnp.concatenate((zh, zh, zl), 0))
        out = matmul(last_ref[...], jnp.concatenate(columns, 1))
        for i in range(2):
            out_ref[pl.ds(2 * pair + i, blocks, stride=stride), :] = out[
                :, i * lanes : (i + 1) * lanes
            ]


def copies_of(source_ref, target_ref, sems):
    count = sems.shape[0]
    chunk = source_ref.shape[0] // count
    return [
        pltpu.make_async_copy(
            source_ref.at[pl.ds(i * chunk, chunk)],
            target_ref.at[pl.ds(i * chunk, chunk)],
            sems.at[i],
        )
        for i in range(count)
    ]


def conv_kernel(
    recv_ref, skip_ref, first_ref, last_ref, twiddle_ref, inner_ref, inverse_ref,
    mixed_ref, kept_ref, spec_ref, x_ref, u_ref, z_ref, y_ref, sems,
):
    blocks, rows, lanes = recv_ref.shape
    channels = rows // 2
    half = channels * blocks
    wide = rows + 8
    for a in range(blocks):
        x_ref[pl.ds(a * wide, rows), :] = recv_ref[a].astype(f32)
    copies = copies_of(spec_ref, kept_ref, sems)
    forward(x_ref, wide, rows, first_ref, twiddle_ref, inner_ref, u_ref, spec_ref, copies)
    for c in range(channels):
        prod = pl.ds(c * blocks, blocks)
        filt = pl.ds(half + c * blocks, blocks)
        fre = spec_ref[filt, :lanes] + skip_ref[c]
        fim = spec_ref[filt, lanes:]
        pre, pim = spec_ref[prod, :lanes], spec_ref[prod, lanes:]
        put(u_ref, prod, 0, pre * fre - pim * fim)
        put(u_ref, prod, lanes, pre * fim + pim * fre)
    wide = channels + 8
    inverse(channels, last_ref, twiddle_ref, inverse_ref, u_ref, z_ref, y_ref, wide)
    for a in range(blocks):
        mixed_ref[a] = y_ref[pl.ds(a * wide, channels), :].astype(bf16)
    for copy in copies:
        copy.wait()


def lag_kernel(
    recv_ref, skip_ref, first_ref, last_ref, twiddle_ref, inner_ref, inverse_ref, kept_ref, *rest
):
    out_ref, spec_ref, x_ref, g_ref, u_ref, z_ref, y_ref, sems = rest[-8:]
    blocks, channels, lanes = recv_ref.shape
    rows = 2 * channels
    half = channels * blocks
    copies = copies_of(kept_ref, spec_ref, sems)
    ahead = len(copies) // 2
    for i in range(ahead):
        copies[i].start()
        copies[ahead + i].start()
    wide = channels + 8
    for a in range(blocks):
        x_ref[pl.ds(a * wide, channels), :] = recv_ref[a].astype(f32)
    forward(x_ref, wide, channels, first_ref, twiddle_ref, inner_ref, u_ref, g_ref)
    for c in range(channels):
        if c % (channels // ahead) == 0:
            copies[c * ahead // channels].wait()
            copies[ahead + c * ahead // channels].wait()
        prod = pl.ds(c * blocks, blocks)
        filt = pl.ds(half + c * blocks, blocks)
        gre, gim = g_ref[prod, :lanes], g_ref[prod, lanes:]
        for source, target in ((filt, prod), (prod, filt)):
            sre, sim = spec_ref[source, :lanes], spec_ref[source, lanes:]
            if source is filt:
                sre = sre + skip_ref[c]
            put(u_ref, target, 0, sre * gre + sim * gim)
            put(u_ref, target, lanes, sre * gim - sim * gre)
    wide = rows + 8
    inverse(rows, last_ref, twiddle_ref, inverse_ref, u_ref, z_ref, y_ref, wide)
    for a in range(blocks):
        out_ref[a] = y_ref[pl.ds(a * wide, rows), :].astype(bf16)


def send_kernel(
    key_hbm, value_hbm, filters_hbm, out_ref, key_ref, value_ref, filters_ref, sems
):
    tokens, width = key_ref.shape
    peers, rows, _ = out_ref.shape
    channels = rows // 2
    group = tokens // channels
    copies = [
        pltpu.make_async_copy(source, target, sems.at[i])
        for i, (source, target) in enumerate(
            ((filters_hbm, filters_ref), (key_hbm, key_ref), (value_hbm, value_ref))
        )
    ]
    for copy in copies:
        copy.start()
    copies[0].wait()
    for j in range(width // tokens):
        cols = pl.ds(j * tokens, tokens)
        dest = pl.ds(j * group, group)
        out_ref[dest, channels:, :] = filters_ref[:, cols].T.reshape(group, channels, tokens)
    copies[1].wait()
    copies[2].wait()
    for j in range(width // tokens):
        cols = pl.ds(j * tokens, tokens)
        dest = pl.ds(j * group, group)
        product = key_ref[:, cols].astype(f32) * value_ref[:, cols].astype(f32)
        out_ref[dest, :channels, :] = product.astype(bf16).T.reshape(group, channels, tokens)


def turn_kernel(residual_ref, query_ref, cotangent_ref, gain_ref, res_ref, q_ref, sg_ref):
    tokens, width = residual_ref.shape
    for j in range(width // tokens):
        cols = pl.ds(j * tokens, tokens)
        res_ref[cols, :] = residual_ref[:, cols].T
        q_ref[cols, :] = query_ref[:, cols].T
        sg_ref[cols, :] = (cotangent_ref[:, cols].astype(f32) * gain_ref[:, cols]).T


def sums_kernel(mixed_ref, res_ref, q_ref, sg_ref, out_ref):
    width, tokens = res_ref.shape
    summed = res_ref[...].astype(f32) + q_ref[...].astype(f32) * mixed_ref[...].astype(f32)
    out_ref[0:1, :] = jnp.sum(summed * summed, axis=0, keepdims=True)
    out_ref[1:2, :] = jnp.sum(sg_ref[...] * summed, axis=0, keepdims=True)


def norm_terms(sums_refs, total):
    near, far = sums_refs
    sums = (near[...] + far[...]) * (1.0 / total)
    inv_rms = lax.rsqrt(sums[0:1, :] + epsilon)
    alpha = inv_rms * inv_rms * inv_rms * sums[1:2, :]
    return inv_rms, alpha


def grad_kernel(total, near_ref, far_ref, mixed_ref, res_ref, q_ref, sg_ref, out_ref):
    inv_rms, alpha = norm_terms((near_ref, far_ref), total)
    query = q_ref[...].astype(f32)
    summed = res_ref[...].astype(f32) + query * mixed_ref[...].astype(f32)
    grad_summed = inv_rms * sg_ref[...] - summed * alpha
    out_ref[...] = (grad_summed * query).astype(bf16)


def norm_kernel(
    total, near_ref, far_ref, mixed_ref, res_ref, q_ref, sg_ref, gain_ref, cotangent_ref, key_ref, value_ref,
    normed_ref, gres_ref, gq_ref, ends_ref,
):
    width, tokens = res_ref.shape
    inv_rms, alpha = norm_terms((near_ref, far_ref), total)
    for j in range(width // tokens):
        cols = pl.ds(j * tokens, tokens)
        mixed = mixed_ref[cols, :].astype(f32)
        query = q_ref[cols, :].astype(f32)
        summed = res_ref[cols, :].astype(f32) + query * mixed
        grad_summed = inv_rms * sg_ref[cols, :] - summed * alpha
        unit = (summed * inv_rms).T
        normed_ref[:, cols] = (unit * gain_ref[:, cols]).astype(bf16)
        gres_ref[:, cols] = grad_summed.astype(bf16).T
        gq_ref[:, cols] = (grad_summed * mixed).astype(bf16).T
        grad_mixed = (grad_summed * query).astype(bf16).T.astype(f32)
        product = key_ref[:, cols].astype(f32) * value_ref[:, cols].astype(f32)
        product = product.astype(bf16).astype(f32)
        ends_ref[0:1, cols] = jnp.sum(grad_mixed * product, axis=0, keepdims=True)
        ends_ref[1:2, cols] = jnp.sum(
            cotangent_ref[:, cols].astype(f32) * unit, axis=0, keepdims=True
        )


def finish_kernel(recv_ref, key_ref, value_ref, gk_ref, gv_ref, gf_ref):
    tokens, width = key_ref.shape
    peers, rows, _ = recv_ref.shape
    channels = rows // 2
    group = tokens // channels
    for j in range(width // tokens):
        cols = pl.ds(j * tokens, tokens)
        dest = pl.ds(j * group, group)
        back = recv_ref[dest, :channels, :].reshape(tokens, tokens).T.astype(f32)
        gk_ref[:, cols] = (back * value_ref[:, cols].astype(f32)).astype(bf16)
        gv_ref[:, cols] = (back * key_ref[:, cols].astype(f32)).astype(bf16)
        gf_ref[:, cols] = recv_ref[dest, channels:, :].reshape(tokens, tokens).T.astype(f32)


def places(side, stride, count, step):
    pairs = []
    for source in range(count):
        place = source // stride % side
        pairs.append((source, source + ((place + step) % side - place) * stride))
    return pairs


def sum_over(values, axis, side, stride):
    count = lax.axis_size(axis)
    moved = [
        lax.ppermute(values, axis, places(side, stride, count, step)) for step in range(1, side)
    ]
    for part in moved:
        values = values + part
    return values


def call(kernel, out_shape, n_in, scratch=(), cost=None, smem=(), hbm=(), hbm_out=()):
    def place(i, scalar, far):
        space = pltpu.SMEM if i in scalar else pltpu.HBM if i in far else pltpu.VMEM
        return pl.BlockSpec(memory_space=space)

    outs = out_shape if isinstance(out_shape, tuple) else (out_shape,)
    out_specs = tuple(place(i, (), hbm_out) for i in range(len(outs)))
    return pl.pallas_call(
        kernel,
        out_shape=out_shape,
        in_specs=[place(i, smem, hbm) for i in range(n_in)],
        out_specs=out_specs if isinstance(out_shape, tuple) else out_specs[0],
        scratch_shapes=list(scratch),
        compiler_params=pltpu.CompilerParams(vmem_limit_bytes=48 * 1024 * 1024),
        cost_estimate=cost,
    )


def far_memory(values):
    return pltpu.with_memory_space_constraint(values, pltpu.HBM)


def shape(dims, dtype):
    return jax.ShapeDtypeStruct(dims, dtype)


def run_conv(received, skip_here):
    peers, rows, tokens = received.shape
    channels = rows // 2
    half = channels * peers
    spectra_shape = (2 * half, 2 * tokens)
    vm = pltpu.VMEM
    return call(
        conv_kernel,
        (shape((peers, channels, tokens), bf16), pltpu.HBM(spectra_shape, f32)),
        n_in=7,
        smem=(1,),
        hbm_out=(1,),
        scratch=(
            vm(spectra_shape, f32),
            vm((2 * half + 8 * peers, tokens), f32),
            vm((2 * half, 4 * tokens), bf16),
            vm((half, 2 * tokens), f32),
            vm((half + 8 * peers, tokens), f32),
            pltpu.SemaphoreType.DMA((rows // 4,)),
        ),
    )(received, skip_here, *tables(peers, tokens))


def run_lag(received, skip_here, spectra, *after):
    peers, channels, tokens = received.shape
    half = channels * peers
    spectra_shape = (2 * half, 2 * tokens)
    vm = pltpu.VMEM
    return call(
        lag_kernel,
        shape((peers, 2 * channels, tokens), bf16),
        n_in=8 + len(after),
        smem=(1,),
        hbm=(7, 8),
        scratch=(
            vm(spectra_shape, f32),
            vm((half + 8 * peers, tokens), f32),
            vm((half, 2 * tokens), f32),
            vm((2 * half, 4 * tokens), bf16),
            vm(spectra_shape, f32),
            vm((2 * half + 8 * peers, tokens), f32),
            pltpu.SemaphoreType.DMA((channels // 2,)),
        ),
    )(received, skip_here, *tables(peers, tokens), far_memory(spectra), *after)


sides = (4, 4, 4)


def on_device(
    residual, query_feats, key_feats, value_feats, filters, cotangent, skip_bias, norm_gain
):
    tokens, width = residual.shape
    peers = lax.axis_size("seq")
    total = float(width * lax.axis_size("chan"))
    channels = width // peers
    vm = pltpu.VMEM

    def exchange(values):
        return lax.all_to_all(values, "seq", split_axis=0, concat_axis=0, tiled=True)

    plain = (tokens, width)
    turned = (width, tokens)
    dma = pltpu.SemaphoreType.DMA
    aside = pl.CostEstimate(flops=10**6, bytes_accessed=4 * 10**6, transcendentals=0)
    sent = call(
        send_kernel,
        shape((peers, 2 * channels, tokens), bf16),
        n_in=3,
        hbm=(0, 1, 2),
        scratch=(vm(plain, bf16), vm(plain, bf16), vm(plain, bf16), dma((3,))),
    )(far_memory(key_feats), far_memory(value_feats), far_memory(filters))
    received = exchange(sent)
    gain_row = norm_gain[None, :]
    res_t, q_t, sg_t = call(
        turn_kernel,
        (shape(turned, bf16), shape(turned, bf16), shape(turned, f32)),
        n_in=4,
        cost=aside,
    )(residual, query_feats, cotangent, gain_row)
    skip_here = lax.dynamic_slice_in_dim(skip_bias, lax.axis_index("seq") * channels, channels)
    mixed_sent, spectra = run_conv(received, skip_here)
    mixed_t = exchange(mixed_sent).reshape(width, tokens)
    sums = call(sums_kernel, shape((2, tokens), f32), n_in=4)(mixed_t, res_t, q_t, sg_t)
    near = sum_over(sums, "chan", 2, 1)
    far = lax.ppermute(near, "chan", places(2, 2, 4, 1))
    grad_sent = call(
        functools.partial(grad_kernel, total), shape(turned, bf16), n_in=6
    )(near, far, mixed_t, res_t, q_t, sg_t)
    grad_received = exchange(grad_sent.reshape(peers, channels, tokens))
    normed, grad_residual, grad_query, ends = call(
        functools.partial(norm_kernel, total),
        (shape(plain, bf16), shape(plain, bf16), shape(plain, bf16), shape((2, width), f32)),
        n_in=10,
        cost=aside,
    )(near, far, mixed_t, res_t, q_t, sg_t, gain_row, cotangent, key_feats, value_feats)
    side_z, side_y, side_x = sides
    ends = sum_over(ends, "seq", side_x, 1)
    lag_sent = run_lag(grad_received, skip_here, spectra, ends)
    ends = sum_over(ends, "seq", side_y, side_x)
    ends = sum_over(ends, "seq", side_z, side_x * side_y)
    lag_received = exchange(lag_sent)
    grad_key, grad_value, grad_filter = call(
        finish_kernel,
        (shape(plain, bf16), shape(plain, bf16), shape(plain, f32)),
        n_in=3,
    )(lag_received, key_feats, value_feats)
    return (
        normed,
        grad_residual,
        grad_query,
        grad_key,
        grad_value,
        grad_filter,
        ends[0],
        ends[1],
    )


def solution(mesh):
    return jax.shard_map(
        on_device,
        mesh=mesh,
        in_specs=(P("seq", "chan"),) * 6 + (P("chan"),) * 2,
        out_specs=(P("seq", "chan"),) * 6 + (P("chan"),) * 2,
        check_vma=False,
    )
```

time: 126 us -> 112 us (0.89)
  blocking collectives: 32.4 us -> 0 us
  starting transfers between devices: 24.1 us -> 50.5 us
  local copies, waits for them, and re-layouts: 7.19 us -> 2.12 us
  waiting for transfers between devices: 46.3 us -> 43.4 us
    all_to_all x1 -> x0, blocking collectives: 21.2 us -> none  [exchange(): lax.all_to_all(values, 'seq', split_axis=0, concat_axis=0, tiled=True)]
    ppermute x0 -> x11, starting transfers between devices: none -> 18.3 us  [the longest x10 13.8 us: sum_over(): lax.ppermute(values, axis, places(side, stride, count, step))]
    all_to_all x3 -> x4, waiting for transfers between devices: 46.3 us -> 28.9 us  [exchange(): lax.all_to_all(values, 'seq', split_axis=0, concat_axis=0, tiled=True)]
    ppermute x0 -> x11, waiting for transfers between devices: none -> 14.4 us  [the longest x10 11.5 us: sum_over(): lax.ppermute(values, axis, places(side, stride, count, step))]
    psum x1 -> x0, blocking collectives: 11.2 us -> none  [on_device(): sums = lax.psum(sums, 'chan')]
    all_to_all x3 -> x4, starting transfers between devices: 24.1 us -> 32.2 us  [exchange(): lax.all_to_all(values, 'seq', split_axis=0, concat_axis=0, tiled=True)]
    unnamed x36 -> x28, local copies, waits for them, and re-layouts: 5.82 us -> 0.75 us
  transfers between devices with their start and end apart: 3 -> 15, of which waited for: 3 -> 12; matrix products, arithmetic and copies ran while one was open for 1% -> 1% of each run, Pallas kernels for 1% -> 2%
where the time goes in v2:
time: 112 us
  starting transfers between devices  50.5 us (45%)
  waiting for transfers between devices  43.4 us (39%)
  Pallas kernels  15 us (13%)
  local copies, waits for them, and re-layouts  2.12 us (2%)
    all_to_all x4, starting transfers between devices, exchange(): lax.all_to_all(values, 'seq', split_axis=0, concat_axis=0, tiled=True)  32.2 us
    all_to_all x4, waiting for transfers between devices, exchange(): lax.all_to_all(values, 'seq', split_axis=0, concat_axis=0, tiled=True)  28.9 us
    ppermute x10, starting transfers between devices, sum_over(): lax.ppermute(values, axis, places(side, stride, count, step))  13.8 us
    ppermute x10, waiting for transfers between devices, sum_over(): lax.ppermute(values, axis, places(side, stride, count, step))  11.5 us
    pallas_call x1, Pallas kernels, run_lag(): call(lag_kernel, shape((peers, 2 * channels, tokens), bf16), n_in=8 + len...  4.96 us
    ppermute x1, starting transfers between devices, on_device(): far = lax.ppermute(near, 'chan', places(2, 2, 4, 1))  4.49 us
    pallas_call x1, Pallas kernels, run_conv(): call(conv_kernel, (shape((peers, channels, tokens), bf16), pltpu.HBM(spec...  3.76 us
    ppermute x1, waiting for transfers between devices, on_device(): far = lax.ppermute(near, 'chan', places(2, 2, 4, 1))  2.98 us
  transfers between devices with their start and end apart: 15, of which 12 were waited for; matrix products, arithmetic and copies ran while one was open for 1% of the time, Pallas kernels for 2%

profile of v2, /device:TPU:2, one launch (start us, length us, event | category | flops | bytes accessed | tf_op | source)
XLA Modules:
  0.0 111.8 jit_solution(15877499680707854574)
XLA Ops:
  0.7 2.2 %shard_map.188 = bf16[64,32,128]{2,1,0:T(8,128)(2,1)} custom-call(bf16[128,1024]{1,0:T(8,128)(2,1)} %key_ref.3, bf16[128,1024]{1,0:T(8,128)(2,1)} %value_ref.3, bf16[128,1024]{1,0:T(8,128)(2,1)} %filters_hbm.1), custom_call_target="tpu_custom_call" | custom-call | tf_op jit(solution)/shard_map/pallas_call | solution.py:408
  2.9 12.1 %all-to-all-start = ((bf16[64,32,128]{2,1,0:T(8,128)(2,1)}), bf16[64,32,128]{2,1,0:T(8,128)(2,1)S(1)}, u32[]{:S(2)}, u32[]{:S(2)}) async-start(bf16[64,32,128]{2,1,0:T(8,128)(2,1)} %shard_map.188), calls=%async_computation | async-start | bytes 1048576 | tf_op jit(solution)/shard_map/all_to_all | solution.py:402
  15.8 16.3 %all-to-all-done.recv_ref = bf16[64,32,128]{2,1,0:T(8,128)(2,1)S(1)} async-done(((bf16[64,32,128]{2,1,0:T(8,128)(2,1)}), bf16[64,32,128]{2,1,0:T(8,128)(2,1)S(1)}, u32[]{:S(2)}, u32[]{:S(2)}) %all-to-all-start) | async-done | bytes 524320 | tf_op jit(solution)/shard_map/all_to_all | solution.py:402
  32.1 3.8 %shard_map.189 = (bf16[64,16,128]{2,1,0:T(8,128)(2,1)}, f32[2048,256]{1,0:T(8,128)}) custom-call(bf16[64,32,128]{2,1,0:T(8,128)(2,1)S(1)} %all-to-all-done.recv_ref, f32[16]{0:T(128)S(1)} %dynamic_slice.3.skip_ref, bf16[128,128]{1,0:T(8,128)(2,1)S(1)} %copy-done.9, bf16[64,384]{1,0:T(8,128)(2,1)S(1)} %copy-done.8, f32[128,128]{1,0:T(8,128)S(1)} %copy-done.5, ...), custom_call_target="tpu_custom_call" | custom-call | tf_op jit(solution)/shard_map/pallas_call | solution.py:349
  35.8 5.9 %all-to-all-start.1 = ((bf16[64,16,128]{2,1,0:T(8,128)(2,1)}), bf16[64,16,128]{2,1,0:T(8,128)(2,1)S(1)}, u32[]{:S(2)}, u32[]{:S(2)}) async-start(bf16[64,16,128]{2,1,0:T(8,128)(2,1)} %get-tuple-element.20), calls=%async_computation.1 | async-start | bytes 524288 | tf_op jit(solution)/shard_map/all_to_all | solution.py:402
  42.8 9.8 %all-to-all-done.1 = bf16[64,16,128]{2,1,0:T(8,128)(2,1)S(1)} async-done(((bf16[64,16,128]{2,1,0:T(8,128)(2,1)}), bf16[64,16,128]{2,1,0:T(8,128)(2,1)S(1)}, u32[]{:S(2)}, u32[]{:S(2)}) %all-to-all-start.1) | async-done | bytes 262176 | tf_op jit(solution)/shard_map/all_to_all | solution.py:402
  53.0 1.1 %collective-permute-done = f32[2,128]{1,0:T(2,128)S(1)} collective-permute-done((f32[2,128]{1,0:T(2,128)S(1)}, f32[2,128]{1,0:T(2,128)S(1)}, u32[]{:S(2)}, u32[]{:S(2)}) %collective-permute-start) | collective-permute-done | bytes 1056 | tf_op jit(solution)/shard_map/ppermute | solution.py:310
  54.1 4.5 %collective-permute-start.1 = (f32[2,128]{1,0:T(2,128)S(1)}, f32[2,128]{1,0:T(2,128)S(1)}, u32[]{:S(2)}, u32[]{:S(2)}) collective-permute-start(f32[2,128]{1,0:T(2,128)S(1)} %add.34.near_ref), channel_id=1, source_target_pairs={{0,2},{1,3},{2,0},{3,1},{4,6},{5,7},{6,4},{7,5},{8,10},{9,11},{10,... | collective-permute-start | bytes 3080 | tf_op jit(solution)/shard_map/ppermute | solution.py:428
  58.6 3.0 %collective-permute-done.1.far_ref = f32[2,128]{1,0:T(2,128)S(1)} collective-permute-done((f32[2,128]{1,0:T(2,128)S(1)}, f32[2,128]{1,0:T(2,128)S(1)}, u32[]{:S(2)}, u32[]{:S(2)}) %collective-permute-start.1) | collective-permute-done | bytes 1056 | tf_op jit(solution)/shard_map/ppermute | solution.py:428
  62.5 5.9 %all-to-all-start.2 = ((bf16[64,16,128]{2,1,0:T(8,128)(2,1)}), bf16[64,16,128]{2,1,0:T(8,128)(2,1)S(1)}, u32[]{:S(2)}, u32[]{:S(2)}) async-start(bf16[64,16,128]{2,1,0:T(8,128)(2,1)} %bitcast.2), calls=%async_computation.2 | async-start | bytes 524288 | tf_op jit(solution)/shard_map/all_to_all | solution.py:402
  68.5 1.4 %shard_map.192 = (bf16[128,1024]{1,0:T(8,128)(2,1)}, bf16[128,1024]{1,0:T(8,128)(2,1)}, bf16[128,1024]{1,0:T(8,128)(2,1)}, f32[2,1024]{1,0:T(2,128)S(1)}) custom-call(f32[2,128]{1,0:T(2,128)S(1)} %add.34.near_ref, f32[2,128]{1,0:T(2,128)S(1)} %collective-permute-done.1.far_ref, bf16[1024,128]{1,0:T(8,128)(2,1)S(1)} %bitcast.7, ...), custom_call_target="tpu_custom_call" | custom-call | flops 1000000 | bytes 4000000 | tf_op jit(solution)/shard_map/pallas_call | solution.py:433
  70.3 2.5 %collective-permute-start.3 = (f32[2,1024]{1,0:T(2,128)S(1)}, f32[2,1024]{1,0:T(2,128)S(1)}, u32[]{:S(2)}, u32[]{:S(2)}) collective-permute-start(f32[2,1024]{1,0:T(2,128)S(1)} %get-tuple-element.28), channel_id=1, source_target_pairs={{0,8},{4,12},{8,0},{12,4},{16,24},{20,28},{24,16},{28,20},{32,40},... | collective-permute-start | bytes 24584 | tf_op jit(solution)/shard_map/ppermute | solution.py:310
  72.8 1.8 %collective-permute-start.2 = (f32[2,1024]{1,0:T(2,128)S(1)}, f32[2,1024]{1,0:T(2,128)S(1)}, u32[]{:S(2)}, u32[]{:S(2)}) collective-permute-start(f32[2,1024]{1,0:T(2,128)S(1)} %get-tuple-element.28), channel_id=1, source_target_pairs={{0,4},{4,8},{8,12},{12,0},{16,20},{20,24},{24,28},{28,16},{32,36},... | collective-permute-start | bytes 24584 | tf_op jit(solution)/shard_map/ppermute | solution.py:310
  74.6 1.0 collective-permute-done.3
  76.5 2.8 %all-to-all-done.2.recv_ref = bf16[64,16,128]{2,1,0:T(8,128)(2,1)S(1)} async-done(((bf16[64,16,128]{2,1,0:T(8,128)(2,1)}), bf16[64,16,128]{2,1,0:T(8,128)(2,1)S(1)}, u32[]{:S(2)}, u32[]{:S(2)}) %all-to-all-start.2) | async-done | bytes 262176 | tf_op jit(solution)/shard_map/all_to_all | solution.py:402
  79.3 5.0 %shard_map.194 = bf16[64,32,128]{2,1,0:T(8,128)(2,1)} custom-call(bf16[64,16,128]{2,1,0:T(8,128)(2,1)S(1)} %all-to-all-done.2.recv_ref, f32[16]{0:T(128)S(1)} %copy-done.13, bf16[128,128]{1,0:T(8,128)(2,1)S(1)} %copy-done.9, bf16[64,384]{1,0:T(8,128)(2,1)S(1)} %copy-done.8, f32[128,128]{1,0:T(8,128)S(1)} %copy-done.5, bf16[768,256]{1,0:T(8,128)(2,1)S(1)} %copy-done.3, ...), custom_call_target="tpu_custom_call" | custom-call | tf_op jit(solution)/shard_map/pallas_call | solution.py:371
  84.3 8.2 %all-to-all-start.3 = ((bf16[64,32,128]{2,1,0:T(8,128)(2,1)}), bf16[64,32,128]{2,1,0:T(8,128)(2,1)S(1)}, u32[]{:S(2)}, u32[]{:S(2)}) async-start(bf16[64,32,128]{2,1,0:T(8,128)(2,1)} %shard_map.194), calls=%async_computation.3 | async-start | bytes 1048576 | tf_op jit(solution)/shard_map/all_to_all | solution.py:402
  92.5 2.8 %collective-permute-start.7 = (f32[2,1024]{1,0:T(2,128)S(1)}, f32[2,1024]{1,0:T(2,128)S(1)}, u32[]{:S(2)}, u32[]{:S(2)}) collective-permute-start(f32[2,1024]{1,0:T(2,128)S(1)} %add_add_fusion.2.rest_0_), channel_id=1, source_target_pairs={{0,48},{4,52},{8,56},{12,60},{16,0},{20,4},{24,8},{28,12},{32,16},... | collective-permute-start | bytes 24584 | tf_op jit(solution)/shard_map/ppermute | solution.py:310
  97.6 3.4 %collective-permute-done.6 = f32[2,1024]{1,0:T(2,128)S(1)} collective-permute-done((f32[2,1024]{1,0:T(2,128)S(1)}, f32[2,1024]{1,0:T(2,128)S(1)}, u32[]{:S(2)}, u32[]{:S(2)}) %collective-permute-start.6) | collective-permute-done | bytes 8224 | tf_op jit(solution)/shard_map/ppermute | solution.py:310
  101.0 3.5 %collective-permute-start.10 = (f32[2,1024]{1,0:T(2,128)S(1)}, f32[2,1024]{1,0:T(2,128)S(1)}, u32[]{:S(2)}, u32[]{:S(2)}) collective-permute-start(f32[2,1024]{1,0:T(2,128)S(1)} %add_add_fusion.1), channel_id=1, source_target_pairs={{0,192},{4,196},{8,200},{12,204},{16,208},{20,212},{24,216},{28,22... | collective-permute-start | bytes 24584 | tf_op jit(solution)/shard_map/ppermute | solution.py:310
  104.6 1.0 collective-permute-start.8
  106.0 3.2 %collective-permute-done.9 = f32[2,1024]{1,0:T(2,128)S(1)} collective-permute-done((f32[2,1024]{1,0:T(2,128)S(1)}, f32[2,1024]{1,0:T(2,128)S(1)}, u32[]{:S(2)}, u32[]{:S(2)}) %collective-permute-start.9) | collective-permute-done | bytes 8224 | tf_op jit(solution)/shard_map/ppermute | solution.py:310
  109.1 0.9 collective-permute-done.8
  110.7 1.2 %shard_map.195 = (bf16[128,1024]{1,0:T(8,128)(2,1)}, bf16[128,1024]{1,0:T(8,128)(2,1)}, f32[128,1024]{1,0:T(8,128)}) custom-call(bf16[64,32,128]{2,1,0:T(8,128)(2,1)S(1)} %all-to-all-done.3.recv_ref, bf16[128,1024]{1,0:T(8,128)(2,1)S(1)} %copy-done, bf16[128,1024]{1,0:T(8,128)(2,1)S(1)} %copy-done.1), custom_call_target="tpu_custom_call" | custom-call | tf_op jit(solution)/shard_map/pallas_call | solution.py:445
  (48 shorter events, 7.7 us)
Async XLA Ops:
  0.6 31.4 %copy-start.2 = (bf16[768,256]{1,0:T(8,128)(2,1)S(1)}, bf16[768,256]{1,0:T(8,128)(2,1)}, u32[]{:S(2)}) copy-start(bf16[768,256]{1,0:T(8,128)(2,1)} %constant.26.clone.inverse_ref) | copy-start | bytes 1179652
  0.6 31.4 %copy-start.3 = (bf16[768,256]{1,0:T(8,128)(2,1)S(1)}, bf16[768,256]{1,0:T(8,128)(2,1)}, u32[]{:S(2)}) copy-start(bf16[768,256]{1,0:T(8,128)(2,1)} %constant.25.clone.inner_ref) | copy-start | bytes 1179652
  0.7 31.4 %copy-start.5 = (f32[128,128]{1,0:T(8,128)S(1)}, f32[128,128]{1,0:T(8,128)}, u32[]{:S(2)}) copy-start(f32[128,128]{1,0:T(8,128)} %constant.24.clone.twiddle_ref) | copy-start | bytes 196612
  0.7 31.4 %copy-start.8 = (bf16[64,384]{1,0:T(8,128)(2,1)S(1)}, bf16[64,384]{1,0:T(8,128)(2,1)}, u32[]{:S(2)}) copy-start(bf16[64,384]{1,0:T(8,128)(2,1)} %constant.23.clone.last_ref) | copy-start | bytes 147460
  0.7 31.4 %copy-start.9 = (bf16[128,128]{1,0:T(8,128)(2,1)S(1)}, bf16[128,128]{1,0:T(8,128)(2,1)}, u32[]{:S(2)}) copy-start(bf16[128,128]{1,0:T(8,128)(2,1)} %constant.22.clone.first_ref) | copy-start | bytes 98308
  0.7 41.0 %copy-start.4 = (bf16[128,1024]{1,0:T(8,128)(2,1)S(1)}, bf16[128,1024]{1,0:T(8,128)(2,1)}, u32[]{:S(2)}) copy-start(bf16[128,1024]{1,0:T(8,128)(2,1)} %cotangent_ref.3) | copy-start | bytes 786436
  0.7 41.0 %copy-start.7 = (bf16[128,1024]{1,0:T(8,128)(2,1)S(1)}, bf16[128,1024]{1,0:T(8,128)(2,1)}, u32[]{:S(2)}) copy-start(bf16[128,1024]{1,0:T(8,128)(2,1)} %query_ref.1) | copy-start | bytes 786436
  0.7 41.0 %copy-start.6 = (bf16[128,1024]{1,0:T(8,128)(2,1)S(1)}, bf16[128,1024]{1,0:T(8,128)(2,1)}, u32[]{:S(2)}) copy-start(bf16[128,1024]{1,0:T(8,128)(2,1)} %residual_ref.1) | copy-start | bytes 786436
  2.9 29.1 %all-to-all-start = ((bf16[64,32,128]{2,1,0:T(8,128)(2,1)}), bf16[64,32,128]{2,1,0:T(8,128)(2,1)S(1)}, u32[]{:S(2)}, u32[]{:S(2)}) async-start(bf16[64,32,128]{2,1,0:T(8,128)(2,1)} %shard_map.188), calls=%async_computation | async-start | bytes 1048576 | tf_op jit(solution)/shard_map/all_to_all | solution.py:402
  35.8 16.8 %all-to-all-start.1 = ((bf16[64,16,128]{2,1,0:T(8,128)(2,1)}), bf16[64,16,128]{2,1,0:T(8,128)(2,1)S(1)}, u32[]{:S(2)}, u32[]{:S(2)}) async-start(bf16[64,16,128]{2,1,0:T(8,128)(2,1)} %get-tuple-element.20), calls=%async_computation.1 | async-start | bytes 524288 | tf_op jit(solution)/shard_map/all_to_all | solution.py:402
  42.5 26.0 %copy-start.1 = (bf16[128,1024]{1,0:T(8,128)(2,1)S(1)}, bf16[128,1024]{1,0:T(8,128)(2,1)}, u32[]{:S(2)}) copy-start(bf16[128,1024]{1,0:T(8,128)(2,1)} %value_ref.3) | copy-start | bytes 786436
  52.9 1.2 %collective-permute-start = (f32[2,128]{1,0:T(2,128)S(1)}, f32[2,128]{1,0:T(2,128)S(1)}, u32[]{:S(2)}, u32[]{:S(2)}) collective-permute-start(f32[2,128]{1,0:T(2,128)S(1)} %shard_map.191), channel_id=1, source_target_pairs={{0,1},{1,0},{2,3},{3,2},{4,5},{5,4},{6,7},{7,6},{8,9},{9,8},{10,11... | collective-permute-start | bytes 3080 | tf_op jit(solution)/shard_map/ppermute | solution.py:310
  54.1 7.5 %collective-permute-start.1 = (f32[2,128]{1,0:T(2,128)S(1)}, f32[2,128]{1,0:T(2,128)S(1)}, u32[]{:S(2)}, u32[]{:S(2)}) collective-permute-start(f32[2,128]{1,0:T(2,128)S(1)} %add.34.near_ref), channel_id=1, source_target_pairs={{0,2},{1,3},{2,0},{3,1},{4,6},{5,7},{6,4},{7,5},{8,10},{9,11},{10,... | collective-permute-start | bytes 3080 | tf_op jit(solution)/shard_map/ppermute | solution.py:428
  62.5 16.8 %all-to-all-start.2 = ((bf16[64,16,128]{2,1,0:T(8,128)(2,1)}), bf16[64,16,128]{2,1,0:T(8,128)(2,1)S(1)}, u32[]{:S(2)}, u32[]{:S(2)}) async-start(bf16[64,16,128]{2,1,0:T(8,128)(2,1)} %bitcast.2), calls=%async_computation.2 | async-start | bytes 524288 | tf_op jit(solution)/shard_map/all_to_all | solution.py:402
  69.9 4.7 %collective-permute-start.4 = (f32[2,1024]{1,0:T(2,128)S(1)}, f32[2,1024]{1,0:T(2,128)S(1)}, u32[]{:S(2)}, u32[]{:S(2)}) collective-permute-start(f32[2,1024]{1,0:T(2,128)S(1)} %get-tuple-element.28), channel_id=1, source_target_pairs={{0,12},{4,0},{8,4},{12,8},{16,28},{20,16},{24,20},{28,24},{32,44},... | collective-permute-start | bytes 24584 | tf_op jit(solution)/shard_map/ppermute | solution.py:310
  70.3 5.3 %collective-permute-start.3 = (f32[2,1024]{1,0:T(2,128)S(1)}, f32[2,1024]{1,0:T(2,128)S(1)}, u32[]{:S(2)}, u32[]{:S(2)}) collective-permute-start(f32[2,1024]{1,0:T(2,128)S(1)} %get-tuple-element.28), channel_id=1, source_target_pairs={{0,8},{4,12},{8,0},{12,4},{16,24},{20,28},{24,16},{28,20},{32,40},... | collective-permute-start | bytes 24584 | tf_op jit(solution)/shard_map/ppermute | solution.py:310
  72.8 3.7 %collective-permute-start.2 = (f32[2,1024]{1,0:T(2,128)S(1)}, f32[2,1024]{1,0:T(2,128)S(1)}, u32[]{:S(2)}, u32[]{:S(2)}) collective-permute-start(f32[2,1024]{1,0:T(2,128)S(1)} %get-tuple-element.28), channel_id=1, source_target_pairs={{0,4},{4,8},{8,12},{12,0},{16,20},{20,24},{24,28},{28,16},{32,36},... | collective-permute-start | bytes 24584 | tf_op jit(solution)/shard_map/ppermute | solution.py:310
  84.3 26.4 %all-to-all-start.3 = ((bf16[64,32,128]{2,1,0:T(8,128)(2,1)}), bf16[64,32,128]{2,1,0:T(8,128)(2,1)S(1)}, u32[]{:S(2)}, u32[]{:S(2)}) async-start(bf16[64,32,128]{2,1,0:T(8,128)(2,1)} %shard_map.194), calls=%async_computation.3 | async-start | bytes 1048576 | tf_op jit(solution)/shard_map/all_to_all | solution.py:402
  92.5 5.0 %collective-permute-start.7 = (f32[2,1024]{1,0:T(2,128)S(1)}, f32[2,1024]{1,0:T(2,128)S(1)}, u32[]{:S(2)}, u32[]{:S(2)}) collective-permute-start(f32[2,1024]{1,0:T(2,128)S(1)} %add_add_fusion.2.rest_0_), channel_id=1, source_target_pairs={{0,48},{4,52},{8,56},{12,60},{16,0},{20,4},{24,8},{28,12},{32,16},... | collective-permute-start | bytes 24584 | tf_op jit(solution)/shard_map/ppermute | solution.py:310
  95.3 5.7 %collective-permute-start.6 = (f32[2,1024]{1,0:T(2,128)S(1)}, f32[2,1024]{1,0:T(2,128)S(1)}, u32[]{:S(2)}, u32[]{:S(2)}) collective-permute-start(f32[2,1024]{1,0:T(2,128)S(1)} %add_add_fusion.2.rest_0_), channel_id=1, source_target_pairs={{0,32},{4,36},{8,40},{12,44},{16,48},{20,52},{24,56},{28,60},{32,0... | collective-permute-start | bytes 24584 | tf_op jit(solution)/shard_map/ppermute | solution.py:310
  96.1 4.9 %collective-permute-start.5 = (f32[2,1024]{1,0:T(2,128)S(1)}, f32[2,1024]{1,0:T(2,128)S(1)}, u32[]{:S(2)}, u32[]{:S(2)}) collective-permute-start(f32[2,1024]{1,0:T(2,128)S(1)} %add_add_fusion.2.rest_0_), channel_id=1, source_target_pairs={{0,16},{4,20},{8,24},{12,28},{16,32},{20,36},{24,40},{28,44},{32,4... | collective-permute-start | bytes 24584 | tf_op jit(solution)/shard_map/ppermute | solution.py:310
  101.0 4.9 %collective-permute-start.10 = (f32[2,1024]{1,0:T(2,128)S(1)}, f32[2,1024]{1,0:T(2,128)S(1)}, u32[]{:S(2)}, u32[]{:S(2)}) collective-permute-start(f32[2,1024]{1,0:T(2,128)S(1)} %add_add_fusion.1), channel_id=1, source_target_pairs={{0,192},{4,196},{8,200},{12,204},{16,208},{20,212},{24,216},{28,22... | collective-permute-start | bytes 24584 | tf_op jit(solution)/shard_map/ppermute | solution.py:310
  104.6 4.5 %collective-permute-start.9 = (f32[2,1024]{1,0:T(2,128)S(1)}, f32[2,1024]{1,0:T(2,128)S(1)}, u32[]{:S(2)}, u32[]{:S(2)}) collective-permute-start(f32[2,1024]{1,0:T(2,128)S(1)} %add_add_fusion.1), channel_id=1, source_target_pairs={{0,128},{4,132},{8,136},{12,140},{16,144},{20,148},{24,152},{28,15... | collective-permute-start | bytes 24584 | tf_op jit(solution)/shard_map/ppermute | solution.py:310
  104.6 5.4 %collective-permute-start.8 = (f32[2,1024]{1,0:T(2,128)S(1)}, f32[2,1024]{1,0:T(2,128)S(1)}, u32[]{:S(2)}, u32[]{:S(2)}) collective-permute-start(f32[2,1024]{1,0:T(2,128)S(1)} %add_add_fusion.1), channel_id=1, source_target_pairs={{0,64},{4,68},{8,72},{12,76},{16,80},{20,84},{24,88},{28,92},{32,9... | collective-permute-start | bytes 24584 | tf_op jit(solution)/shard_map/ppermute | solution.py:310
  (5 other events, 97.5 us)

commit v3 on v2

--- a/solution.py
+++ b/solution.py
@@ -92,7 +92,7 @@
             copies[i].start()
 
 
-def inverse(rows, last_ref, twiddle_ref, inverse_ref, u_ref, z_ref, out_ref, stride):
+def inverse(rows, last_ref, twiddle_ref, inverse_ref, u_ref, z_ref, out_ref, stride, base=0):
     blocks = last_ref.shape[0]
     lanes = twiddle_ref.shape[1]
     cosine = twiddle_ref[:blocks]
@@ -100,22 +100,22 @@
     n = 2 * lanes
     chunk = 4 * blocks
     for i in range(rows // 4):
-        c = pl.ds(i * chunk, chunk)
+        c = pl.ds(base * blocks + i * chunk, chunk)
         z_ref[c] = matmul(u_ref[c, : 2 * n], inverse_ref[: 2 * n]) + matmul(
             u_ref[c, :n], inverse_ref[2 * n :]
         )
     for pair in range(rows // 2):
         columns = []
         for row in (2 * pair, 2 * pair + 1):
-            re = z_ref[pl.ds(row * blocks, blocks), :lanes]
-            im = z_ref[pl.ds(row * blocks, blocks), lanes:]
+            re = z_ref[pl.ds((base + row) * blocks, blocks), :lanes]
+            im = z_ref[pl.ds((base + row) * blocks, blocks), lanes:]
             zh, zl = split(
                 jnp.concatenate((re * cosine - im * sine, im * cosine + re * sine), 0)
             )
             columns.append(jnp.concatenate((zh, zh, zl), 0))
         out = matmul(last_ref[...], jnp.concatenate(columns, 1))
         for i in range(2):
-            out_ref[pl.ds(2 * pair + i, blocks, stride=stride), :] = out[
+            out_ref[pl.ds(base + 2 * pair + i, blocks, stride=stride), :] = out[
                 :, i * lanes : (i + 1) * lanes
             ]
 
@@ -164,65 +164,90 @@
 def lag_kernel(
     recv_ref, skip_ref, first_ref, last_ref, twiddle_ref, inner_ref, inverse_ref, kept_ref, *rest
 ):
-    out_ref, spec_ref, x_ref, g_ref, u_ref, z_ref, y_ref, sems = rest[-8:]
+    out_ref, spec_ref, x_ref, g_ref, u_ref, z_ref, y_ref, ready_ref, sems, out_sems = rest[-10:]
     blocks, channels, lanes = recv_ref.shape
     rows = 2 * channels
     half = channels * blocks
     copies = copies_of(kept_ref, spec_ref, sems)
     ahead = len(copies) // 2
     for i in range(ahead):
+        copies[ahead + i].start()
+    for i in range(ahead):
         copies[i].start()
-        copies[ahead + i].start()
     wide = channels + 8
     for a in range(blocks):
         x_ref[pl.ds(a * wide, channels), :] = recv_ref[a].astype(f32)
     forward(x_ref, wide, channels, first_ref, twiddle_ref, inner_ref, u_ref, g_ref)
-    for c in range(channels):
-        if c % (channels // ahead) == 0:
-            copies[c * ahead // channels].wait()
-            copies[ahead + c * ahead // channels].wait()
-        prod = pl.ds(c * blocks, blocks)
-        filt = pl.ds(half + c * blocks, blocks)
-        gre, gim = g_ref[prod, :lanes], g_ref[prod, lanes:]
-        for source, target in ((filt, prod), (prod, filt)):
-            sre, sim = spec_ref[source, :lanes], spec_ref[source, lanes:]
-            if source is filt:
+    wide = rows + 8
+    leaving = []
+    for source, target, lead in ((half, 0, ahead), (0, half, 0)):
+        for c in range(channels):
+            if c % (channels // ahead) == 0:
+                copies[lead + c * ahead // channels].wait()
+            grad = pl.ds(c * blocks, blocks)
+            gre, gim = g_ref[grad, :lanes], g_ref[grad, lanes:]
+            here = pl.ds(source + c * blocks, blocks)
+            sre, sim = spec_ref[here, :lanes], spec_ref[here, lanes:]
+            if source:
                 sre = sre + skip_ref[c]
-            put(u_ref, target, 0, sre * gre + sim * gim)
-            put(u_ref, target, lanes, sre * gim - sim * gre)
-    wide = rows + 8
-    inverse(rows, last_ref, twiddle_ref, inverse_ref, u_ref, z_ref, y_ref, wide)
-    for a in range(blocks):
-        out_ref[a] = y_ref[pl.ds(a * wide, rows), :].astype(bf16)
+            put(u_ref, pl.ds(target + c * blocks, blocks), 0, sre * gre + sim * gim)
+            put(u_ref, pl.ds(target + c * blocks, blocks), lanes, sre * gim - sim * gre)
+        inverse(
+            channels, last_ref, twiddle_ref, inverse_ref, u_ref, z_ref, y_ref, wide, target // blocks
+        )
+        first = target // blocks
+        for a in range(blocks):
+            ready_ref[first // channels, a] = y_ref[pl.ds(a * wide + first, channels), :].astype(bf16)
+        leaving.append(
+            pltpu.make_async_copy(
+                ready_ref.at[first // channels],
+                out_ref.at[:, pl.ds(first, channels), :],
+                out_sems.at[first // channels],
+            )
+        )
+        leaving[-1].start()
+    for copy in leaving:
+        copy.wait()
 
 
 def send_kernel(
-    key_hbm, value_hbm, filters_hbm, out_ref, key_ref, value_ref, filters_ref, sems
+    key_hbm, value_hbm, filters_hbm, out_hbm, key_ref, value_ref, filters_ref, out_ref, sems, out_sems
 ):
     tokens, width = key_ref.shape
     peers, rows, _ = out_ref.shape
     channels = rows // 2
     group = tokens // channels
-    copies = [
-        pltpu.make_async_copy(source, target, sems.at[i])
-        for i, (source, target) in enumerate(
-            ((filters_hbm, filters_ref), (key_hbm, key_ref), (value_hbm, value_ref))
-        )
-    ]
-    for copy in copies:
-        copy.start()
-    copies[0].wait()
-    for j in range(width // tokens):
-        cols = pl.ds(j * tokens, tokens)
-        dest = pl.ds(j * group, group)
-        out_ref[dest, channels:, :] = filters_ref[:, cols].T.reshape(group, channels, tokens)
-    copies[1].wait()
-    copies[2].wait()
-    for j in range(width // tokens):
-        cols = pl.ds(j * tokens, tokens)
-        dest = pl.ds(j * group, group)
-        product = key_ref[:, cols].astype(f32) * value_ref[:, cols].astype(f32)
-        out_ref[dest, :channels, :] = product.astype(bf16).T.reshape(group, channels, tokens)
+    parts = out_sems.shape[0]
+    arriving = []
+    for part in range(parts):
+        cols = pl.ds(part * (width // parts), width // parts)
+        pairs = ((key_hbm, key_ref), (value_hbm, value_ref), (filters_hbm, filters_ref))
+        arriving.append(
+            [
+                pltpu.make_async_copy(source.at[:, cols], target.at[:, cols], sems.at[part, i])
+                for i, (source, target) in enumerate(pairs)
+            ]
+        )
+        for copy in arriving[-1]:
+            copy.start()
+    leaving = []
+    for part in range(parts):
+        for copy in arriving[part]:
+            copy.wait()
+        steps = width // tokens // parts
+        for j in range(part * steps, (part + 1) * steps):
+            cols = pl.ds(j * tokens, tokens)
+            dest = pl.ds(j * group, group)
+            product = key_ref[:, cols].astype(f32) * value_ref[:, cols].astype(f32)
+            out_ref[dest, :channels, :] = product.astype(bf16).T.reshape(group, channels, tokens)
+            out_ref[dest, channels:, :] = filters_ref[:, cols].T.reshape(group, channels, tokens)
+        dest = pl.ds(part * (peers // parts), peers // parts)
+        leaving.append(
+            pltpu.make_async_copy(out_ref.at[dest], out_hbm.at[dest], out_sems.at[part])
+        )
+        leaving[-1].start()
+    for copy in leaving:
+        copy.wait()
 
 
 def turn_kernel(residual_ref, query_ref, cotangent_ref, gain_ref, res_ref, q_ref, sg_ref):
@@ -249,12 +274,23 @@
     return inv_rms, alpha
 
 
-def grad_kernel(total, near_ref, far_ref, mixed_ref, res_ref, q_ref, sg_ref, out_ref):
+def grad_kernel(total, near_ref, far_ref, mixed_ref, res_ref, q_ref, sg_ref, out_hbm, out_ref, sems):
     inv_rms, alpha = norm_terms((near_ref, far_ref), total)
-    query = q_ref[...].astype(f32)
-    summed = res_ref[...].astype(f32) + query * mixed_ref[...].astype(f32)
-    grad_summed = inv_rms * sg_ref[...] - summed * alpha
-    out_ref[...] = (grad_summed * query).astype(bf16)
+    parts = sems.shape[0]
+    size = res_ref.shape[0] // parts
+    leaving = []
+    for part in range(parts):
+        here = pl.ds(part * size, size)
+        query = q_ref[here].astype(f32)
+        summed = res_ref[here].astype(f32) + query * mixed_ref[here].astype(f32)
+        grad_summed = inv_rms * sg_ref[here] - summed * alpha
+        out_ref[here] = (grad_summed * query).astype(bf16)
+        leaving.append(
+            pltpu.make_async_copy(out_ref.at[here], out_hbm.at[here], sems.at[part])
+        )
+        leaving[-1].start()
+    for copy in leaving:
+        copy.wait()
 
 
 def norm_kernel(
@@ -282,18 +318,33 @@
         )
 
 
-def finish_kernel(recv_ref, key_ref, value_ref, gk_ref, gv_ref, gf_ref):
+def finish_kernel(
+    recv_ref, key_ref, value_ref, gk_hbm, gv_hbm, gf_hbm, gk_ref, gv_ref, gf_ref, sems
+):
     tokens, width = key_ref.shape
     peers, rows, _ = recv_ref.shape
     channels = rows // 2
     group = tokens // channels
-    for j in range(width // tokens):
-        cols = pl.ds(j * tokens, tokens)
-        dest = pl.ds(j * group, group)
-        back = recv_ref[dest, :channels, :].reshape(tokens, tokens).T.astype(f32)
-        gk_ref[:, cols] = (back * value_ref[:, cols].astype(f32)).astype(bf16)
-        gv_ref[:, cols] = (back * key_ref[:, cols].astype(f32)).astype(bf16)
-        gf_ref[:, cols] = recv_ref[dest, channels:, :].reshape(tokens, tokens).T.astype(f32)
+    parts = sems.shape[0]
+    steps = width // tokens // parts
+    leaving = []
+    for part in range(parts):
+        for j in range(part * steps, (part + 1) * steps):
+            cols = pl.ds(j * tokens, tokens)
+            dest = pl.ds(j * group, group)
+            back = recv_ref[dest, :channels, :].reshape(tokens, tokens).T.astype(f32)
+            gk_ref[:, cols] = (back * value_ref[:, cols].astype(f32)).astype(bf16)
+            gv_ref[:, cols] = (back * key_ref[:, cols].astype(f32)).astype(bf16)
+            gf_ref[:, cols] = recv_ref[dest, channels:, :].reshape(tokens, tokens).T.astype(f32)
+        cols = pl.ds(part * (width // parts), width // parts)
+        pairs = ((gk_ref, gk_hbm), (gv_ref, gv_hbm), (gf_ref, gf_hbm))
+        for i, (source, target) in enumerate(pairs):
+            leaving.append(
+                pltpu.make_async_copy(source.at[:, cols], target.at[:, cols], sems.at[part, i])
+            )
+            leaving[-1].start()
+    for copy in leaving:
+        copy.wait()
 
 
 def places(side, stride, count, step):
@@ -304,11 +355,20 @@
     return pairs
 
 
-def sum_over(values, axis, side, stride):
+def add_kernel(*refs):
+    *sources, out_ref = refs
+    own, *others = (ref[...] for ref in sources)
+    out_ref[...] = sum(others, own)
+
+
+def sum_over(values, axis, side, stride, cost=None):
     count = lax.axis_size(axis)
     moved = [
         lax.ppermute(values, axis, places(side, stride, count, step)) for step in range(1, side)
     ]
+    if cost is not None:
+        out = shape(values.shape, values.dtype)
+        return call(add_kernel, out, n_in=side, cost=cost)(values, *moved)
     for part in moved:
         values = values + part
     return values
@@ -370,10 +430,11 @@
     vm = pltpu.VMEM
     return call(
         lag_kernel,
-        shape((peers, 2 * channels, tokens), bf16),
+        pltpu.HBM((peers, 2 * channels, tokens), bf16),
         n_in=8 + len(after),
         smem=(1,),
         hbm=(7, 8),
+        hbm_out=(0,),
         scratch=(
             vm(spectra_shape, f32),
             vm((half + 8 * peers, tokens), f32),
@@ -381,7 +442,9 @@
             vm((2 * half, 4 * tokens), bf16),
             vm(spectra_shape, f32),
             vm((2 * half + 8 * peers, tokens), f32),
+            vm((2, peers, channels, tokens), bf16),
             pltpu.SemaphoreType.DMA((channels // 2,)),
+            pltpu.SemaphoreType.DMA((2,)),
         ),
     )(received, skip_here, *tables(peers, tokens), far_memory(spectra), *after)
 
@@ -405,12 +468,21 @@
     turned = (width, tokens)
     dma = pltpu.SemaphoreType.DMA
     aside = pl.CostEstimate(flops=10**6, bytes_accessed=4 * 10**6, transcendentals=0)
+    parts = 4
     sent = call(
         send_kernel,
-        shape((peers, 2 * channels, tokens), bf16),
+        pltpu.HBM((peers, 2 * channels, tokens), bf16),
         n_in=3,
         hbm=(0, 1, 2),
-        scratch=(vm(plain, bf16), vm(plain, bf16), vm(plain, bf16), dma((3,))),
+        hbm_out=(0,),
+        scratch=(
+            vm(plain, bf16),
+            vm(plain, bf16),
+            vm(plain, bf16),
+            vm((peers, 2 * channels, tokens), bf16),
+            dma((parts, 3)),
+            dma((parts,)),
+        ),
     )(far_memory(key_feats), far_memory(value_feats), far_memory(filters))
     received = exchange(sent)
     gain_row = norm_gain[None, :]
@@ -427,7 +499,11 @@
     near = sum_over(sums, "chan", 2, 1)
     far = lax.ppermute(near, "chan", places(2, 2, 4, 1))
     grad_sent = call(
-        functools.partial(grad_kernel, total), shape(turned, bf16), n_in=6
+        functools.partial(grad_kernel, total),
+        pltpu.HBM(turned, bf16),
+        n_in=6,
+        hbm_out=(0,),
+        scratch=(vm(turned, bf16), dma((parts,))),
     )(near, far, mixed_t, res_t, q_t, sg_t)
     grad_received = exchange(grad_sent.reshape(peers, channels, tokens))
     normed, grad_residual, grad_query, ends = call(
@@ -439,13 +515,17 @@
     side_z, side_y, side_x = sides
     ends = sum_over(ends, "seq", side_x, 1)
     lag_sent = run_lag(grad_received, skip_here, spectra, ends)
-    ends = sum_over(ends, "seq", side_y, side_x)
+    late = pl.CostEstimate(flops=3 * 10**10, bytes_accessed=10**8, transcendentals=0)
+    ends = sum_over(ends, "seq", 2, side_x, late)
+    ends = sum_over(ends, "seq", side_y // 2, 2 * side_x)
     ends = sum_over(ends, "seq", side_z, side_x * side_y)
     lag_received = exchange(lag_sent)
     grad_key, grad_value, grad_filter = call(
         finish_kernel,
         (shape(plain, bf16), shape(plain, bf16), shape(plain, f32)),
         n_in=3,
+        hbm_out=(0, 1, 2),
+        scratch=(vm(plain, bf16), vm(plain, bf16), vm(plain, f32), dma((parts, 3))),
     )(lag_received, key_feats, value_feats)
     return (
         normed,

time: 112 us -> 111 us (level)
  waiting for transfers between devices: 43.4 us -> 40.2 us
  starting transfers between devices: 50.5 us -> 52.4 us
    all_to_all x4, waiting for transfers between devices: 28.9 us -> 27.2 us  [exchange(): lax.all_to_all(values, 'seq', split_axis=0, concat_axis=0, tiled=True)]
    all_to_all x4, starting transfers between devices: 32.2 us -> 33.6 us  [exchange(): lax.all_to_all(values, 'seq', split_axis=0, concat_axis=0, tiled=True)]
    ppermute x10 -> x9, waiting for transfers between devices: 11.5 us -> 10.1 us  [sum_over(): lax.ppermute(values, axis, places(side, stride, count, step))]
    ppermute x10 -> x9, starting transfers between devices: 13.8 us -> 14.3 us  [sum_over(): lax.ppermute(values, axis, places(side, stride, count, step))]
    pallas_call x3 -> x4, Pallas kernels: 7.99 us -> 7.59 us  [the longest x1 4.53 us: run_lag(): call(lag_kernel, pltpu.HBM((peers, 2 * channels, tokens), bf16), n_in=8 +...]
  transfers between devices with their start and end apart: 15 -> 14, of which waited for: 12 -> 11; matrix products, arithmetic and copies ran while one was open for 1% -> 1% of each run, Pallas kernels for 2% -> 6%
where the time goes in v3:
time: 111 us; the launch traced here: 110 us
  starting transfers between devices  52.4 us (47%)
  waiting for transfers between devices  40.2 us (36%)
  Pallas kernels  14.5 us (13%)
  local copies, waits for them, and re-layouts  2.12 us (2%)
    all_to_all x4, starting transfers between devices, exchange(): lax.all_to_all(values, 'seq', split_axis=0, concat_axis=0, tiled=True)  33.6 us
    all_to_all x4, waiting for transfers between devices, exchange(): lax.all_to_all(values, 'seq', split_axis=0, concat_axis=0, tiled=True)  27.2 us
    ppermute x9, starting transfers between devices, sum_over(): lax.ppermute(values, axis, places(side, stride, count, step))  14.3 us
    ppermute x9, waiting for transfers between devices, sum_over(): lax.ppermute(values, axis, places(side, stride, count, step))  10.1 us
    pallas_call x1, Pallas kernels, run_lag(): call(lag_kernel, pltpu.HBM((peers, 2 * channels, tokens), bf16), n_in=8 +...  4.53 us
    ppermute x1, starting transfers between devices, on_device(): far = lax.ppermute(near, 'chan', places(2, 2, 4, 1))  4.49 us
    pallas_call x1, Pallas kernels, run_conv(): call(conv_kernel, (shape((peers, channels, tokens), bf16), pltpu.HBM(spec...  3.77 us
    ppermute x1, waiting for transfers between devices, on_device(): far = lax.ppermute(near, 'chan', places(2, 2, 4, 1))  2.98 us
  transfers between devices with their start and end apart: 14, of which 11 were waited for; matrix products, arithmetic and copies ran while one was open for 1% of the time, Pallas kernels for 6%

profile of v3, /device:TPU:2, one launch (start us, length us, event | category | flops | bytes accessed | tf_op | source)
XLA Modules:
  0.0 110.4 jit_solution(11239613828999937884)
XLA Ops:
  0.7 2.2 %shard_map.188 = bf16[64,32,128]{2,1,0:T(8,128)(2,1)} custom-call(bf16[128,1024]{1,0:T(8,128)(2,1)} %key_ref.3, bf16[128,1024]{1,0:T(8,128)(2,1)} %value_ref.3, bf16[128,1024]{1,0:T(8,128)(2,1)} %filters_hbm.1), custom_call_target="tpu_custom_call" | custom-call | tf_op jit(solution)/shard_map/pallas_call | solution.py:472
  3.0 12.1 %all-to-all-start = ((bf16[64,32,128]{2,1,0:T(8,128)(2,1)}), bf16[64,32,128]{2,1,0:T(8,128)(2,1)S(1)}, u32[]{:S(2)}, u32[]{:S(2)}) async-start(bf16[64,32,128]{2,1,0:T(8,128)(2,1)} %shard_map.188), calls=%async_computation | async-start | bytes 1048576 | tf_op jit(solution)/shard_map/all_to_all | solution.py:465
  15.8 16.3 %all-to-all-done.recv_ref = bf16[64,32,128]{2,1,0:T(8,128)(2,1)S(1)} async-done(((bf16[64,32,128]{2,1,0:T(8,128)(2,1)}), bf16[64,32,128]{2,1,0:T(8,128)(2,1)S(1)}, u32[]{:S(2)}, u32[]{:S(2)}) %all-to-all-start) | async-done | bytes 524320 | tf_op jit(solution)/shard_map/all_to_all | solution.py:465
  32.1 3.8 %shard_map.189 = (bf16[64,16,128]{2,1,0:T(8,128)(2,1)}, f32[2048,256]{1,0:T(8,128)}) custom-call(bf16[64,32,128]{2,1,0:T(8,128)(2,1)S(1)} %all-to-all-done.recv_ref, f32[16]{0:T(128)S(1)} %dynamic_slice.3.skip_ref, bf16[128,128]{1,0:T(8,128)(2,1)S(1)} %copy-done.9, bf16[64,384]{1,0:T(8,128)(2,1)S(1)} %copy-done.8, f32[128,128]{1,0:T(8,128)S(1)} %copy-done.5, ...), custom_call_target="tpu_custom_call" | custom-call | tf_op jit(solution)/shard_map/pallas_call | solution.py:409
  35.9 5.9 %all-to-all-start.1 = ((bf16[64,16,128]{2,1,0:T(8,128)(2,1)}), bf16[64,16,128]{2,1,0:T(8,128)(2,1)S(1)}, u32[]{:S(2)}, u32[]{:S(2)}) async-start(bf16[64,16,128]{2,1,0:T(8,128)(2,1)} %get-tuple-element.20), calls=%async_computation.1 | async-start | bytes 524288 | tf_op jit(solution)/shard_map/all_to_all | solution.py:465
  42.9 9.8 %all-to-all-done.1 = bf16[64,16,128]{2,1,0:T(8,128)(2,1)S(1)} async-done(((bf16[64,16,128]{2,1,0:T(8,128)(2,1)}), bf16[64,16,128]{2,1,0:T(8,128)(2,1)S(1)}, u32[]{:S(2)}, u32[]{:S(2)}) %all-to-all-start.1) | async-done | bytes 262176 | tf_op jit(solution)/shard_map/all_to_all | solution.py:465
  53.1 1.1 %collective-permute-done = f32[2,128]{1,0:T(2,128)S(1)} collective-permute-done((f32[2,128]{1,0:T(2,128)S(1)}, f32[2,128]{1,0:T(2,128)S(1)}, u32[]{:S(2)}, u32[]{:S(2)}) %collective-permute-start) | collective-permute-done | bytes 1056 | tf_op jit(solution)/shard_map/ppermute | solution.py:367
  54.2 4.5 %collective-permute-start.1 = (f32[2,128]{1,0:T(2,128)S(1)}, f32[2,128]{1,0:T(2,128)S(1)}, u32[]{:S(2)}, u32[]{:S(2)}) collective-permute-start(f32[2,128]{1,0:T(2,128)S(1)} %add.28.near_ref), channel_id=1, source_target_pairs={{0,2},{1,3},{2,0},{3,1},{4,6},{5,7},{6,4},{7,5},{8,10},{9,11},{10,... | collective-permute-start | bytes 3080 | tf_op jit(solution)/shard_map/ppermute | solution.py:500
  58.7 3.0 %collective-permute-done.1.far_ref = f32[2,128]{1,0:T(2,128)S(1)} collective-permute-done((f32[2,128]{1,0:T(2,128)S(1)}, f32[2,128]{1,0:T(2,128)S(1)}, u32[]{:S(2)}, u32[]{:S(2)}) %collective-permute-start.1) | collective-permute-done | bytes 1056 | tf_op jit(solution)/shard_map/ppermute | solution.py:500
  62.5 5.9 %all-to-all-start.2 = ((bf16[64,16,128]{2,1,0:T(8,128)(2,1)}), bf16[64,16,128]{2,1,0:T(8,128)(2,1)S(1)}, u32[]{:S(2)}, u32[]{:S(2)}) async-start(bf16[64,16,128]{2,1,0:T(8,128)(2,1)} %bitcast.10), calls=%async_computation.2 | async-start | bytes 524288 | tf_op jit(solution)/shard_map/all_to_all | solution.py:465
  68.5 1.4 %shard_map.192 = (bf16[128,1024]{1,0:T(8,128)(2,1)}, bf16[128,1024]{1,0:T(8,128)(2,1)}, bf16[128,1024]{1,0:T(8,128)(2,1)}, f32[2,1024]{1,0:T(2,128)S(1)}) custom-call(f32[2,128]{1,0:T(2,128)S(1)} %add.28.near_ref, f32[2,128]{1,0:T(2,128)S(1)} %collective-permute-done.1.far_ref, bf16[1024,128]{1,0:T(8,128)(2,1)S(1)} %bitcast.7, ...), custom_call_target="tpu_custom_call" | custom-call | flops 1000000 | bytes 4000000 | tf_op jit(solution)/shard_map/pallas_call | solution.py:509
  70.4 2.5 %collective-permute-start.3 = (f32[2,1024]{1,0:T(2,128)S(1)}, f32[2,1024]{1,0:T(2,128)S(1)}, u32[]{:S(2)}, u32[]{:S(2)}) collective-permute-start(f32[2,1024]{1,0:T(2,128)S(1)} %get-tuple-element.28), channel_id=1, source_target_pairs={{0,8},{4,12},{8,0},{12,4},{16,24},{20,28},{24,16},{28,20},{32,40},... | collective-permute-start | bytes 24584 | tf_op jit(solution)/shard_map/ppermute | solution.py:367
  72.8 1.8 %collective-permute-start.2 = (f32[2,1024]{1,0:T(2,128)S(1)}, f32[2,1024]{1,0:T(2,128)S(1)}, u32[]{:S(2)}, u32[]{:S(2)}) collective-permute-start(f32[2,1024]{1,0:T(2,128)S(1)} %get-tuple-element.28), channel_id=1, source_target_pairs={{0,4},{4,8},{8,12},{12,0},{16,20},{20,24},{24,28},{28,16},{32,36},... | collective-permute-start | bytes 24584 | tf_op jit(solution)/shard_map/ppermute | solution.py:367
  74.6 1.0 collective-permute-done.3
  76.5 1.7 %collective-permute-start.5 = (f32[2,1024]{1,0:T(2,128)S(1)}, f32[2,1024]{1,0:T(2,128)S(1)}, u32[]{:S(2)}, u32[]{:S(2)}) collective-permute-start(f32[2,1024]{1,0:T(2,128)S(1)} %add_add_fusion.1.rest_0_.refs_0_), channel_id=1, source_target_pairs={{0,16},{4,20},{8,24},{12,28},{16,0},{20,4},{24,8},{28,12},{32,48},... | collective-permute-start | bytes 24584 | tf_op jit(solution)/shard_map/ppermute | solution.py:367
  78.2 1.1 %all-to-all-done.2.recv_ref = bf16[64,16,128]{2,1,0:T(8,128)(2,1)S(1)} async-done(((bf16[64,16,128]{2,1,0:T(8,128)(2,1)}), bf16[64,16,128]{2,1,0:T(8,128)(2,1)S(1)}, u32[]{:S(2)}, u32[]{:S(2)}) %all-to-all-start.2) | async-done | bytes 262176 | tf_op jit(solution)/shard_map/all_to_all | solution.py:465
  79.4 4.5 %shard_map.194 = bf16[64,32,128]{2,1,0:T(8,128)(2,1)} custom-call(bf16[64,16,128]{2,1,0:T(8,128)(2,1)S(1)} %all-to-all-done.2.recv_ref, f32[16]{0:T(128)S(1)} %copy-done.13, bf16[128,128]{1,0:T(8,128)(2,1)S(1)} %copy-done.9, bf16[64,384]{1,0:T(8,128)(2,1)S(1)} %copy-done.8, f32[128,128]{1,0:T(8,128)S(1)} %copy-done.5, bf16[768,256]{1,0:T(8,128)(2,1)S(1)} %copy-done.3, ...), custom_call_target="tpu_custom_call" | custom-call | tf_op jit(solution)/shard_map/pallas_call | solution.py:431
  83.9 9.7 %all-to-all-start.3 = ((bf16[64,32,128]{2,1,0:T(8,128)(2,1)}), bf16[64,32,128]{2,1,0:T(8,128)(2,1)S(1)}, u32[]{:S(2)}, u32[]{:S(2)}) async-start(bf16[64,32,128]{2,1,0:T(8,128)(2,1)} %shard_map.194), calls=%async_computation.3 | async-start | bytes 1048576 | tf_op jit(solution)/shard_map/all_to_all | solution.py:465
  93.6 3.1 %collective-permute-start.6 = (f32[2,1024]{1,0:T(2,128)S(1)}, f32[2,1024]{1,0:T(2,128)S(1)}, u32[]{:S(2)}, u32[]{:S(2)}) collective-permute-start(f32[2,1024]{1,0:T(2,128)S(1)} %shard_map.196), channel_id=1, source_target_pairs={{0,32},{4,36},{8,40},{12,44},{16,48},{20,52},{24,56},{28,60},{32,0... | collective-permute-start | bytes 24584 | tf_op jit(solution)/shard_map/ppermute | solution.py:367
  96.7 2.2 %collective-permute-done.6 = f32[2,1024]{1,0:T(2,128)S(1)} collective-permute-done((f32[2,1024]{1,0:T(2,128)S(1)}, f32[2,1024]{1,0:T(2,128)S(1)}, u32[]{:S(2)}, u32[]{:S(2)}) %collective-permute-start.6) | collective-permute-done | bytes 8224 | tf_op jit(solution)/shard_map/ppermute | solution.py:367
  98.9 3.8 %collective-permute-start.9 = (f32[2,1024]{1,0:T(2,128)S(1)}, f32[2,1024]{1,0:T(2,128)S(1)}, u32[]{:S(2)}, u32[]{:S(2)}) collective-permute-start(f32[2,1024]{1,0:T(2,128)S(1)} %add.32), channel_id=1, source_target_pairs={{0,192},{4,196},{8,200},{12,204},{16,208},{20,212},{24,216},{28,22... | collective-permute-start | bytes 24584 | tf_op jit(solution)/shard_map/ppermute | solution.py:367
  104.0 3.2 %collective-permute-done.8 = f32[2,1024]{1,0:T(2,128)S(1)} collective-permute-done((f32[2,1024]{1,0:T(2,128)S(1)}, f32[2,1024]{1,0:T(2,128)S(1)}, u32[]{:S(2)}, u32[]{:S(2)}) %collective-permute-start.8) | collective-permute-done | bytes 8224 | tf_op jit(solution)/shard_map/ppermute | solution.py:367
  107.2 1.2 %collective-permute-done.7 = f32[2,1024]{1,0:T(2,128)S(1)} collective-permute-done((f32[2,1024]{1,0:T(2,128)S(1)}, f32[2,1024]{1,0:T(2,128)S(1)}, u32[]{:S(2)}, u32[]{:S(2)}) %collective-permute-start.7) | collective-permute-done | bytes 8224 | tf_op jit(solution)/shard_map/ppermute | solution.py:367
  109.1 1.2 %shard_map.195 = (bf16[128,1024]{1,0:T(8,128)(2,1)}, bf16[128,1024]{1,0:T(8,128)(2,1)}, f32[128,1024]{1,0:T(8,128)}) custom-call(bf16[64,32,128]{2,1,0:T(8,128)(2,1)S(1)} %all-to-all-done.3.recv_ref, bf16[128,1024]{1,0:T(8,128)(2,1)S(1)} %copy-done, bf16[128,1024]{1,0:T(8,128)(2,1)S(1)} %copy-done.1), custom_call_target="tpu_custom_call" | custom-call | tf_op jit(solution)/shard_map/pallas_call | solution.py:523
  (47 shorter events, 6.4 us)
Async XLA Ops:
  0.6 31.5 %copy-start.2 = (bf16[768,256]{1,0:T(8,128)(2,1)S(1)}, bf16[768,256]{1,0:T(8,128)(2,1)}, u32[]{:S(2)}) copy-start(bf16[768,256]{1,0:T(8,128)(2,1)} %constant.26.clone.inverse_ref) | copy-start | bytes 1179652
  0.6 31.4 %copy-start.3 = (bf16[768,256]{1,0:T(8,128)(2,1)S(1)}, bf16[768,256]{1,0:T(8,128)(2,1)}, u32[]{:S(2)}) copy-start(bf16[768,256]{1,0:T(8,128)(2,1)} %constant.25.clone.inner_ref) | copy-start | bytes 1179652
  0.7 31.4 %copy-start.5 = (f32[128,128]{1,0:T(8,128)S(1)}, f32[128,128]{1,0:T(8,128)}, u32[]{:S(2)}) copy-start(f32[128,128]{1,0:T(8,128)} %constant.24.clone.twiddle_ref) | copy-start | bytes 196612
  0.7 31.4 %copy-start.8 = (bf16[64,384]{1,0:T(8,128)(2,1)S(1)}, bf16[64,384]{1,0:T(8,128)(2,1)}, u32[]{:S(2)}) copy-start(bf16[64,384]{1,0:T(8,128)(2,1)} %constant.23.clone.last_ref) | copy-start | bytes 147460
  0.7 31.4 %copy-start.9 = (bf16[128,128]{1,0:T(8,128)(2,1)S(1)}, bf16[128,128]{1,0:T(8,128)(2,1)}, u32[]{:S(2)}) copy-start(bf16[128,128]{1,0:T(8,128)(2,1)} %constant.22.clone.first_ref) | copy-start | bytes 98308
  0.7 41.1 %copy-start.4 = (bf16[128,1024]{1,0:T(8,128)(2,1)S(1)}, bf16[128,1024]{1,0:T(8,128)(2,1)}, u32[]{:S(2)}) copy-start(bf16[128,1024]{1,0:T(8,128)(2,1)} %cotangent_ref.3) | copy-start | bytes 786436
  0.7 41.1 %copy-start.7 = (bf16[128,1024]{1,0:T(8,128)(2,1)S(1)}, bf16[128,1024]{1,0:T(8,128)(2,1)}, u32[]{:S(2)}) copy-start(bf16[128,1024]{1,0:T(8,128)(2,1)} %query_ref.1) | copy-start | bytes 786436
  0.7 41.1 %copy-start.6 = (bf16[128,1024]{1,0:T(8,128)(2,1)S(1)}, bf16[128,1024]{1,0:T(8,128)(2,1)}, u32[]{:S(2)}) copy-start(bf16[128,1024]{1,0:T(8,128)(2,1)} %residual_ref.1) | copy-start | bytes 786436
  3.0 29.1 %all-to-all-start = ((bf16[64,32,128]{2,1,0:T(8,128)(2,1)}), bf16[64,32,128]{2,1,0:T(8,128)(2,1)S(1)}, u32[]{:S(2)}, u32[]{:S(2)}) async-start(bf16[64,32,128]{2,1,0:T(8,128)(2,1)} %shard_map.188), calls=%async_computation | async-start | bytes 1048576 | tf_op jit(solution)/shard_map/all_to_all | solution.py:465
  35.9 16.8 %all-to-all-start.1 = ((bf16[64,16,128]{2,1,0:T(8,128)(2,1)}), bf16[64,16,128]{2,1,0:T(8,128)(2,1)S(1)}, u32[]{:S(2)}, u32[]{:S(2)}) async-start(bf16[64,16,128]{2,1,0:T(8,128)(2,1)} %get-tuple-element.20), calls=%async_computation.1 | async-start | bytes 524288 | tf_op jit(solution)/shard_map/all_to_all | solution.py:465
  42.5 25.9 %copy-start = (bf16[128,1024]{1,0:T(8,128)(2,1)S(1)}, bf16[128,1024]{1,0:T(8,128)(2,1)}, u32[]{:S(2)}) copy-start(bf16[128,1024]{1,0:T(8,128)(2,1)} %key_ref.3) | copy-start | bytes 786436
  42.5 26.0 %copy-start.1 = (bf16[128,1024]{1,0:T(8,128)(2,1)S(1)}, bf16[128,1024]{1,0:T(8,128)(2,1)}, u32[]{:S(2)}) copy-start(bf16[128,1024]{1,0:T(8,128)(2,1)} %value_ref.3) | copy-start | bytes 786436
  53.0 1.2 %collective-permute-start = (f32[2,128]{1,0:T(2,128)S(1)}, f32[2,128]{1,0:T(2,128)S(1)}, u32[]{:S(2)}, u32[]{:S(2)}) collective-permute-start(f32[2,128]{1,0:T(2,128)S(1)} %shard_map.191), channel_id=1, source_target_pairs={{0,1},{1,0},{2,3},{3,2},{4,5},{5,4},{6,7},{7,6},{8,9},{9,8},{10,11... | collective-permute-start | bytes 3080 | tf_op jit(solution)/shard_map/ppermute | solution.py:367
  54.2 7.5 %collective-permute-start.1 = (f32[2,128]{1,0:T(2,128)S(1)}, f32[2,128]{1,0:T(2,128)S(1)}, u32[]{:S(2)}, u32[]{:S(2)}) collective-permute-start(f32[2,128]{1,0:T(2,128)S(1)} %add.28.near_ref), channel_id=1, source_target_pairs={{0,2},{1,3},{2,0},{3,1},{4,6},{5,7},{6,4},{7,5},{8,10},{9,11},{10,... | collective-permute-start | bytes 3080 | tf_op jit(solution)/shard_map/ppermute | solution.py:500
  62.5 16.8 %all-to-all-start.2 = ((bf16[64,16,128]{2,1,0:T(8,128)(2,1)}), bf16[64,16,128]{2,1,0:T(8,128)(2,1)S(1)}, u32[]{:S(2)}, u32[]{:S(2)}) async-start(bf16[64,16,128]{2,1,0:T(8,128)(2,1)} %bitcast.10), calls=%async_computation.2 | async-start | bytes 524288 | tf_op jit(solution)/shard_map/all_to_all | solution.py:465
  69.9 4.7 %collective-permute-start.4 = (f32[2,1024]{1,0:T(2,128)S(1)}, f32[2,1024]{1,0:T(2,128)S(1)}, u32[]{:S(2)}, u32[]{:S(2)}) collective-permute-start(f32[2,1024]{1,0:T(2,128)S(1)} %get-tuple-element.28), channel_id=1, source_target_pairs={{0,12},{4,0},{8,4},{12,8},{16,28},{20,16},{24,20},{28,24},{32,44},... | collective-permute-start | bytes 24584 | tf_op jit(solution)/shard_map/ppermute | solution.py:367
  70.4 5.3 %collective-permute-start.3 = (f32[2,1024]{1,0:T(2,128)S(1)}, f32[2,1024]{1,0:T(2,128)S(1)}, u32[]{:S(2)}, u32[]{:S(2)}) collective-permute-start(f32[2,1024]{1,0:T(2,128)S(1)} %get-tuple-element.28), channel_id=1, source_target_pairs={{0,8},{4,12},{8,0},{12,4},{16,24},{20,28},{24,16},{28,20},{32,40},... | collective-permute-start | bytes 24584 | tf_op jit(solution)/shard_map/ppermute | solution.py:367
  72.8 3.7 %collective-permute-start.2 = (f32[2,1024]{1,0:T(2,128)S(1)}, f32[2,1024]{1,0:T(2,128)S(1)}, u32[]{:S(2)}, u32[]{:S(2)}) collective-permute-start(f32[2,1024]{1,0:T(2,128)S(1)} %get-tuple-element.28), channel_id=1, source_target_pairs={{0,4},{4,8},{8,12},{12,0},{16,20},{20,24},{24,28},{28,16},{32,36},... | collective-permute-start | bytes 24584 | tf_op jit(solution)/shard_map/ppermute | solution.py:367
  76.5 17.1 %collective-permute-start.5 = (f32[2,1024]{1,0:T(2,128)S(1)}, f32[2,1024]{1,0:T(2,128)S(1)}, u32[]{:S(2)}, u32[]{:S(2)}) collective-permute-start(f32[2,1024]{1,0:T(2,128)S(1)} %add_add_fusion.1.rest_0_.refs_0_), channel_id=1, source_target_pairs={{0,16},{4,20},{8,24},{12,28},{16,0},{20,4},{24,8},{28,12},{32,48},... | collective-permute-start | bytes 24584 | tf_op jit(solution)/shard_map/ppermute | solution.py:367
  83.9 25.2 %all-to-all-start.3 = ((bf16[64,32,128]{2,1,0:T(8,128)(2,1)}), bf16[64,32,128]{2,1,0:T(8,128)(2,1)S(1)}, u32[]{:S(2)}, u32[]{:S(2)}) async-start(bf16[64,32,128]{2,1,0:T(8,128)(2,1)} %shard_map.194), calls=%async_computation.3 | async-start | bytes 1048576 | tf_op jit(solution)/shard_map/all_to_all | solution.py:465
  93.6 5.2 %collective-permute-start.6 = (f32[2,1024]{1,0:T(2,128)S(1)}, f32[2,1024]{1,0:T(2,128)S(1)}, u32[]{:S(2)}, u32[]{:S(2)}) collective-permute-start(f32[2,1024]{1,0:T(2,128)S(1)} %shard_map.196), channel_id=1, source_target_pairs={{0,32},{4,36},{8,40},{12,44},{16,48},{20,52},{24,56},{28,60},{32,0... | collective-permute-start | bytes 24584 | tf_op jit(solution)/shard_map/ppermute | solution.py:367
  98.9 5.1 %collective-permute-start.9 = (f32[2,1024]{1,0:T(2,128)S(1)}, f32[2,1024]{1,0:T(2,128)S(1)}, u32[]{:S(2)}, u32[]{:S(2)}) collective-permute-start(f32[2,1024]{1,0:T(2,128)S(1)} %add.32), channel_id=1, source_target_pairs={{0,192},{4,196},{8,200},{12,204},{16,208},{20,212},{24,216},{28,22... | collective-permute-start | bytes 24584 | tf_op jit(solution)/shard_map/ppermute | solution.py:367
  102.6 4.5 %collective-permute-start.8 = (f32[2,1024]{1,0:T(2,128)S(1)}, f32[2,1024]{1,0:T(2,128)S(1)}, u32[]{:S(2)}, u32[]{:S(2)}) collective-permute-start(f32[2,1024]{1,0:T(2,128)S(1)} %add.32), channel_id=1, source_target_pairs={{0,128},{4,132},{8,136},{12,140},{16,144},{20,148},{24,152},{28,15... | collective-permute-start | bytes 24584 | tf_op jit(solution)/shard_map/ppermute | solution.py:367
  103.0 5.4 %collective-permute-start.7 = (f32[2,1024]{1,0:T(2,128)S(1)}, f32[2,1024]{1,0:T(2,128)S(1)}, u32[]{:S(2)}, u32[]{:S(2)}) collective-permute-start(f32[2,1024]{1,0:T(2,128)S(1)} %add.32), channel_id=1, source_target_pairs={{0,64},{4,68},{8,72},{12,76},{16,80},{20,84},{24,88},{28,92},{32,9... | collective-permute-start | bytes 24584 | tf_op jit(solution)/shard_map/ppermute | solution.py:367
  (4 other events, 71.5 us)

commit v4 on v3

--- a/solution.py
+++ b/solution.py
@@ -293,22 +293,18 @@
         copy.wait()
 
 
-def norm_kernel(
-    total, near_ref, far_ref, mixed_ref, res_ref, q_ref, sg_ref, gain_ref, cotangent_ref, key_ref, value_ref,
-    normed_ref, gres_ref, gq_ref, ends_ref,
+def ends_kernel(
+    total, near_ref, far_ref, mixed_ref, res_ref, q_ref, sg_ref, cotangent_ref, key_ref, value_ref,
+    ends_ref,
 ):
     width, tokens = res_ref.shape
     inv_rms, alpha = norm_terms((near_ref, far_ref), total)
     for j in range(width // tokens):
         cols = pl.ds(j * tokens, tokens)
-        mixed = mixed_ref[cols, :].astype(f32)
         query = q_ref[cols, :].astype(f32)
-        summed = res_ref[cols, :].astype(f32) + query * mixed
+        summed = res_ref[cols, :].astype(f32) + query * mixed_ref[cols, :].astype(f32)
         grad_summed = inv_rms * sg_ref[cols, :] - summed * alpha
         unit = (summed * inv_rms).T
-        normed_ref[:, cols] = (unit * gain_ref[:, cols]).astype(bf16)
-        gres_ref[:, cols] = grad_summed.astype(bf16).T
-        gq_ref[:, cols] = (grad_summed * mixed).astype(bf16).T
         grad_mixed = (grad_summed * query).astype(bf16).T.astype(f32)
         product = key_ref[:, cols].astype(f32) * value_ref[:, cols].astype(f32)
         product = product.astype(bf16).astype(f32)
@@ -316,6 +312,22 @@
         ends_ref[1:2, cols] = jnp.sum(
             cotangent_ref[:, cols].astype(f32) * unit, axis=0, keepdims=True
         )
+
+
+def norm_kernel(
+    total, near_ref, far_ref, mixed_ref, res_ref, q_ref, sg_ref, gain_ref,
+    normed_ref, gres_ref, gq_ref,
+):
+    width, tokens = res_ref.shape
+    inv_rms, alpha = norm_terms((near_ref, far_ref), total)
+    for j in range(width // tokens):
+        cols = pl.ds(j * tokens, tokens)
+        mixed = mixed_ref[cols, :].astype(f32)
+        summed = res_ref[cols, :].astype(f32) + q_ref[cols, :].astype(f32) * mixed
+        grad_summed = inv_rms * sg_ref[cols, :] - summed * alpha
+        normed_ref[:, cols] = ((summed * inv_rms).T * gain_ref[:, cols]).astype(bf16)
+        gres_ref[:, cols] = grad_summed.astype(bf16).T
+        gq_ref[:, cols] = (grad_summed * mixed).astype(bf16).T
 
 
 def finish_kernel(
@@ -506,12 +518,15 @@
         scratch=(vm(turned, bf16), dma((parts,))),
     )(near, far, mixed_t, res_t, q_t, sg_t)
     grad_received = exchange(grad_sent.reshape(peers, channels, tokens))
-    normed, grad_residual, grad_query, ends = call(
+    ends = call(
+        functools.partial(ends_kernel, total), shape((2, width), f32), n_in=9, cost=aside
+    )(near, far, mixed_t, res_t, q_t, sg_t, cotangent, key_feats, value_feats)
+    normed, grad_residual, grad_query = call(
         functools.partial(norm_kernel, total),
-        (shape(plain, bf16), shape(plain, bf16), shape(plain, bf16), shape((2, width), f32)),
-        n_in=10,
+        (shape(plain, bf16), shape(plain, bf16), shape(plain, bf16)),
+        n_in=7,
         cost=aside,
-    )(near, far, mixed_t, res_t, q_t, sg_t, gain_row, cotangent, key_feats, value_feats)
+    )(near, far, mixed_t, res_t, q_t, sg_t, gain_row)
     side_z, side_y, side_x = sides
     ends = sum_over(ends, "seq", side_x, 1)
     lag_sent = run_lag(grad_received, skip_here, spectra, ends)

time: 111 us -> 109 us (0.982)
  waiting for transfers between devices: 40.2 us -> 38 us
    ppermute x9, waiting for transfers between devices: 10.1 us -> 6.51 us  [sum_over(): lax.ppermute(values, axis, places(side, stride, count, step))]
    all_to_all x4, waiting for transfers between devices: 27.2 us -> 28.5 us  [exchange(): lax.all_to_all(values, 'seq', split_axis=0, concat_axis=0, tiled=True)]
  transfers between devices with their start and end apart: 14 -> 14, of which waited for: 11 -> 10; matrix products, arithmetic and copies ran while one was open for 1% -> 1% of each run, Pallas kernels for 6% -> 6%
where the time goes in v4:
time: 109 us
  starting transfers between devices  53 us (49%)
  waiting for transfers between devices  38 us (35%)
  Pallas kernels  14.7 us (13%)
  local copies, waits for them, and re-layouts  2.12 us (2%)
    all_to_all x4, starting transfers between devices, exchange(): lax.all_to_all(values, 'seq', split_axis=0, concat_axis=0, tiled=True)  33.3 us
    all_to_all x4, waiting for transfers between devices, exchange(): lax.all_to_all(values, 'seq', split_axis=0, concat_axis=0, tiled=True)  28.5 us
    ppermute x9, starting transfers between devices, sum_over(): lax.ppermute(values, axis, places(side, stride, count, step))  15.2 us
    ppermute x9, waiting for transfers between devices, sum_over(): lax.ppermute(values, axis, places(side, stride, count, step))  6.51 us
    pallas_call x1, Pallas kernels, run_lag(): call(lag_kernel, pltpu.HBM((peers, 2 * channels, tokens), bf16), n_in=8 +...  4.53 us
    ppermute x1, starting transfers between devices, on_device(): far = lax.ppermute(near, 'chan', places(2, 2, 4, 1))  4.49 us
    pallas_call x1, Pallas kernels, run_conv(): call(conv_kernel, (shape((peers, channels, tokens), bf16), pltpu.HBM(spec...  3.77 us
    ppermute x1, waiting for transfers between devices, on_device(): far = lax.ppermute(near, 'chan', places(2, 2, 4, 1))  2.98 us
  transfers between devices with their start and end apart: 14, of which 10 were waited for; matrix products, arithmetic and copies ran while one was open for 1% of the time, Pallas kernels for 6%

profile of v4, /device:TPU:2, one launch (start us, length us, event | category | flops | bytes accessed | tf_op | source)
XLA Modules:
  0.0 108.9 jit_solution(17765785264514774786)
XLA Ops:
  0.7 2.2 %shard_map.188 = bf16[64,32,128]{2,1,0:T(8,128)(2,1)} custom-call(bf16[128,1024]{1,0:T(8,128)(2,1)} %key_ref.3, bf16[128,1024]{1,0:T(8,128)(2,1)} %value_ref.3, bf16[128,1024]{1,0:T(8,128)(2,1)} %filters_hbm.1), custom_call_target="tpu_custom_call" | custom-call | tf_op jit(solution)/shard_map/pallas_call | solution.py:484
  3.0 12.1 %all-to-all-start = ((bf16[64,32,128]{2,1,0:T(8,128)(2,1)}), bf16[64,32,128]{2,1,0:T(8,128)(2,1)S(1)}, u32[]{:S(2)}, u32[]{:S(2)}) async-start(bf16[64,32,128]{2,1,0:T(8,128)(2,1)} %shard_map.188), calls=%async_computation | async-start | bytes 1048576 | tf_op jit(solution)/shard_map/all_to_all | solution.py:477
  15.8 16.3 %all-to-all-done.recv_ref = bf16[64,32,128]{2,1,0:T(8,128)(2,1)S(1)} async-done(((bf16[64,32,128]{2,1,0:T(8,128)(2,1)}), bf16[64,32,128]{2,1,0:T(8,128)(2,1)S(1)}, u32[]{:S(2)}, u32[]{:S(2)}) %all-to-all-start) | async-done | bytes 524320 | tf_op jit(solution)/shard_map/all_to_all | solution.py:477
  32.1 3.8 %shard_map.189 = (bf16[64,16,128]{2,1,0:T(8,128)(2,1)}, f32[2048,256]{1,0:T(8,128)}) custom-call(bf16[64,32,128]{2,1,0:T(8,128)(2,1)S(1)} %all-to-all-done.recv_ref, f32[16]{0:T(128)S(1)} %dynamic_slice.3.skip_ref, bf16[128,128]{1,0:T(8,128)(2,1)S(1)} %copy-done.9, bf16[64,384]{1,0:T(8,128)(2,1)S(1)} %copy-done.8, f32[128,128]{1,0:T(8,128)S(1)} %copy-done.5, ...), custom_call_target="tpu_custom_call" | custom-call | tf_op jit(solution)/shard_map/pallas_call | solution.py:421
  35.9 5.9 %all-to-all-start.1 = ((bf16[64,16,128]{2,1,0:T(8,128)(2,1)}), bf16[64,16,128]{2,1,0:T(8,128)(2,1)S(1)}, u32[]{:S(2)}, u32[]{:S(2)}) async-start(bf16[64,16,128]{2,1,0:T(8,128)(2,1)} %get-tuple-element.19), calls=%async_computation.1 | async-start | bytes 524288 | tf_op jit(solution)/shard_map/all_to_all | solution.py:477
  42.9 9.8 %all-to-all-done.1 = bf16[64,16,128]{2,1,0:T(8,128)(2,1)S(1)} async-done(((bf16[64,16,128]{2,1,0:T(8,128)(2,1)}), bf16[64,16,128]{2,1,0:T(8,128)(2,1)S(1)}, u32[]{:S(2)}, u32[]{:S(2)}) %all-to-all-start.1) | async-done | bytes 262176 | tf_op jit(solution)/shard_map/all_to_all | solution.py:477
  53.1 1.1 %collective-permute-done = f32[2,128]{1,0:T(2,128)S(1)} collective-permute-done((f32[2,128]{1,0:T(2,128)S(1)}, f32[2,128]{1,0:T(2,128)S(1)}, u32[]{:S(2)}, u32[]{:S(2)}) %collective-permute-start) | collective-permute-done | bytes 1056 | tf_op jit(solution)/shard_map/ppermute | solution.py:379
  54.2 4.5 %collective-permute-start.1 = (f32[2,128]{1,0:T(2,128)S(1)}, f32[2,128]{1,0:T(2,128)S(1)}, u32[]{:S(2)}, u32[]{:S(2)}) collective-permute-start(f32[2,128]{1,0:T(2,128)S(1)} %add.28.near_ref), channel_id=1, source_target_pairs={{0,2},{1,3},{2,0},{3,1},{4,6},{5,7},{6,4},{7,5},{8,10},{9,11},{10,... | collective-permute-start | bytes 3080 | tf_op jit(solution)/shard_map/ppermute | solution.py:512
  58.7 3.0 %collective-permute-done.1.far_ref = f32[2,128]{1,0:T(2,128)S(1)} collective-permute-done((f32[2,128]{1,0:T(2,128)S(1)}, f32[2,128]{1,0:T(2,128)S(1)}, u32[]{:S(2)}, u32[]{:S(2)}) %collective-permute-start.1) | collective-permute-done | bytes 1056 | tf_op jit(solution)/shard_map/ppermute | solution.py:512
  62.5 5.9 %all-to-all-start.2 = ((bf16[64,16,128]{2,1,0:T(8,128)(2,1)}), bf16[64,16,128]{2,1,0:T(8,128)(2,1)S(1)}, u32[]{:S(2)}, u32[]{:S(2)}) async-start(bf16[64,16,128]{2,1,0:T(8,128)(2,1)} %bitcast.11), calls=%async_computation.2 | async-start | bytes 524288 | tf_op jit(solution)/shard_map/all_to_all | solution.py:477
  68.9 1.5 %collective-permute-start.2 = (f32[2,1024]{1,0:T(2,128)S(1)}, f32[2,1024]{1,0:T(2,128)S(1)}, u32[]{:S(2)}, u32[]{:S(2)}) collective-permute-start(f32[2,1024]{1,0:T(2,128)S(1)} %shard_map.194), channel_id=1, source_target_pairs={{0,4},{4,8},{8,12},{12,0},{16,20},{20,24},{24,28},{28,16},{32,36},... | collective-permute-start | bytes 24584 | tf_op jit(solution)/shard_map/ppermute | solution.py:379
  71.5 2.2 %collective-permute-start.4 = (f32[2,1024]{1,0:T(2,128)S(1)}, f32[2,1024]{1,0:T(2,128)S(1)}, u32[]{:S(2)}, u32[]{:S(2)}) collective-permute-start(f32[2,1024]{1,0:T(2,128)S(1)} %shard_map.194), channel_id=1, source_target_pairs={{0,12},{4,0},{8,4},{12,8},{16,28},{20,16},{24,20},{28,24},{32,44},... | collective-permute-start | bytes 24584 | tf_op jit(solution)/shard_map/ppermute | solution.py:379
  73.7 2.0 %collective-permute-done.3 = f32[2,1024]{1,0:T(2,128)S(1)} collective-permute-done((f32[2,1024]{1,0:T(2,128)S(1)}, f32[2,1024]{1,0:T(2,128)S(1)}, u32[]{:S(2)}, u32[]{:S(2)}) %collective-permute-start.3) | collective-permute-done | bytes 8224 | tf_op jit(solution)/shard_map/ppermute | solution.py:379
  75.7 1.8 %collective-permute-start.5 = (f32[2,1024]{1,0:T(2,128)S(1)}, f32[2,1024]{1,0:T(2,128)S(1)}, u32[]{:S(2)}, u32[]{:S(2)}) collective-permute-start(f32[2,1024]{1,0:T(2,128)S(1)} %add_add_fusion.1.rest_0_.refs_0_), channel_id=1, source_target_pairs={{0,16},{4,20},{8,24},{12,28},{16,0},{20,4},{24,8},{28,12},{32,48},... | collective-permute-start | bytes 24584 | tf_op jit(solution)/shard_map/ppermute | solution.py:379
  77.4 1.9 %all-to-all-done.2.recv_ref = bf16[64,16,128]{2,1,0:T(8,128)(2,1)S(1)} async-done(((bf16[64,16,128]{2,1,0:T(8,128)(2,1)}), bf16[64,16,128]{2,1,0:T(8,128)(2,1)S(1)}, u32[]{:S(2)}, u32[]{:S(2)}) %all-to-all-start.2) | async-done | bytes 262176 | tf_op jit(solution)/shard_map/all_to_all | solution.py:477
  79.4 4.5 %shard_map.195 = bf16[64,32,128]{2,1,0:T(8,128)(2,1)} custom-call(bf16[64,16,128]{2,1,0:T(8,128)(2,1)S(1)} %all-to-all-done.2.recv_ref, f32[16]{0:T(128)S(1)} %copy-done.13, bf16[128,128]{1,0:T(8,128)(2,1)S(1)} %copy-done.9, bf16[64,384]{1,0:T(8,128)(2,1)S(1)} %copy-done.8, f32[128,128]{1,0:T(8,128)S(1)} %copy-done.5, bf16[768,256]{1,0:T(8,128)(2,1)S(1)} %copy-done.2, ...), custom_call_target="tpu_custom_call" | custom-call | tf_op jit(solution)/shard_map/pallas_call | solution.py:443
  83.9 9.3 %all-to-all-start.3 = ((bf16[64,32,128]{2,1,0:T(8,128)(2,1)}), bf16[64,32,128]{2,1,0:T(8,128)(2,1)S(1)}, u32[]{:S(2)}, u32[]{:S(2)}) async-start(bf16[64,32,128]{2,1,0:T(8,128)(2,1)} %shard_map.195), calls=%async_computation.3 | async-start | bytes 1048576 | tf_op jit(solution)/shard_map/all_to_all | solution.py:477
  93.3 3.1 %collective-permute-start.6 = (f32[2,1024]{1,0:T(2,128)S(1)}, f32[2,1024]{1,0:T(2,128)S(1)}, u32[]{:S(2)}, u32[]{:S(2)}) collective-permute-start(f32[2,1024]{1,0:T(2,128)S(1)} %shard_map.197), channel_id=1, source_target_pairs={{0,32},{4,36},{8,40},{12,44},{16,48},{20,52},{24,56},{28,60},{32,0... | collective-permute-start | bytes 24584 | tf_op jit(solution)/shard_map/ppermute | solution.py:379
  96.3 2.2 %collective-permute-done.6 = f32[2,1024]{1,0:T(2,128)S(1)} collective-permute-done((f32[2,1024]{1,0:T(2,128)S(1)}, f32[2,1024]{1,0:T(2,128)S(1)}, u32[]{:S(2)}, u32[]{:S(2)}) %collective-permute-start.6) | collective-permute-done | bytes 8224 | tf_op jit(solution)/shard_map/ppermute | solution.py:379
  98.5 2.7 %collective-permute-start.7 = (f32[2,1024]{1,0:T(2,128)S(1)}, f32[2,1024]{1,0:T(2,128)S(1)}, u32[]{:S(2)}, u32[]{:S(2)}) collective-permute-start(f32[2,1024]{1,0:T(2,128)S(1)} %add.32), channel_id=1, source_target_pairs={{0,64},{4,68},{8,72},{12,76},{16,80},{20,84},{24,88},{28,92},{32,9... | collective-permute-start | bytes 24584 | tf_op jit(solution)/shard_map/ppermute | solution.py:379
  101.2 1.7 %collective-permute-start.8 = (f32[2,1024]{1,0:T(2,128)S(1)}, f32[2,1024]{1,0:T(2,128)S(1)}, u32[]{:S(2)}, u32[]{:S(2)}) collective-permute-start(f32[2,1024]{1,0:T(2,128)S(1)} %add.32), channel_id=1, source_target_pairs={{0,128},{4,132},{8,136},{12,140},{16,144},{20,148},{24,152},{28,15... | collective-permute-start | bytes 24584 | tf_op jit(solution)/shard_map/ppermute | solution.py:379
  102.9 1.2 %collective-permute-start.9 = (f32[2,1024]{1,0:T(2,128)S(1)}, f32[2,1024]{1,0:T(2,128)S(1)}, u32[]{:S(2)}, u32[]{:S(2)}) collective-permute-start(f32[2,1024]{1,0:T(2,128)S(1)} %add.32), channel_id=1, source_target_pairs={{0,192},{4,196},{8,200},{12,204},{16,208},{20,212},{24,216},{28,22... | collective-permute-start | bytes 24584 | tf_op jit(solution)/shard_map/ppermute | solution.py:379
  104.1 1.2 %shard_map.192 = (bf16[128,1024]{1,0:T(8,128)(2,1)}, bf16[128,1024]{1,0:T(8,128)(2,1)}, bf16[128,1024]{1,0:T(8,128)(2,1)}) custom-call(f32[2,128]{1,0:T(2,128)S(1)} %add.28.near_ref, f32[2,128]{1,0:T(2,128)S(1)} %collective-permute-done.1.far_ref, bf16[1024,128]{1,0:T(8,128)(2,1)S(1)} %bitcast.8, bf16[1024,128]{1,0:T(8,128)(2,1)S(1)} %get-tuple-element.20.res_ref, ...), custom_call_target="tpu_custom_call" | custom-call | flops 1000000 | bytes 4000000 | tf_op jit(solution)/shard_map/pallas_call | solution.py:524
  107.6 1.2 %shard_map.196 = (bf16[128,1024]{1,0:T(8,128)(2,1)}, bf16[128,1024]{1,0:T(8,128)(2,1)}, f32[128,1024]{1,0:T(8,128)}) custom-call(bf16[64,32,128]{2,1,0:T(8,128)(2,1)S(1)} %all-to-all-done.3.recv_ref, bf16[128,1024]{1,0:T(8,128)(2,1)S(1)} %copy-done, bf16[128,1024]{1,0:T(8,128)(2,1)S(1)} %copy-done.1), custom_call_target="tpu_custom_call" | custom-call | tf_op jit(solution)/shard_map/pallas_call | solution.py:538
  (48 shorter events, 6.8 us)
Async XLA Ops:
  0.6 31.5 %copy-start.9 = (bf16[128,128]{1,0:T(8,128)(2,1)S(1)}, bf16[128,128]{1,0:T(8,128)(2,1)}, u32[]{:S(2)}) copy-start(bf16[128,128]{1,0:T(8,128)(2,1)} %constant.22.clone.first_ref) | copy-start | bytes 98308
  0.6 31.5 %copy-start.8 = (bf16[64,384]{1,0:T(8,128)(2,1)S(1)}, bf16[64,384]{1,0:T(8,128)(2,1)}, u32[]{:S(2)}) copy-start(bf16[64,384]{1,0:T(8,128)(2,1)} %constant.23.clone.last_ref) | copy-start | bytes 147460
  0.7 31.4 %copy-start.5 = (f32[128,128]{1,0:T(8,128)S(1)}, f32[128,128]{1,0:T(8,128)}, u32[]{:S(2)}) copy-start(f32[128,128]{1,0:T(8,128)} %constant.24.clone.twiddle_ref) | copy-start | bytes 196612
  0.7 31.4 %copy-start.2 = (bf16[768,256]{1,0:T(8,128)(2,1)S(1)}, bf16[768,256]{1,0:T(8,128)(2,1)}, u32[]{:S(2)}) copy-start(bf16[768,256]{1,0:T(8,128)(2,1)} %constant.25.clone.inner_ref) | copy-start | bytes 1179652
  0.7 31.4 %copy-start.3 = (bf16[768,256]{1,0:T(8,128)(2,1)S(1)}, bf16[768,256]{1,0:T(8,128)(2,1)}, u32[]{:S(2)}) copy-start(bf16[768,256]{1,0:T(8,128)(2,1)} %constant.26.clone.inverse_ref) | copy-start | bytes 1179652
  0.7 41.1 %copy-start.6 = (bf16[128,1024]{1,0:T(8,128)(2,1)S(1)}, bf16[128,1024]{1,0:T(8,128)(2,1)}, u32[]{:S(2)}) copy-start(bf16[128,1024]{1,0:T(8,128)(2,1)} %residual_ref.1) | copy-start | bytes 786436
  0.7 41.1 %copy-start.7 = (bf16[128,1024]{1,0:T(8,128)(2,1)S(1)}, bf16[128,1024]{1,0:T(8,128)(2,1)}, u32[]{:S(2)}) copy-start(bf16[128,1024]{1,0:T(8,128)(2,1)} %query_ref.1) | copy-start | bytes 786436
  0.7 41.1 %copy-start.4 = (bf16[128,1024]{1,0:T(8,128)(2,1)S(1)}, bf16[128,1024]{1,0:T(8,128)(2,1)}, u32[]{:S(2)}) copy-start(bf16[128,1024]{1,0:T(8,128)(2,1)} %cotangent_ref.3) | copy-start | bytes 786436
  3.0 29.1 %all-to-all-start = ((bf16[64,32,128]{2,1,0:T(8,128)(2,1)}), bf16[64,32,128]{2,1,0:T(8,128)(2,1)S(1)}, u32[]{:S(2)}, u32[]{:S(2)}) async-start(bf16[64,32,128]{2,1,0:T(8,128)(2,1)} %shard_map.188), calls=%async_computation | async-start | bytes 1048576 | tf_op jit(solution)/shard_map/all_to_all | solution.py:477
  35.9 16.8 %all-to-all-start.1 = ((bf16[64,16,128]{2,1,0:T(8,128)(2,1)}), bf16[64,16,128]{2,1,0:T(8,128)(2,1)S(1)}, u32[]{:S(2)}, u32[]{:S(2)}) async-start(bf16[64,16,128]{2,1,0:T(8,128)(2,1)} %get-tuple-element.19), calls=%async_computation.1 | async-start | bytes 524288 | tf_op jit(solution)/shard_map/all_to_all | solution.py:477
  42.5 25.9 %copy-start = (bf16[128,1024]{1,0:T(8,128)(2,1)S(1)}, bf16[128,1024]{1,0:T(8,128)(2,1)}, u32[]{:S(2)}) copy-start(bf16[128,1024]{1,0:T(8,128)(2,1)} %key_ref.3) | copy-start | bytes 786436
  42.5 26.0 %copy-start.1 = (bf16[128,1024]{1,0:T(8,128)(2,1)S(1)}, bf16[128,1024]{1,0:T(8,128)(2,1)}, u32[]{:S(2)}) copy-start(bf16[128,1024]{1,0:T(8,128)(2,1)} %value_ref.3) | copy-start | bytes 786436
  53.0 1.2 %collective-permute-start = (f32[2,128]{1,0:T(2,128)S(1)}, f32[2,128]{1,0:T(2,128)S(1)}, u32[]{:S(2)}, u32[]{:S(2)}) collective-permute-start(f32[2,128]{1,0:T(2,128)S(1)} %shard_map.191), channel_id=1, source_target_pairs={{0,1},{1,0},{2,3},{3,2},{4,5},{5,4},{6,7},{7,6},{8,9},{9,8},{10,11... | collective-permute-start | bytes 3080 | tf_op jit(solution)/shard_map/ppermute | solution.py:379
  54.2 7.5 %collective-permute-start.1 = (f32[2,128]{1,0:T(2,128)S(1)}, f32[2,128]{1,0:T(2,128)S(1)}, u32[]{:S(2)}, u32[]{:S(2)}) collective-permute-start(f32[2,128]{1,0:T(2,128)S(1)} %add.28.near_ref), channel_id=1, source_target_pairs={{0,2},{1,3},{2,0},{3,1},{4,6},{5,7},{6,4},{7,5},{8,10},{9,11},{10,... | collective-permute-start | bytes 3080 | tf_op jit(solution)/shard_map/ppermute | solution.py:512
  62.5 16.8 %all-to-all-start.2 = ((bf16[64,16,128]{2,1,0:T(8,128)(2,1)}), bf16[64,16,128]{2,1,0:T(8,128)(2,1)S(1)}, u32[]{:S(2)}, u32[]{:S(2)}) async-start(bf16[64,16,128]{2,1,0:T(8,128)(2,1)} %bitcast.11), calls=%async_computation.2 | async-start | bytes 524288 | tf_op jit(solution)/shard_map/all_to_all | solution.py:477
  68.9 4.8 %collective-permute-start.2 = (f32[2,1024]{1,0:T(2,128)S(1)}, f32[2,1024]{1,0:T(2,128)S(1)}, u32[]{:S(2)}, u32[]{:S(2)}) collective-permute-start(f32[2,1024]{1,0:T(2,128)S(1)} %shard_map.194), channel_id=1, source_target_pairs={{0,4},{4,8},{8,12},{12,0},{16,20},{20,24},{24,28},{28,16},{32,36},... | collective-permute-start | bytes 24584 | tf_op jit(solution)/shard_map/ppermute | solution.py:379
  70.4 5.2 %collective-permute-start.3 = (f32[2,1024]{1,0:T(2,128)S(1)}, f32[2,1024]{1,0:T(2,128)S(1)}, u32[]{:S(2)}, u32[]{:S(2)}) collective-permute-start(f32[2,1024]{1,0:T(2,128)S(1)} %shard_map.194), channel_id=1, source_target_pairs={{0,8},{4,12},{8,0},{12,4},{16,24},{20,28},{24,16},{28,20},{32,40},... | collective-permute-start | bytes 24584 | tf_op jit(solution)/shard_map/ppermute | solution.py:379
  71.5 4.2 %collective-permute-start.4 = (f32[2,1024]{1,0:T(2,128)S(1)}, f32[2,1024]{1,0:T(2,128)S(1)}, u32[]{:S(2)}, u32[]{:S(2)}) collective-permute-start(f32[2,1024]{1,0:T(2,128)S(1)} %shard_map.194), channel_id=1, source_target_pairs={{0,12},{4,0},{8,4},{12,8},{16,28},{20,16},{24,20},{28,24},{32,44},... | collective-permute-start | bytes 24584 | tf_op jit(solution)/shard_map/ppermute | solution.py:379
  75.7 17.6 %collective-permute-start.5 = (f32[2,1024]{1,0:T(2,128)S(1)}, f32[2,1024]{1,0:T(2,128)S(1)}, u32[]{:S(2)}, u32[]{:S(2)}) collective-permute-start(f32[2,1024]{1,0:T(2,128)S(1)} %add_add_fusion.1.rest_0_.refs_0_), channel_id=1, source_target_pairs={{0,16},{4,20},{8,24},{12,28},{16,0},{20,4},{24,8},{28,12},{32,48},... | collective-permute-start | bytes 24584 | tf_op jit(solution)/shard_map/ppermute | solution.py:379
  83.9 23.7 %all-to-all-start.3 = ((bf16[64,32,128]{2,1,0:T(8,128)(2,1)}), bf16[64,32,128]{2,1,0:T(8,128)(2,1)S(1)}, u32[]{:S(2)}, u32[]{:S(2)}) async-start(bf16[64,32,128]{2,1,0:T(8,128)(2,1)} %shard_map.195), calls=%async_computation.3 | async-start | bytes 1048576 | tf_op jit(solution)/shard_map/all_to_all | solution.py:477
  93.3 5.2 %collective-permute-start.6 = (f32[2,1024]{1,0:T(2,128)S(1)}, f32[2,1024]{1,0:T(2,128)S(1)}, u32[]{:S(2)}, u32[]{:S(2)}) collective-permute-start(f32[2,1024]{1,0:T(2,128)S(1)} %shard_map.197), channel_id=1, source_target_pairs={{0,32},{4,36},{8,40},{12,44},{16,48},{20,52},{24,56},{28,60},{32,0... | collective-permute-start | bytes 24584 | tf_op jit(solution)/shard_map/ppermute | solution.py:379
  98.5 6.8 %collective-permute-start.7 = (f32[2,1024]{1,0:T(2,128)S(1)}, f32[2,1024]{1,0:T(2,128)S(1)}, u32[]{:S(2)}, u32[]{:S(2)}) collective-permute-start(f32[2,1024]{1,0:T(2,128)S(1)} %add.32), channel_id=1, source_target_pairs={{0,64},{4,68},{8,72},{12,76},{16,80},{20,84},{24,88},{28,92},{32,9... | collective-permute-start | bytes 24584 | tf_op jit(solution)/shard_map/ppermute | solution.py:379
  101.2 4.6 %collective-permute-start.8 = (f32[2,1024]{1,0:T(2,128)S(1)}, f32[2,1024]{1,0:T(2,128)S(1)}, u32[]{:S(2)}, u32[]{:S(2)}) collective-permute-start(f32[2,1024]{1,0:T(2,128)S(1)} %add.32), channel_id=1, source_target_pairs={{0,128},{4,132},{8,136},{12,140},{16,144},{20,148},{24,152},{28,15... | collective-permute-start | bytes 24584 | tf_op jit(solution)/shard_map/ppermute | solution.py:379
  102.9 3.7 %collective-permute-start.9 = (f32[2,1024]{1,0:T(2,128)S(1)}, f32[2,1024]{1,0:T(2,128)S(1)}, u32[]{:S(2)}, u32[]{:S(2)}) collective-permute-start(f32[2,1024]{1,0:T(2,128)S(1)} %add.32), channel_id=1, source_target_pairs={{0,192},{4,196},{8,200},{12,204},{16,208},{20,212},{24,216},{28,22... | collective-permute-start | bytes 24584 | tf_op jit(solution)/shard_map/ppermute | solution.py:379
  (4 other events, 56.8 us)

commit v5 on v4

--- a/solution.py
+++ b/solution.py
@@ -135,7 +135,7 @@
 
 def conv_kernel(
     recv_ref, skip_ref, first_ref, last_ref, twiddle_ref, inner_ref, inverse_ref,
-    mixed_ref, kept_ref, spec_ref, x_ref, u_ref, z_ref, y_ref, sems,
+    mixed_ref, kept_ref, spec_ref, x_ref, u_ref, z_ref, y_ref, ready_ref, sems, out_sems,
 ):
     blocks, rows, lanes = recv_ref.shape
     channels = rows // 2
@@ -155,9 +155,13 @@
         put(u_ref, prod, lanes, pre * fim + pim * fre)
     wide = channels + 8
     inverse(channels, last_ref, twiddle_ref, inverse_ref, u_ref, z_ref, y_ref, wide)
+    leaving = copies_of(ready_ref, mixed_ref, out_sems)
+    size = blocks // len(leaving)
     for a in range(blocks):
-        mixed_ref[a] = y_ref[pl.ds(a * wide, channels), :].astype(bf16)
-    for copy in copies:
+        ready_ref[a] = y_ref[pl.ds(a * wide, channels), :].astype(bf16)
+        if a % size == size - 1:
+            leaving[a // size].start()
+    for copy in copies + leaving:
         copy.wait()
 
 
@@ -420,17 +424,19 @@
     vm = pltpu.VMEM
     return call(
         conv_kernel,
-        (shape((peers, channels, tokens), bf16), pltpu.HBM(spectra_shape, f32)),
+        (pltpu.HBM((peers, channels, tokens), bf16), pltpu.HBM(spectra_shape, f32)),
         n_in=7,
         smem=(1,),
-        hbm_out=(1,),
+        hbm_out=(0, 1),
         scratch=(
             vm(spectra_shape, f32),
             vm((2 * half + 8 * peers, tokens), f32),
             vm((2 * half, 4 * tokens), bf16),
             vm((half, 2 * tokens), f32),
             vm((half + 8 * peers, tokens), f32),
+            vm((peers, channels, tokens), bf16),
             pltpu.SemaphoreType.DMA((rows // 4,)),
+            pltpu.SemaphoreType.DMA((4,)),
         ),
     )(received, skip_here, *tables(peers, tokens))
 
@@ -531,9 +537,10 @@
     ends = sum_over(ends, "seq", side_x, 1)
     lag_sent = run_lag(grad_received, skip_here, spectra, ends)
     late = pl.CostEstimate(flops=3 * 10**10, bytes_accessed=10**8, transcendentals=0)
-    ends = sum_over(ends, "seq", 2, side_x, late)
-    ends = sum_over(ends, "seq", side_y // 2, 2 * side_x)
-    ends = sum_over(ends, "seq", side_z, side_x * side_y)
+    plane = side_x * side_y
+    ends = sum_over(ends, "seq", 2, side_z // 2 * plane, late)
+    ends = sum_over(ends, "seq", side_z // 2, plane)
+    ends = sum_over(ends, "seq", side_y, side_x)
     lag_received = exchange(lag_sent)
     grad_key, grad_value, grad_filter = call(
         finish_kernel,

time: 109 us -> 109 us (level)
  starting transfers between devices: 53 us -> 51.8 us
    ppermute x9, waiting for transfers between devices: 6.51 us -> 8.39 us  [sum_over(): lax.ppermute(values, axis, places(side, stride, count, step))]
    all_to_all x4, waiting for transfers between devices: 28.5 us -> 27.1 us  [exchange(): lax.all_to_all(values, 'seq', split_axis=0, concat_axis=0, tiled=True)]
  transfers between devices with their start and end apart: 14 -> 14, of which waited for: 10 -> 8; matrix products, arithmetic and copies ran while one was open for 1% -> 1% of each run, Pallas kernels for 6% -> 6%
where the time goes in v5:
time: 109 us; the launch traced here: 108 us
  starting transfers between devices  51.8 us (48%)
  waiting for transfers between devices  38.5 us (35%)
  Pallas kernels  14.7 us (13%)
  local copies, waits for them, and re-layouts  2.12 us (2%)
    all_to_all x4, starting transfers between devices, exchange(): lax.all_to_all(values, 'seq', split_axis=0, concat_axis=0, tiled=True)  32.6 us
    all_to_all x4, waiting for transfers between devices, exchange(): lax.all_to_all(values, 'seq', split_axis=0, concat_axis=0, tiled=True)  27.1 us
    ppermute x9, starting transfers between devices, sum_over(): lax.ppermute(values, axis, places(side, stride, count, step))  14.7 us
    ppermute x9, waiting for transfers between devices, sum_over(): lax.ppermute(values, axis, places(side, stride, count, step))  8.39 us
    pallas_call x1, Pallas kernels, run_lag(): call(lag_kernel, pltpu.HBM((peers, 2 * channels, tokens), bf16), n_in=8 +...  4.53 us
    ppermute x1, starting transfers between devices, on_device(): far = lax.ppermute(near, 'chan', places(2, 2, 4, 1))  4.49 us
    pallas_call x1, Pallas kernels, run_conv(): call(conv_kernel, (pltpu.HBM((peers, channels, tokens), bf16), pltpu.HBM(...  3.72 us
    ppermute x1, waiting for transfers between devices, on_device(): far = lax.ppermute(near, 'chan', places(2, 2, 4, 1))  2.98 us
  transfers between devices with their start and end apart: 14, of which 8 were waited for; matrix products, arithmetic and copies ran while one was open for 1% of the time, Pallas kernels for 6%

profile of v5, /device:TPU:2, one launch (start us, length us, event | category | flops | bytes accessed | tf_op | source)
XLA Modules:
  0.0 108.2 jit_solution(16765533930264002127)
XLA Ops:
  0.7 2.2 %shard_map.188 = bf16[64,32,128]{2,1,0:T(8,128)(2,1)} custom-call(bf16[128,1024]{1,0:T(8,128)(2,1)} %key_ref.3, bf16[128,1024]{1,0:T(8,128)(2,1)} %value_ref.3, bf16[128,1024]{1,0:T(8,128)(2,1)} %filters_hbm.1), custom_call_target="tpu_custom_call" | custom-call | tf_op jit(solution)/shard_map/pallas_call | solution.py:490
  3.0 12.1 %all-to-all-start = ((bf16[64,32,128]{2,1,0:T(8,128)(2,1)}), bf16[64,32,128]{2,1,0:T(8,128)(2,1)S(1)}, u32[]{:S(2)}, u32[]{:S(2)}) async-start(bf16[64,32,128]{2,1,0:T(8,128)(2,1)} %shard_map.188), calls=%async_computation | async-start | bytes 1048576 | tf_op jit(solution)/shard_map/all_to_all | solution.py:483
  15.8 16.3 %all-to-all-done.recv_ref = bf16[64,32,128]{2,1,0:T(8,128)(2,1)S(1)} async-done(((bf16[64,32,128]{2,1,0:T(8,128)(2,1)}), bf16[64,32,128]{2,1,0:T(8,128)(2,1)S(1)}, u32[]{:S(2)}, u32[]{:S(2)}) %all-to-all-start) | async-done | bytes 524320 | tf_op jit(solution)/shard_map/all_to_all | solution.py:483
  32.1 3.7 %shard_map.189 = (bf16[64,16,128]{2,1,0:T(8,128)(2,1)}, f32[2048,256]{1,0:T(8,128)}) custom-call(bf16[64,32,128]{2,1,0:T(8,128)(2,1)S(1)} %all-to-all-done.recv_ref, f32[16]{0:T(128)S(1)} %dynamic_slice.3.skip_ref, bf16[128,128]{1,0:T(8,128)(2,1)S(1)} %copy-done.9, bf16[64,384]{1,0:T(8,128)(2,1)S(1)} %copy-done.8, f32[128,128]{1,0:T(8,128)S(1)} %copy-done.5, ...), custom_call_target="tpu_custom_call" | custom-call | tf_op jit(solution)/shard_map/pallas_call | solution.py:425
  35.9 5.9 %all-to-all-start.1 = ((bf16[64,16,128]{2,1,0:T(8,128)(2,1)}), bf16[64,16,128]{2,1,0:T(8,128)(2,1)S(1)}, u32[]{:S(2)}, u32[]{:S(2)}) async-start(bf16[64,16,128]{2,1,0:T(8,128)(2,1)} %get-tuple-element.19), calls=%async_computation.1 | async-start | bytes 524288 | tf_op jit(solution)/shard_map/all_to_all | solution.py:483
  42.8 9.8 %all-to-all-done.1 = bf16[64,16,128]{2,1,0:T(8,128)(2,1)S(1)} async-done(((bf16[64,16,128]{2,1,0:T(8,128)(2,1)}), bf16[64,16,128]{2,1,0:T(8,128)(2,1)S(1)}, u32[]{:S(2)}, u32[]{:S(2)}) %all-to-all-start.1) | async-done | bytes 262176 | tf_op jit(solution)/shard_map/all_to_all | solution.py:483
  53.0 1.1 %collective-permute-done = f32[2,128]{1,0:T(2,128)S(1)} collective-permute-done((f32[2,128]{1,0:T(2,128)S(1)}, f32[2,128]{1,0:T(2,128)S(1)}, u32[]{:S(2)}, u32[]{:S(2)}) %collective-permute-start) | collective-permute-done | bytes 1056 | tf_op jit(solution)/shard_map/ppermute | solution.py:383
  54.2 4.5 %collective-permute-start.1 = (f32[2,128]{1,0:T(2,128)S(1)}, f32[2,128]{1,0:T(2,128)S(1)}, u32[]{:S(2)}, u32[]{:S(2)}) collective-permute-start(f32[2,128]{1,0:T(2,128)S(1)} %add.28.near_ref), channel_id=1, source_target_pairs={{0,2},{1,3},{2,0},{3,1},{4,6},{5,7},{6,4},{7,5},{8,10},{9,11},{10,... | collective-permute-start | bytes 3080 | tf_op jit(solution)/shard_map/ppermute | solution.py:518
  58.7 3.0 %collective-permute-done.1.far_ref = f32[2,128]{1,0:T(2,128)S(1)} collective-permute-done((f32[2,128]{1,0:T(2,128)S(1)}, f32[2,128]{1,0:T(2,128)S(1)}, u32[]{:S(2)}, u32[]{:S(2)}) %collective-permute-start.1) | collective-permute-done | bytes 1056 | tf_op jit(solution)/shard_map/ppermute | solution.py:518
  62.5 5.9 %all-to-all-start.2 = ((bf16[64,16,128]{2,1,0:T(8,128)(2,1)}), bf16[64,16,128]{2,1,0:T(8,128)(2,1)S(1)}, u32[]{:S(2)}, u32[]{:S(2)}) async-start(bf16[64,16,128]{2,1,0:T(8,128)(2,1)} %bitcast.11), calls=%async_computation.2 | async-start | bytes 524288 | tf_op jit(solution)/shard_map/all_to_all | solution.py:483
  68.9 1.5 %collective-permute-start.2 = (f32[2,1024]{1,0:T(2,128)S(1)}, f32[2,1024]{1,0:T(2,128)S(1)}, u32[]{:S(2)}, u32[]{:S(2)}) collective-permute-start(f32[2,1024]{1,0:T(2,128)S(1)} %shard_map.194), channel_id=1, source_target_pairs={{0,4},{4,8},{8,12},{12,0},{16,20},{20,24},{24,28},{28,16},{32,36},... | collective-permute-start | bytes 24584 | tf_op jit(solution)/shard_map/ppermute | solution.py:383
  70.4 1.1 collective-permute-start.3
  71.5 2.2 %collective-permute-start.4 = (f32[2,1024]{1,0:T(2,128)S(1)}, f32[2,1024]{1,0:T(2,128)S(1)}, u32[]{:S(2)}, u32[]{:S(2)}) collective-permute-start(f32[2,1024]{1,0:T(2,128)S(1)} %shard_map.194), channel_id=1, source_target_pairs={{0,12},{4,0},{8,4},{12,8},{16,28},{20,16},{24,20},{28,24},{32,44},... | collective-permute-start | bytes 24584 | tf_op jit(solution)/shard_map/ppermute | solution.py:383
  73.6 2.0 %collective-permute-done.3 = f32[2,1024]{1,0:T(2,128)S(1)} collective-permute-done((f32[2,1024]{1,0:T(2,128)S(1)}, f32[2,1024]{1,0:T(2,128)S(1)}, u32[]{:S(2)}, u32[]{:S(2)}) %collective-permute-start.3) | collective-permute-done | bytes 8224 | tf_op jit(solution)/shard_map/ppermute | solution.py:383
  75.6 2.7 %collective-permute-start.5 = (f32[2,1024]{1,0:T(2,128)S(1)}, f32[2,1024]{1,0:T(2,128)S(1)}, u32[]{:S(2)}, u32[]{:S(2)}) collective-permute-start(f32[2,1024]{1,0:T(2,128)S(1)} %add_add_fusion.1.rest_0_.refs_0_), channel_id=1, source_target_pairs={{0,128},{4,132},{8,136},{12,140},{16,144},{20,148},{24,152},{28,15... | collective-permute-start | bytes 24584 | tf_op jit(solution)/shard_map/ppermute | solution.py:383
  78.3 1.0 all-to-all-done.2.recv_ref
  79.3 4.5 %shard_map.195 = bf16[64,32,128]{2,1,0:T(8,128)(2,1)} custom-call(bf16[64,16,128]{2,1,0:T(8,128)(2,1)S(1)} %all-to-all-done.2.recv_ref, f32[16]{0:T(128)S(1)} %copy-done.13, bf16[128,128]{1,0:T(8,128)(2,1)S(1)} %copy-done.9, bf16[64,384]{1,0:T(8,128)(2,1)S(1)} %copy-done.8, f32[128,128]{1,0:T(8,128)S(1)} %copy-done.5, bf16[768,256]{1,0:T(8,128)(2,1)S(1)} %copy-done.2, ...), custom_call_target="tpu_custom_call" | custom-call | tf_op jit(solution)/shard_map/pallas_call | solution.py:449
  83.9 8.7 %all-to-all-start.3 = ((bf16[64,32,128]{2,1,0:T(8,128)(2,1)}), bf16[64,32,128]{2,1,0:T(8,128)(2,1)S(1)}, u32[]{:S(2)}, u32[]{:S(2)}) async-start(bf16[64,32,128]{2,1,0:T(8,128)(2,1)} %shard_map.195), calls=%async_computation.3 | async-start | bytes 1048576 | tf_op jit(solution)/shard_map/all_to_all | solution.py:483
  92.6 1.6 %collective-permute-start.6 = (f32[2,1024]{1,0:T(2,128)S(1)}, f32[2,1024]{1,0:T(2,128)S(1)}, u32[]{:S(2)}, u32[]{:S(2)}) collective-permute-start(f32[2,1024]{1,0:T(2,128)S(1)} %shard_map.197), channel_id=1, source_target_pairs={{0,64},{4,68},{8,72},{12,76},{16,80},{20,84},{24,88},{28,92},{32,9... | collective-permute-start | bytes 24584 | tf_op jit(solution)/shard_map/ppermute | solution.py:383
  94.2 4.4 %collective-permute-done.6 = f32[2,1024]{1,0:T(2,128)S(1)} collective-permute-done((f32[2,1024]{1,0:T(2,128)S(1)}, f32[2,1024]{1,0:T(2,128)S(1)}, u32[]{:S(2)}, u32[]{:S(2)}) %collective-permute-start.6) | collective-permute-done | bytes 8224 | tf_op jit(solution)/shard_map/ppermute | solution.py:383
  99.5 3.1 %collective-permute-start.8 = (f32[2,1024]{1,0:T(2,128)S(1)}, f32[2,1024]{1,0:T(2,128)S(1)}, u32[]{:S(2)}, u32[]{:S(2)}) collective-permute-start(f32[2,1024]{1,0:T(2,128)S(1)} %add.32), channel_id=1, source_target_pairs={{0,32},{4,36},{8,40},{12,44},{16,48},{20,52},{24,56},{28,60},{32,0... | collective-permute-start | bytes 24584 | tf_op jit(solution)/shard_map/ppermute | solution.py:383
  102.6 1.6 %collective-permute-start.9 = (f32[2,1024]{1,0:T(2,128)S(1)}, f32[2,1024]{1,0:T(2,128)S(1)}, u32[]{:S(2)}, u32[]{:S(2)}) collective-permute-start(f32[2,1024]{1,0:T(2,128)S(1)} %add.32), channel_id=1, source_target_pairs={{0,48},{4,52},{8,56},{12,60},{16,0},{20,4},{24,8},{28,12},{32,16},... | collective-permute-start | bytes 24584 | tf_op jit(solution)/shard_map/ppermute | solution.py:383
  104.2 1.2 %shard_map.192 = (bf16[128,1024]{1,0:T(8,128)(2,1)}, bf16[128,1024]{1,0:T(8,128)(2,1)}, bf16[128,1024]{1,0:T(8,128)(2,1)}) custom-call(f32[2,128]{1,0:T(2,128)S(1)} %add.28.near_ref, f32[2,128]{1,0:T(2,128)S(1)} %collective-permute-done.1.far_ref, bf16[1024,128]{1,0:T(8,128)(2,1)S(1)} %bitcast.8, bf16[1024,128]{1,0:T(8,128)(2,1)S(1)} %get-tuple-element.20.res_ref, ...), custom_call_target="tpu_custom_call" | custom-call | flops 1000000 | bytes 4000000 | tf_op jit(solution)/shard_map/pallas_call | solution.py:530
  106.9 1.2 %shard_map.196 = (bf16[128,1024]{1,0:T(8,128)(2,1)}, bf16[128,1024]{1,0:T(8,128)(2,1)}, f32[128,1024]{1,0:T(8,128)}) custom-call(bf16[64,32,128]{2,1,0:T(8,128)(2,1)S(1)} %all-to-all-done.3.recv_ref, bf16[128,1024]{1,0:T(8,128)(2,1)S(1)} %copy-done, bf16[128,1024]{1,0:T(8,128)(2,1)S(1)} %copy-done.1), custom_call_target="tpu_custom_call" | custom-call | tf_op jit(solution)/shard_map/pallas_call | solution.py:545
  (48 shorter events, 6.0 us)
Async XLA Ops:
  0.6 31.5 %copy-start.9 = (bf16[128,128]{1,0:T(8,128)(2,1)S(1)}, bf16[128,128]{1,0:T(8,128)(2,1)}, u32[]{:S(2)}) copy-start(bf16[128,128]{1,0:T(8,128)(2,1)} %constant.22.clone.first_ref) | copy-start | bytes 98308
  0.6 31.5 %copy-start.8 = (bf16[64,384]{1,0:T(8,128)(2,1)S(1)}, bf16[64,384]{1,0:T(8,128)(2,1)}, u32[]{:S(2)}) copy-start(bf16[64,384]{1,0:T(8,128)(2,1)} %constant.23.clone.last_ref) | copy-start | bytes 147460
  0.7 31.4 %copy-start.5 = (f32[128,128]{1,0:T(8,128)S(1)}, f32[128,128]{1,0:T(8,128)}, u32[]{:S(2)}) copy-start(f32[128,128]{1,0:T(8,128)} %constant.24.clone.twiddle_ref) | copy-start | bytes 196612
  0.7 31.4 %copy-start.2 = (bf16[768,256]{1,0:T(8,128)(2,1)S(1)}, bf16[768,256]{1,0:T(8,128)(2,1)}, u32[]{:S(2)}) copy-start(bf16[768,256]{1,0:T(8,128)(2,1)} %constant.25.clone.inner_ref) | copy-start | bytes 1179652
  0.7 31.4 %copy-start.3 = (bf16[768,256]{1,0:T(8,128)(2,1)S(1)}, bf16[768,256]{1,0:T(8,128)(2,1)}, u32[]{:S(2)}) copy-start(bf16[768,256]{1,0:T(8,128)(2,1)} %constant.26.clone.inverse_ref) | copy-start | bytes 1179652
  0.7 41.1 %copy-start.6 = (bf16[128,1024]{1,0:T(8,128)(2,1)S(1)}, bf16[128,1024]{1,0:T(8,128)(2,1)}, u32[]{:S(2)}) copy-start(bf16[128,1024]{1,0:T(8,128)(2,1)} %residual_ref.1) | copy-start | bytes 786436
  0.7 41.1 %copy-start.7 = (bf16[128,1024]{1,0:T(8,128)(2,1)S(1)}, bf16[128,1024]{1,0:T(8,128)(2,1)}, u32[]{:S(2)}) copy-start(bf16[128,1024]{1,0:T(8,128)(2,1)} %query_ref.1) | copy-start | bytes 786436
  0.7 41.1 %copy-start.4 = (bf16[128,1024]{1,0:T(8,128)(2,1)S(1)}, bf16[128,1024]{1,0:T(8,128)(2,1)}, u32[]{:S(2)}) copy-start(bf16[128,1024]{1,0:T(8,128)(2,1)} %cotangent_ref.3) | copy-start | bytes 786436
  3.0 29.1 %all-to-all-start = ((bf16[64,32,128]{2,1,0:T(8,128)(2,1)}), bf16[64,32,128]{2,1,0:T(8,128)(2,1)S(1)}, u32[]{:S(2)}, u32[]{:S(2)}) async-start(bf16[64,32,128]{2,1,0:T(8,128)(2,1)} %shard_map.188), calls=%async_computation | async-start | bytes 1048576 | tf_op jit(solution)/shard_map/all_to_all | solution.py:483
  35.9 16.8 %all-to-all-start.1 = ((bf16[64,16,128]{2,1,0:T(8,128)(2,1)}), bf16[64,16,128]{2,1,0:T(8,128)(2,1)S(1)}, u32[]{:S(2)}, u32[]{:S(2)}) async-start(bf16[64,16,128]{2,1,0:T(8,128)(2,1)} %get-tuple-element.19), calls=%async_computation.1 | async-start | bytes 524288 | tf_op jit(solution)/shard_map/all_to_all | solution.py:483
  42.5 25.9 %copy-start = (bf16[128,1024]{1,0:T(8,128)(2,1)S(1)}, bf16[128,1024]{1,0:T(8,128)(2,1)}, u32[]{:S(2)}) copy-start(bf16[128,1024]{1,0:T(8,128)(2,1)} %key_ref.3) | copy-start | bytes 786436
  42.5 26.0 %copy-start.1 = (bf16[128,1024]{1,0:T(8,128)(2,1)S(1)}, bf16[128,1024]{1,0:T(8,128)(2,1)}, u32[]{:S(2)}) copy-start(bf16[128,1024]{1,0:T(8,128)(2,1)} %value_ref.3) | copy-start | bytes 786436
  52.9 1.2 %collective-permute-start = (f32[2,128]{1,0:T(2,128)S(1)}, f32[2,128]{1,0:T(2,128)S(1)}, u32[]{:S(2)}, u32[]{:S(2)}) collective-permute-start(f32[2,128]{1,0:T(2,128)S(1)} %shard_map.191), channel_id=1, source_target_pairs={{0,1},{1,0},{2,3},{3,2},{4,5},{5,4},{6,7},{7,6},{8,9},{9,8},{10,11... | collective-permute-start | bytes 3080 | tf_op jit(solution)/shard_map/ppermute | solution.py:383
  54.2 7.5 %collective-permute-start.1 = (f32[2,128]{1,0:T(2,128)S(1)}, f32[2,128]{1,0:T(2,128)S(1)}, u32[]{:S(2)}, u32[]{:S(2)}) collective-permute-start(f32[2,128]{1,0:T(2,128)S(1)} %add.28.near_ref), channel_id=1, source_target_pairs={{0,2},{1,3},{2,0},{3,1},{4,6},{5,7},{6,4},{7,5},{8,10},{9,11},{10,... | collective-permute-start | bytes 3080 | tf_op jit(solution)/shard_map/ppermute | solution.py:518
  62.5 16.8 %all-to-all-start.2 = ((bf16[64,16,128]{2,1,0:T(8,128)(2,1)}), bf16[64,16,128]{2,1,0:T(8,128)(2,1)S(1)}, u32[]{:S(2)}, u32[]{:S(2)}) async-start(bf16[64,16,128]{2,1,0:T(8,128)(2,1)} %bitcast.11), calls=%async_computation.2 | async-start | bytes 524288 | tf_op jit(solution)/shard_map/all_to_all | solution.py:483
  68.9 4.8 %collective-permute-start.2 = (f32[2,1024]{1,0:T(2,128)S(1)}, f32[2,1024]{1,0:T(2,128)S(1)}, u32[]{:S(2)}, u32[]{:S(2)}) collective-permute-start(f32[2,1024]{1,0:T(2,128)S(1)} %shard_map.194), channel_id=1, source_target_pairs={{0,4},{4,8},{8,12},{12,0},{16,20},{20,24},{24,28},{28,16},{32,36},... | collective-permute-start | bytes 24584 | tf_op jit(solution)/shard_map/ppermute | solution.py:383
  70.4 5.2 %collective-permute-start.3 = (f32[2,1024]{1,0:T(2,128)S(1)}, f32[2,1024]{1,0:T(2,128)S(1)}, u32[]{:S(2)}, u32[]{:S(2)}) collective-permute-start(f32[2,1024]{1,0:T(2,128)S(1)} %shard_map.194), channel_id=1, source_target_pairs={{0,8},{4,12},{8,0},{12,4},{16,24},{20,28},{24,16},{28,20},{32,40},... | collective-permute-start | bytes 24584 | tf_op jit(solution)/shard_map/ppermute | solution.py:383
  71.5 4.2 %collective-permute-start.4 = (f32[2,1024]{1,0:T(2,128)S(1)}, f32[2,1024]{1,0:T(2,128)S(1)}, u32[]{:S(2)}, u32[]{:S(2)}) collective-permute-start(f32[2,1024]{1,0:T(2,128)S(1)} %shard_map.194), channel_id=1, source_target_pairs={{0,12},{4,0},{8,4},{12,8},{16,28},{20,16},{24,20},{28,24},{32,44},... | collective-permute-start | bytes 24584 | tf_op jit(solution)/shard_map/ppermute | solution.py:383
  75.6 16.9 %collective-permute-start.5 = (f32[2,1024]{1,0:T(2,128)S(1)}, f32[2,1024]{1,0:T(2,128)S(1)}, u32[]{:S(2)}, u32[]{:S(2)}) collective-permute-start(f32[2,1024]{1,0:T(2,128)S(1)} %add_add_fusion.1.rest_0_.refs_0_), channel_id=1, source_target_pairs={{0,128},{4,132},{8,136},{12,140},{16,144},{20,148},{24,152},{28,15... | collective-permute-start | bytes 24584 | tf_op jit(solution)/shard_map/ppermute | solution.py:383
  83.9 23.0 %all-to-all-start.3 = ((bf16[64,32,128]{2,1,0:T(8,128)(2,1)}), bf16[64,32,128]{2,1,0:T(8,128)(2,1)S(1)}, u32[]{:S(2)}, u32[]{:S(2)}) async-start(bf16[64,32,128]{2,1,0:T(8,128)(2,1)} %shard_map.195), calls=%async_computation.3 | async-start | bytes 1048576 | tf_op jit(solution)/shard_map/all_to_all | solution.py:483
  92.6 5.9 %collective-permute-start.6 = (f32[2,1024]{1,0:T(2,128)S(1)}, f32[2,1024]{1,0:T(2,128)S(1)}, u32[]{:S(2)}, u32[]{:S(2)}) collective-permute-start(f32[2,1024]{1,0:T(2,128)S(1)} %shard_map.197), channel_id=1, source_target_pairs={{0,64},{4,68},{8,72},{12,76},{16,80},{20,84},{24,88},{28,92},{32,9... | collective-permute-start | bytes 24584 | tf_op jit(solution)/shard_map/ppermute | solution.py:383
  98.5 6.8 %collective-permute-start.7 = (f32[2,1024]{1,0:T(2,128)S(1)}, f32[2,1024]{1,0:T(2,128)S(1)}, u32[]{:S(2)}, u32[]{:S(2)}) collective-permute-start(f32[2,1024]{1,0:T(2,128)S(1)} %add.32), channel_id=1, source_target_pairs={{0,16},{4,20},{8,24},{12,28},{16,32},{20,36},{24,40},{28,44},{32,4... | collective-permute-start | bytes 24584 | tf_op jit(solution)/shard_map/ppermute | solution.py:383
  99.5 5.8 %collective-permute-start.8 = (f32[2,1024]{1,0:T(2,128)S(1)}, f32[2,1024]{1,0:T(2,128)S(1)}, u32[]{:S(2)}, u32[]{:S(2)}) collective-permute-start(f32[2,1024]{1,0:T(2,128)S(1)} %add.32), channel_id=1, source_target_pairs={{0,32},{4,36},{8,40},{12,44},{16,48},{20,52},{24,56},{28,60},{32,0... | collective-permute-start | bytes 24584 | tf_op jit(solution)/shard_map/ppermute | solution.py:383
  102.6 3.7 %collective-permute-start.9 = (f32[2,1024]{1,0:T(2,128)S(1)}, f32[2,1024]{1,0:T(2,128)S(1)}, u32[]{:S(2)}, u32[]{:S(2)}) collective-permute-start(f32[2,1024]{1,0:T(2,128)S(1)} %add.32), channel_id=1, source_target_pairs={{0,48},{4,52},{8,56},{12,60},{16,0},{20,4},{24,8},{28,12},{32,16},... | collective-permute-start | bytes 24584 | tf_op jit(solution)/shard_map/ppermute | solution.py:383
  (4 other events, 57.4 us)
